TPU v7x, 32 devices: a whole 2x2x4 slice. The times are simulated.
32 devices in a mesh: grp: 2 (over y), win: 4 (over z), uly: 4 (over x, core).
Axes of the slice: x: 2, y: 2, z: 4, core: 2. Of those that a mesh axis runs over, the one named last changes fastest.
Arguments:
- query_rows: bfloat16 [8, 16, 64, 5120], P(('grp', 'win'), None, 'uly'), parts along dimension 0, may hold values from -140 to 140
- key_rows: bfloat16 [8, 16, 64, 5120], P(('grp', 'win'), None, 'uly'), parts along dimension 0, may hold values from -140 to 140
- value_rows: bfloat16 [8, 16, 64, 5120], P(('grp', 'win'), None, 'uly'), parts along dimension 0, may hold values from -6 to 6
- query_gain: float32 [5120], replicated, may hold values from 0.25 to 1.75
- key_gain: float32 [5120], replicated, may hold values from 0.25 to 1.75
- window_start: int32 [8], P('grp'), parts along dimension 0, may hold values from 0 to 40, as said below
- owner_of_phase: int32 [8], P('grp'), parts along dimension 0, may hold values from 0 to 3, each once
- blend_weight: int32 [8, 16], P('grp'), parts along dimension 0, may hold values from 1 to 8
Outputs:
- owned_frames: bfloat16 [96, 64, 5120], P(('grp', 'win'), 'uly'), parts along dimension 0
- next_windows: bfloat16 [8, 16, 64, 5120], P(('grp', 'win'), None, 'uly'), parts along dimension 0
There are 2 independent parts, one for each index of `grp`. A program takes and returns all parts, laid end to end along the dimension named above; an argument that names none is the same for every part. Nothing has to cross between parts.
Inputs may be any that keep to these rules, and one draw needn't show every extreme that they name: `window_start`: window w starts at frame w * 12 plus an offset of 0 to 4; in some pair of consecutive windows (the last one followed by the first counts as consecutive) the first offset is 4 and the second 0. `owner_of_phase`: a permutation.
All inputs are finite; a program needn't handle non-finite values.
Results may differ from a plain program's by a relative error of at most 0.0015.
The roundings to bfloat16 on the way count: a program that leaves them out, or rounds other values in their place, can miss the bound.
Values may be sent and summed in bfloat16 or wider, within the bound.
No kernel may reach another device: no remote copies, remote signals or barrier semaphores. Data moves between devices by JAX's collectives and lax.ppermute only.
A program may use at most 128 MiB of HBM per device.

v0:
```python
import math

import jax
import jax.numpy as jnp
from jax import lax
from jax.sharding import PartitionSpec as P

HEADS = 40
WF = 16
FR = 12


def normalize(row_block, gain_vector):
    floats = row_block.astype(jnp.float32)
    mean_square = jnp.mean(floats * floats, axis=-1, keepdims=True)
    return (floats * lax.rsqrt(mean_square + 1e-06) * gain_vector).astype(jnp.bfloat16)


def head_attention(operands):
    query_head, key_head, value_head = operands
    scores = jnp.dot(query_head, key_head.T, preferred_element_type=jnp.float32) * (
        1.0 / math.sqrt(query_head.shape[-1])
    )
    row_max = jnp.max(scores, axis=-1, keepdims=True)
    exponent = jnp.exp(scores - row_max)
    weights = (exponent / jnp.sum(exponent, axis=-1, keepdims=True)).astype(jnp.bfloat16)
    return jnp.dot(weights, value_head, preferred_element_type=jnp.float32).astype(jnp.bfloat16)


def attend(operands):
    query_part, key_part, value_part = operands
    heads_here = query_part.shape[3]
    head_size = query_part.shape[4]
    token_count = query_part.shape[0] * query_part.shape[1]

    def flatten(tensor):
        return jnp.moveaxis(tensor.reshape(token_count, heads_here, head_size), 1, 0)

    result = lax.map(head_attention, (flatten(query_part), flatten(key_part), flatten(value_part)))
    return jnp.moveaxis(result, 0, 1).reshape(query_part.shape)


def table_lookup(table_row, wanted, length):
    entries = jnp.arange(length, dtype=jnp.int32)
    return jnp.sum(jnp.where(wanted[..., None] == entries, table_row, 0), axis=-1)


def send_owners(frame_rows, inverse, my_start, windows, capacity):
    slot_index = jnp.arange(capacity, dtype=jnp.int32)
    position_in = (inverse[:, None] - my_start) % windows + slot_index[None, :] * windows
    is_valid = (position_in < WF).reshape(-1)
    picked = jnp.take(frame_rows, jnp.minimum(position_in, WF - 1).reshape(-1), axis=0)
    picked = jnp.where(is_valid[:, None, None], picked, jnp.zeros_like(picked))
    packed = picked.reshape(windows, capacity, frame_rows.shape[1], frame_rows.shape[2])
    return lax.all_to_all(packed, "win", split_axis=0, concat_axis=0, tiled=True)


def combine_owned(received, window_start, blend_weight, my_phase, windows, frames_total, capacity):
    slot_index = jnp.arange(capacity, dtype=jnp.int32)
    source_pos = (my_phase - window_start[:, None]) % windows + slot_index[None, :] * windows
    arrived = source_pos < WF
    slot_at = (window_start[:, None] + source_pos) % frames_total // windows
    factor = table_lookup(blend_weight[:, None, :], source_pos, WF)
    owned_range = jnp.arange(FR, dtype=jnp.int32)
    mixing = jnp.where(
        (slot_at[None] == owned_range[:, None, None]) & arrived[None], factor[None], 0
    )
    mixing = mixing.reshape(FR, windows * capacity).astype(jnp.float32)
    numerator = jnp.dot(
        mixing.astype(jnp.bfloat16),
        received.reshape(windows * capacity, -1),
        preferred_element_type=jnp.float32,
    )
    denominator = jnp.sum(mixing, axis=1)
    owned = (numerator / denominator[:, None]).astype(jnp.bfloat16)
    return owned.reshape(FR, received.shape[2], received.shape[3])


def per_device(
    query_rows,
    key_rows,
    value_rows,
    query_gain,
    key_gain,
    window_start,
    owner_of_phase,
    blend_weight,
):
    windows = lax.axis_size("win")
    ulysses = lax.axis_size("uly")
    position = lax.axis_index("win")
    frames_total = FR * windows
    capacity = (WF + windows - 1) // windows
    shift_frames = FR // 2
    local_tokens = query_rows.shape[2]
    feature_count = query_rows.shape[3]
    groups = HEADS // ulysses
    head_size = feature_count // HEADS
    split_shape = (WF, local_tokens, ulysses, groups, head_size)
    query_heads = normalize(query_rows[0], query_gain).reshape(split_shape)
    key_heads = normalize(key_rows[0], key_gain).reshape(split_shape)
    value_heads = value_rows[0].reshape(split_shape)
    attended = attend(
        (
            lax.all_to_all(query_heads, "uly", split_axis=2, concat_axis=1, tiled=True),
            lax.all_to_all(key_heads, "uly", split_axis=2, concat_axis=1, tiled=True),
            lax.all_to_all(value_heads, "uly", split_axis=2, concat_axis=1, tiled=True),
        )
    )
    own_out = lax.all_to_all(attended, "uly", split_axis=1, concat_axis=2, tiled=True).reshape(
        WF, local_tokens, feature_count
    )
    phases = jnp.arange(windows, dtype=jnp.int32)
    inverse = jnp.sum(
        jnp.where(owner_of_phase[None, :] == phases[:, None], phases[None, :], 0), axis=1
    )
    my_start = window_start[position]
    my_phase = inverse[position]
    frame_range = jnp.arange(WF, dtype=jnp.int32)
    received = send_owners(own_out, inverse, my_start, windows, capacity)
    owned = combine_owned(
        received, window_start, blend_weight, my_phase, windows, frames_total, capacity
    )
    slot_index = jnp.arange(capacity, dtype=jnp.int32)
    target_pos = (my_phase - window_start[:, None] - shift_frames) % windows + slot_index[
        None, :
    ] * windows
    target_valid = (target_pos < WF).reshape(-1)
    target_slot = (
        (window_start[:, None] + shift_frames + target_pos) % frames_total // windows
    ).reshape(-1)
    outgoing = jnp.take(owned, target_slot, axis=0)
    outgoing = jnp.where(target_valid[:, None, None], outgoing, jnp.zeros_like(outgoing))
    outgoing = outgoing.reshape(windows, capacity, local_tokens, feature_count)
    returned = lax.all_to_all(outgoing, "win", split_axis=0, concat_axis=0, tiled=True)
    needed_phase = (my_start + shift_frames + frame_range) % windows
    source_owner = table_lookup(owner_of_phase[None, :], needed_phase, windows)
    flat_index = source_owner * capacity + frame_range // windows
    next_rows = jnp.take(
        returned.reshape(windows * capacity, local_tokens, feature_count), flat_index, axis=0
    )
    return (owned, next_rows[None])


def solution(mesh):
    placed = (
        P(("grp", "win"), None, "uly", None),
        P(("grp", "win"), None, "uly", None),
        P(("grp", "win"), None, "uly", None),
        P(),
        P(),
        P("grp"),
        P("grp"),
        P("grp", None),
    )
    return jax.shard_map(
        per_device,
        mesh=mesh,
        in_specs=placed,
        out_specs=(P(("grp", "win"), "uly", None), P(("grp", "win"), None, "uly", None)),
        check_vma=False,
    )
```

profile of v0, /device:TPU:0, one launch (start us, length us, event | category | flops | bytes accessed | tf_op | source)
XLA Modules:
  0.0 380.4 jit_solution(709549636202989451)
XLA Ops:
  0.6 6.8 %reshape.405 = f32[16,16,4,10,128]{4,3,2,1,0:T(8,128)} reshape(bf16[1,16,16,5120]{3,2,1,0:T(8,128)(2,1)} %param.13) | data formatting | bytes 7864320 | tf_op jit(solution)/shard_map/convert_element_type | solution.py:14
  8.2 4.0 %multiply_convert_fusion = bf16[16,16,4,10,128]{4,3,2,1,0:T(8,128)(2,1)S(1)} fusion(f32[16,16,4,10,128]{4,3,2,1,0:T(8,128)} %reshape.405, f32[4,10,128]{2,1,0:T(8,128)S(1)} %mul.80, f32[16,16]{1,0:T(8,128)S(1)} %add_rsqrt_fusion), kind=kLoop, calls=%fused_computation.23 | loop fusion | flops 3932160 | bytes 7885824 | tf_op jit(solution)/shard_map/convert_element_type | solution.py:16
  12.2 4.6 %copy.33 = bf16[16,16,4,10,128]{4,1,3,0,2:T(8,128)(2,1)} copy(bf16[16,16,4,10,128]{4,3,2,1,0:T(8,128)(2,1)S(1)} %multiply_convert_fusion) | data formatting | bytes 5242880 | tf_op jit(solution)/shard_map/convert_element_type | solution.py:16
  16.9 4.2 %all-to-all-start.1 = ((bf16[16,16,4,10,128]{4,1,3,0,2:T(8,128)(2,1)}), bf16[16,16,4,10,128]{4,1,3,0,2:T(8,128)(2,1)S(1)}, u32[]{:S(2)}, u32[]{:S(2)}) async-start(bf16[16,16,4,10,128]{4,1,3,0,2:T(8,128)(2,1)} %copy.33), calls=%async_computation.1 | async-start | bytes 5242880 | tf_op jit(solution)/shard_map/all_to_all | solution.py:106
  21.1 6.7 %reshape.404 = f32[16,16,4,10,128]{4,3,2,1,0:T(8,128)} reshape(bf16[1,16,16,5120]{3,2,1,0:T(8,128)(2,1)} %param.12) | data formatting | bytes 7864320 | tf_op jit(solution)/shard_map/convert_element_type | solution.py:14
  27.7 2.3 multiply_reduce_fusion.2
  30.1 4.1 %multiply_convert_fusion.1 = bf16[16,16,4,10,128]{4,3,2,1,0:T(8,128)(2,1)S(1)} fusion(f32[16,16,4,10,128]{4,3,2,1,0:T(8,128)} %reshape.404, f32[4,10,128]{2,1,0:T(8,128)S(1)} %mul.74, f32[16,16]{1,0:T(8,128)S(1)} %add_rsqrt_fusion.1), kind=kLoop, calls=%fused_computation.24 | loop fusion | flops 3932160 | bytes 7885824 | tf_op jit(solution)/shard_map/convert_element_type | solution.py:16
  34.1 4.5 %copy.31 = bf16[16,16,4,10,128]{4,1,3,0,2:T(8,128)(2,1)} copy(bf16[16,16,4,10,128]{4,3,2,1,0:T(8,128)(2,1)S(1)} %multiply_convert_fusion.1) | data formatting | bytes 5242880 | tf_op jit(solution)/shard_map/convert_element_type | solution.py:16
  38.7 13.7 %all-to-all-done.1 = bf16[16,16,4,10,128]{4,1,3,0,2:T(8,128)(2,1)S(1)} async-done(((bf16[16,16,4,10,128]{4,1,3,0,2:T(8,128)(2,1)}), bf16[16,16,4,10,128]{4,1,3,0,2:T(8,128)(2,1)S(1)}, u32[]{:S(2)}, u32[]{:S(2)}) %all-to-all-start.1) | async-done | bytes 2621472 | tf_op jit(solution)/shard_map/all_to_all | solution.py:106
  52.4 4.7 %all-to-all-start = ((bf16[16,16,4,10,128]{4,1,3,0,2:T(8,128)(2,1)}), bf16[16,16,4,10,128]{4,1,3,0,2:T(8,128)(2,1)}, u32[]{:S(2)}, u32[]{:S(2)}) async-start(bf16[16,16,4,10,128]{4,1,3,0,2:T(8,128)(2,1)} %copy.31), calls=%async_computation | async-start | bytes 5242880 | tf_op jit(solution)/shard_map/all_to_all | solution.py:105
  57.1 6.4 %reshape_squeeze.3 = bf16[16,16,4,10,128]{4,3,2,1,0:T(8,128)(2,1)} reshape(bf16[1,16,16,5120]{3,2,1,0:T(8,128)(2,1)} %param.14) | data formatting | bytes 5242880 | tf_op jit(solution)/shard_map/reshape;squeeze | solution.py:102
  63.5 6.7 %copy.35 = bf16[16,16,4,10,128]{4,1,3,0,2:T(8,128)(2,1)} copy(bf16[16,16,4,10,128]{4,3,2,1,0:T(8,128)(2,1)} %reshape_squeeze.3) | data formatting | bytes 5242880 | tf_op jit(solution)/shard_map/reshape;squeeze | solution.py:102
  70.2 18.1 %all-to-all-done = bf16[16,16,4,10,128]{4,1,3,0,2:T(8,128)(2,1)} async-done(((bf16[16,16,4,10,128]{4,1,3,0,2:T(8,128)(2,1)}), bf16[16,16,4,10,128]{4,1,3,0,2:T(8,128)(2,1)}, u32[]{:S(2)}, u32[]{:S(2)}) %all-to-all-start) | async-done | bytes 2621472 | tf_op jit(solution)/shard_map/all_to_all | solution.py:105
  88.3 4.5 %all-to-all-start.2 = ((bf16[16,16,4,10,128]{4,1,3,0,2:T(8,128)(2,1)}), bf16[16,16,4,10,128]{4,1,3,0,2:T(8,128)(2,1)}, u32[]{:S(2)}, u32[]{:S(2)}) async-start(bf16[16,16,4,10,128]{4,1,3,0,2:T(8,128)(2,1)} %copy.35), calls=%async_computation.2 | async-start | bytes 5242880 | tf_op jit(solution)/shard_map/all_to_all | solution.py:107
  92.9 2.3 copy.34
  95.2 2.5 copy.32
  97.7 26.6 %all-to-all-done.2 = bf16[16,16,4,10,128]{4,1,3,0,2:T(8,128)(2,1)} async-done(((bf16[16,16,4,10,128]{4,1,3,0,2:T(8,128)(2,1)}), bf16[16,16,4,10,128]{4,1,3,0,2:T(8,128)(2,1)}, u32[]{:S(2)}, u32[]{:S(2)}) %all-to-all-start.2) | async-done | bytes 2621472 | tf_op jit(solution)/shard_map/all_to_all | solution.py:107
  124.3 4.0 %copy.36 = bf16[16,16,4,10,128]{4,1,2,0,3:T(8,128)(2,1)} copy(bf16[16,16,4,10,128]{4,1,3,0,2:T(8,128)(2,1)} %all-to-all-done.2) | data formatting | bytes 5242880 | tf_op jit(solution)/shard_map/all_to_all | solution.py:107
  128.3 52.7 %while.10 = (s32[]{:T(128)}, bf16[10,1024,128]{2,1,0:T(8,128)(2,1)}, bf16[10,1024,128]{2,1,0:T(8,128)(2,1)S(1)}, bf16[10,1024,128]{2,1,0:T(8,128)(2,1)}, bf16[10,1024,128]{2,1,0:T(8,128)(2,1)}, /*index=5*/s32[]{:T(128)}) while((s32[]{:T(128)}, bf16[10,1024,128]{2,1,0:T(8,128)(2,1)}, bf16[10,1024,128]{2,1,0:T(8,128)(2,1)S(1)}, ...), condition=%wide.region_7.8_spmd, body=%wide.region_4.7_spmd.sunk | while | flops 546437120 | bytes 13654085 | solution.py:39
  130.7 2.9 fusion.37
  136.0 2.9 fusion.37
  141.3 2.9 fusion.37
  146.5 2.9 fusion.37
  151.8 2.9 fusion.37
  157.1 2.9 fusion.37
  159.9 1.7 multiply_reduce_fusion.4
  162.3 2.9 fusion.37
  165.2 1.7 multiply_reduce_fusion.4
  167.6 2.9 fusion.37
  170.5 1.7 multiply_reduce_fusion.4
  172.9 2.9 fusion.37
  175.8 1.7 multiply_reduce_fusion.4
  178.2 2.9 fusion.37
  181.0 4.9 %copy.37 = bf16[16,64,1,10,128]{4,0,3,2,1:T(8,128)(2,1)} copy(bf16[16,64,1,10,128]{4,1,0,3,2:T(8,128)(2,1)} %bitcast.19) | data formatting | bytes 5242880 | tf_op jit(solution)/shard_map/reshape | solution.py:40
  186.0 4.0 %all-to-all-start.3 = ((bf16[16,64,1,10,128]{4,0,3,2,1:T(8,128)(2,1)}), bf16[16,64,1,10,128]{4,0,3,2,1:T(8,128)(2,1)S(1)}, u32[]{:S(2)}, u32[]{:S(2)}) async-start(bf16[16,64,1,10,128]{4,0,3,2,1:T(8,128)(2,1)} %copy.37), calls=%async_computation.3 | async-start | bytes 5242880 | tf_op jit(solution)/shard_map/all_to_all | solution.py:110
  193.0 28.1 %all-to-all-done.3 = bf16[16,64,1,10,128]{4,0,3,2,1:T(8,128)(2,1)S(1)} async-done(((bf16[16,64,1,10,128]{4,0,3,2,1:T(8,128)(2,1)}), bf16[16,64,1,10,128]{4,0,3,2,1:T(8,128)(2,1)S(1)}, u32[]{:S(2)}, u32[]{:S(2)}) %all-to-all-start.3) | async-done | bytes 2621472 | tf_op jit(solution)/shard_map/all_to_all | solution.py:110
  222.1 4.3 %copy.39 = bf16[16,16,4,1,10,128]{5,4,2,1,0,3:T(8,128)(2,1)} copy(bf16[16,16,4,1,10,128]{5,1,2,4,0,3:T(8,128)(2,1)S(1)} %bitcast.83) | data formatting | bytes 5242880 | tf_op jit(solution)/shard_map/all_to_all | solution.py:110
  226.3 5.1 %reshape.399 = bf16[16,16,5120]{2,1,0:T(8,128)(2,1)S(1)} reshape(bf16[16,16,4,1,10,128]{5,4,2,1,0,3:T(8,128)(2,1)} %copy.39) | data formatting | bytes 5242880 | tf_op jit(solution)/shard_map/reshape | solution.py:110
  231.5 2.2 gather_fusion.1
  233.7 3.6 select_select_fusion
  237.3 5.8 %all-to-all-start.4 = ((bf16[4,4,16,5120]{3,2,1,0:T(8,128)(2,1)}), bf16[4,4,16,5120]{3,2,1,0:T(8,128)(2,1)S(1)}, u32[]{:S(2)}, u32[]{:S(2)}) async-start(bf16[4,4,16,5120]{3,2,1,0:T(8,128)(2,1)} %bitcast.81), calls=%async_computation.4 | async-start | bytes 5242880 | tf_op jit(solution)/shard_map/all_to_all | solution.py:55
  244.0 58.3 %all-to-all-done.4 = bf16[4,4,16,5120]{3,2,1,0:T(8,128)(2,1)S(1)} async-done(((bf16[4,4,16,5120]{3,2,1,0:T(8,128)(2,1)}), bf16[4,4,16,5120]{3,2,1,0:T(8,128)(2,1)S(1)}, u32[]{:S(2)}, u32[]{:S(2)}) %all-to-all-start.4) | async-done | bytes 2621472 | tf_op jit(solution)/shard_map/all_to_all | solution.py:55
  306.3 2.2 gather_fusion
  308.5 3.6 select_select_fusion.1
  312.1 3.7 all-to-all-start.5
  316.4 58.2 %all-to-all-done.5 = bf16[4,4,16,5120]{3,2,1,0:T(8,128)(2,1)S(1)} async-done(((bf16[4,4,16,5120]{3,2,1,0:T(8,128)(2,1)}), bf16[4,4,16,5120]{3,2,1,0:T(8,128)(2,1)S(1)}, u32[]{:S(2)}, u32[]{:S(2)}) %all-to-all-start.5) | async-done | bytes 2621472 | tf_op jit(solution)/shard_map/all_to_all | solution.py:135
  374.6 2.2 gather_fusion.2
  376.8 3.5 select_bitcast_fusion
  (69 shorter events, 26.9 us)
Async XLA Ops:
  0.6 6.8 %copy-start.1 = (bf16[1,16,16,5120]{3,2,1,0:T(8,128)(2,1)S(1)}, bf16[1,16,16,5120]{3,2,1,0:T(8,128)(2,1)}, u32[]{:S(2)}) copy-start(bf16[1,16,16,5120]{3,2,1,0:T(8,128)(2,1)} %param.13) | copy-start | bytes 7864324
  7.5 0.7 copy-start.2
  16.9 35.5 %all-to-all-start.1 = ((bf16[16,16,4,10,128]{4,1,3,0,2:T(8,128)(2,1)}), bf16[16,16,4,10,128]{4,1,3,0,2:T(8,128)(2,1)S(1)}, u32[]{:S(2)}, u32[]{:S(2)}) async-start(bf16[16,16,4,10,128]{4,1,3,0,2:T(8,128)(2,1)} %copy.33), calls=%async_computation.1 | async-start | bytes 5242880 | tf_op jit(solution)/shard_map/all_to_all | solution.py:106
  21.1 6.7 %copy-start.3 = (f32[5120]{0:T(1024)S(1)}, f32[5120]{0:T(1024)}, u32[]{:S(2)}) copy-start(f32[5120]{0:T(1024)} %param.15) | copy-start | bytes 61444
  52.4 35.9 %all-to-all-start = ((bf16[16,16,4,10,128]{4,1,3,0,2:T(8,128)(2,1)}), bf16[16,16,4,10,128]{4,1,3,0,2:T(8,128)(2,1)}, u32[]{:S(2)}, u32[]{:S(2)}) async-start(bf16[16,16,4,10,128]{4,1,3,0,2:T(8,128)(2,1)} %copy.31), calls=%async_computation | async-start | bytes 5242880 | tf_op jit(solution)/shard_map/all_to_all | solution.py:105
  88.3 35.9 %all-to-all-start.2 = ((bf16[16,16,4,10,128]{4,1,3,0,2:T(8,128)(2,1)}), bf16[16,16,4,10,128]{4,1,3,0,2:T(8,128)(2,1)}, u32[]{:S(2)}, u32[]{:S(2)}) async-start(bf16[16,16,4,10,128]{4,1,3,0,2:T(8,128)(2,1)} %copy.35), calls=%async_computation.2 | async-start | bytes 5242880 | tf_op jit(solution)/shard_map/all_to_all | solution.py:107
  186.0 4.0 %copy-start.6 = (s32[4]{0:T(128)S(1)}, s32[4]{0:T(128)}, u32[]{:S(2)}) copy-start(s32[4]{0:T(128)} %param.18) | copy-start | bytes 52
  186.0 4.7 %copy-start.5 = (s32[4]{0:T(128)S(1)}, s32[4]{0:T(128)}, u32[]{:S(2)}) copy-start(s32[4]{0:T(128)} %param.17) | copy-start | bytes 52
  186.0 35.1 %all-to-all-start.3 = ((bf16[16,64,1,10,128]{4,0,3,2,1:T(8,128)(2,1)}), bf16[16,64,1,10,128]{4,0,3,2,1:T(8,128)(2,1)S(1)}, u32[]{:S(2)}, u32[]{:S(2)}) async-start(bf16[16,64,1,10,128]{4,0,3,2,1:T(8,128)(2,1)} %copy.37), calls=%async_computation.3 | async-start | bytes 5242880 | tf_op jit(solution)/shard_map/all_to_all | solution.py:110
  237.3 5.9 %copy-start.4 = (s32[4,16]{1,0:T(4,128)S(1)}, s32[4,16]{1,0:T(4,128)}, u32[]{:S(2)}) copy-start(s32[4,16]{1,0:T(4,128)} %param.19) | copy-start | bytes 772
  237.3 65.1 %all-to-all-start.4 = ((bf16[4,4,16,5120]{3,2,1,0:T(8,128)(2,1)}), bf16[4,4,16,5120]{3,2,1,0:T(8,128)(2,1)S(1)}, u32[]{:S(2)}, u32[]{:S(2)}) async-start(bf16[4,4,16,5120]{3,2,1,0:T(8,128)(2,1)} %bitcast.81), calls=%async_computation.4 | async-start | bytes 5242880 | tf_op jit(solution)/shard_map/all_to_all | solution.py:55
  306.3 2.2 copy-start
  312.1 62.6 %all-to-all-start.5 = ((bf16[4,4,16,5120]{3,2,1,0:T(8,128)(2,1)}), bf16[4,4,16,5120]{3,2,1,0:T(8,128)(2,1)S(1)}, u32[]{:S(2)}, u32[]{:S(2)}) async-start(bf16[4,4,16,5120]{3,2,1,0:T(8,128)(2,1)} %select_select_fusion.1), calls=%async_computation.5 | async-start | bytes 5242880 | tf_op jit(solution)/shard_map/all_to_all | solution.py:135
where the time goes:
time: 382 us; the launch traced here: 380 us
  waiting for transfers between devices  203 us (53%)
  local copies, waits for them, and re-layouts  71.6 us (19%)
  matrix products  46.2 us (12%)
  other arithmetic  31.1 us (8%)
  starting transfers between devices  27 us (7%)
    all_to_all x1, waiting for transfers between devices, send_owners(): lax.all_to_all(packed, 'win', split_axis=0, concat_axis=0, tiled=True)  58.3 us
    all_to_all x1, waiting for transfers between devices, per_device(): lax.all_to_all(outgoing, 'win', split_axis=0, concat_axis=0, tiled=True)  58.2 us
    dot_general x10, matrix products, head_attention(): jnp.dot(weights, value_head, preferred_element_type=jnp.float32)  28.7 us
    all_to_all x1, waiting for transfers between devices, per_device(): lax.all_to_all(attended, 'uly', split_axis=1, concat_axis=2, tiled=True)  28.1 us
    all_to_all x1, waiting for transfers between devices, per_device(): lax.all_to_all(value_heads, 'uly', split_axis=2, concat_axis=1, tiled=True)  26.6 us
    all_to_all x1, waiting for transfers between devices, per_device(): lax.all_to_all(query_heads, 'uly', split_axis=2, concat_axis=1, tiled=True)  18.1 us
    dot_general x10, matrix products, head_attention(): jnp.dot(query_head, key_head.T, preferred_element_type=jnp.float32)  16.6 us
    all_to_all x1, waiting for transfers between devices, per_device(): lax.all_to_all(key_heads, 'uly', split_axis=2, concat_axis=1, tiled=True)  13.7 us
  transfers between devices with their start and end apart: 6, of which 6 were waited for; matrix products, arithmetic and copies ran while one was open for 10% of the time, Pallas kernels for 0%

commit v1 on v0

v1 whole, which is shorter than its diff:
```python
import functools
import math

import jax
import jax.numpy as jnp
from jax import lax
from jax.experimental import pallas as pl
from jax.experimental.pallas import tpu as pltpu
from jax.sharding import PartitionSpec as P

HEADS = 40
WF = 16
FR = 12
MARGIN = WF - FR
SHIFT = FR // 2
NEXT = SHIFT + MARGIN
CHUNK_HEADS = (8, 8, 8, 8, 8)
VMEM_LIMIT = 48 * 1024 * 1024


def params():
    return pltpu.CompilerParams(vmem_limit_bytes=VMEM_LIMIT)


def normalized(rows, gain):
    floats = rows.astype(jnp.float32)
    mean_square = jnp.mean(floats * floats, axis=-1, keepdims=True)
    return (floats * lax.rsqrt(mean_square + 1e-06) * gain).astype(jnp.bfloat16)


def query_kernel(query_ref, gain_ref, out_ref):
    out_ref[...] = normalized(query_ref[...], gain_ref[...])


def normalize_queries(rows, gain, frames_per_step=4):
    frames, tokens, features = rows.shape
    block = (frames_per_step, tokens, features)
    return pl.pallas_call(
        query_kernel,
        grid=(frames // frames_per_step,),
        in_specs=[
            pl.BlockSpec(block, lambda i: (i, 0, 0)),
            pl.BlockSpec((1, 1, features), lambda i: (0, 0, 0)),
        ],
        out_specs=pl.BlockSpec(block, lambda i: (i, 0, 0)),
        out_shape=jax.ShapeDtypeStruct(rows.shape, jnp.bfloat16),
        compiler_params=params(),
        cost_estimate=pl.CostEstimate(
            flops=rows.size * 6, bytes_accessed=rows.size * 4, transcendentals=0
        ),
        name="query_norm",
    )(rows, gain)


def pack_kernel(key_ref, value_ref, gain_ref, *out_refs):
    keys = normalized(key_ref[...], gain_ref[...])
    offset = 0
    for out_ref in out_refs:
        width = out_ref.shape[-1]
        out_ref[0] = keys[:, :, offset : offset + width]
        out_ref[1] = value_ref[:, :, offset : offset + width]
        offset += width


def pack_keys_values(key_rows, value_rows, gain, widths, frames_per_step=4):
    frames, tokens, features = key_rows.shape
    block = (frames_per_step, tokens, features)
    return pl.pallas_call(
        pack_kernel,
        grid=(frames // frames_per_step,),
        in_specs=[
            pl.BlockSpec(block, lambda i: (i, 0, 0)),
            pl.BlockSpec(block, lambda i: (i, 0, 0)),
            pl.BlockSpec((1, 1, features), lambda i: (0, 0, 0)),
        ],
        out_specs=[
            pl.BlockSpec((2, frames_per_step, tokens, width), lambda i: (0, i, 0, 0))
            for width in widths
        ],
        out_shape=[
            jax.ShapeDtypeStruct((2, frames, tokens, width), jnp.bfloat16) for width in widths
        ],
        compiler_params=params(),
        cost_estimate=pl.CostEstimate(
            flops=key_rows.size * 6, bytes_accessed=key_rows.size * 8, transcendentals=0
        ),
        name="key_norm_pack",
    )(key_rows, value_rows, gain)


def attention_kernel(head_size, query_ref, *refs):
    sources, (out_ref, first_ref, last_ref) = refs[:-3], refs[-3:]
    frames, tokens, width = query_ref.shape
    rows = frames * tokens
    factor = math.log2(math.e) / math.sqrt(head_size)
    contract = (((1,), (1,)), ((), ()))
    for start in range(0, width, head_size):
        columns = slice(start, start + head_size)
        query = query_ref[:, :, columns].reshape(rows, head_size)
        scores = [
            lax.dot_general(
                query,
                source[0, :, :, columns].reshape(rows, head_size),
                contract,
                preferred_element_type=jnp.float32,
            )
            for source in sources
        ]
        row_max = functools.reduce(jnp.maximum, scores)
        row_max = jnp.max(row_max, axis=-1, keepdims=True)
        exponents = [jnp.exp2((score - row_max) * factor) for score in scores]
        total = jnp.sum(functools.reduce(jnp.add, exponents), axis=-1, keepdims=True)
        inverse = 1.0 / total
        result = jnp.zeros((rows, head_size), jnp.float32)
        for exponent, source in zip(exponents, sources):
            weights = (exponent * inverse).astype(jnp.bfloat16)
            result += jnp.dot(
                weights,
                source[1, :, :, columns].reshape(rows, head_size),
                preferred_element_type=jnp.float32,
            )
        result = result.astype(jnp.bfloat16).reshape(frames, tokens, head_size)
        out_ref[:, :, columns] = result
        first_ref[:, :, columns] = result[:MARGIN]
        last_ref[:, :, columns] = result[frames - MARGIN :]


def attend(queries, sources, base, width, head_size, block_width):
    frames, tokens, _ = queries.shape
    base_block = base // block_width
    rows = frames * tokens
    heads = width // head_size
    keys = rows * len(sources)

    def spec(count):
        return pl.BlockSpec((count, tokens, block_width), lambda i: (0, 0, i))

    return pl.pallas_call(
        functools.partial(attention_kernel, head_size),
        grid=(width // block_width,),
        in_specs=[
            pl.BlockSpec((frames, tokens, block_width), lambda i: (0, 0, base_block + i))
        ]
        + [
            pl.BlockSpec((2, frames, tokens, block_width), lambda i: (0, 0, 0, i))
            for _ in sources
        ],
        out_specs=[spec(frames), spec(MARGIN), spec(MARGIN)],
        out_shape=[
            jax.ShapeDtypeStruct((count, tokens, width), jnp.bfloat16)
            for count in (frames, MARGIN, MARGIN)
        ],
        compiler_params=params(),
        cost_estimate=pl.CostEstimate(
            flops=4 * rows * keys * width,
            bytes_accessed=rows * width * 4 * (1 + len(sources)),
            transcendentals=rows * keys * heads,
        ),
        name="attention",
    )(queries, *sources)


def phase_of(owner_ref, wanted, windows):
    phase = jnp.int32(0)
    for index in range(windows):
        phase = jnp.where(owner_ref[index] == wanted, index, phase)
    return phase


def first_owned(phase, windows):
    return lax.rem(phase + (windows - 1) * MARGIN, windows)


def extra_owned(windows):
    return [i for i in range(FR // windows) if windows * (i + 1) > NEXT]


def blend_kernel(
    windows, place_ref, start_ref, owner_ref, weight_ref, out_ref, before_ref, after_ref, home_ref, *sent_refs
):
    here = place_ref[0]
    before = lax.rem(here + windows - 1, windows)
    after = lax.rem(here + 1, windows)
    offset = start_ref[here] - here * FR
    offset_before = start_ref[before] - before * FR
    offset_after = start_ref[after] - after * FR
    for frame in range(FR):
        place = frame + MARGIN - offset
        weight = weight_ref[here, place].astype(jnp.float32)
        numerator = out_ref[place].astype(jnp.float32) * weight
        denominator = weight
        if frame < MARGIN:
            valid = frame < offset_before
            slot = jnp.minimum(frame + MARGIN - offset_before, MARGIN - 1)
            weight = jnp.where(valid, weight_ref[before, slot + FR], 0).astype(jnp.float32)
            numerator += before_ref[slot].astype(jnp.float32) * weight
            denominator += weight
        if frame >= FR - MARGIN:
            slot = frame - (FR - MARGIN) - offset_after
            valid = slot >= 0
            slot = jnp.maximum(slot, 0)
            weight = jnp.where(valid, weight_ref[after, slot], 0).astype(jnp.float32)
            numerator += after_ref[slot].astype(jnp.float32) * weight
            denominator += weight
        home_ref[frame] = (numerator / denominator).astype(jnp.bfloat16)
    for step, sent_ref in enumerate(sent_refs, 1):
        target = lax.rem(here + step, windows)
        first = first_owned(phase_of(owner_ref, target, windows), windows)
        if step < windows - 1:
            for index in range(FR // windows):
                sent_ref[index] = home_ref[first + index * windows]
        else:
            sent_ref[:NEXT] = home_ref[:NEXT]
            for slot, index in enumerate(extra_owned(windows)):
                sent_ref[NEXT + slot] = home_ref[first + index * windows]


def blend(tables, out, before, after, windows, block_width):
    _, tokens, width = out.shape
    counts = [FR] + [FR // windows] * (windows - 2) + [NEXT + len(extra_owned(windows))]

    def spec(count):
        return pl.BlockSpec((count, tokens, block_width), lambda i: (0, 0, i))

    return pl.pallas_call(
        functools.partial(blend_kernel, windows),
        grid=(width // block_width,),
        in_specs=[pl.BlockSpec(memory_space=pltpu.SMEM) for _ in tables]
        + [spec(out.shape[0]), spec(MARGIN), spec(MARGIN)],
        out_specs=[spec(count) for count in counts],
        out_shape=[jax.ShapeDtypeStruct((count, tokens, width), jnp.bfloat16) for count in counts],
        compiler_params=params(),
        cost_estimate=pl.CostEstimate(
            flops=tokens * width * FR * 8,
            bytes_accessed=tokens * width * 2 * (WF + 2 * MARGIN + sum(counts)),
            transcendentals=0,
        ),
        name="blend",
    )(*tables, out, before, after)


def place_kernel(windows, place_ref, start_ref, owner_ref, weight_ref, home_ref, *refs):
    received, (owned_ref, next_ref) = refs[: windows - 1], refs[-2:]
    here = place_ref[0]
    phase = phase_of(owner_ref, here, windows)
    first = first_owned(phase, windows)
    slot_base = (first + MARGIN) // windows
    count = FR // windows
    extra = extra_owned(windows)
    for step in range(windows):
        source = lax.rem(here + windows - step, windows)
        for index in range(count):
            slot = lax.rem(source * count + slot_base + index, FR)
            if step == 0:
                row = home_ref[first + index * windows]
            elif step < windows - 1:
                row = received[step - 1][index]
            elif index in extra:
                row = received[step - 1][NEXT + extra.index(index)]
            else:
                row = received[step - 1][first + index * windows]
            owned_ref[slot] = row
    offset = start_ref[here] - here * FR + SHIFT - MARGIN
    from_after = received[-1]
    for frame in range(WF):
        wanted = offset + frame
        if frame + MARGIN + SHIFT - MARGIN < FR:
            next_ref[frame] = home_ref[wanted]
        elif frame + SHIFT - MARGIN >= FR:
            next_ref[frame] = from_after[wanted - FR]
        else:
            inside = wanted < FR
            next_ref[frame] = jnp.where(
                inside,
                home_ref[jnp.minimum(wanted, FR - 1)],
                from_after[jnp.maximum(wanted - FR, 0)],
            )


def place(tables, home, received, base, features, targets, windows, block_width):
    _, tokens, width = home.shape
    base_block = base // block_width

    def spec(count):
        return pl.BlockSpec((count, tokens, block_width), lambda i: (0, 0, i))

    def out_spec(count):
        return pl.BlockSpec((count, tokens, block_width), lambda i: (0, 0, base_block + i))

    operands = (*tables, home, *received)
    return pl.pallas_call(
        functools.partial(place_kernel, windows),
        grid=(width // block_width,),
        in_specs=[pl.BlockSpec(memory_space=pltpu.SMEM) for _ in tables]
        + [spec(array.shape[0]) for array in (home, *received)]
        + [pl.BlockSpec(memory_space=pl.ANY) for _ in targets],
        out_specs=[out_spec(FR), out_spec(WF)],
        out_shape=[
            jax.ShapeDtypeStruct((count, tokens, features), jnp.bfloat16) for count in (FR, WF)
        ],
        input_output_aliases={len(operands) + i: i for i in range(len(targets))},
        compiler_params=params(),
        cost_estimate=pl.CostEstimate(
            flops=0, bytes_accessed=tokens * width * 4 * (FR + WF), transcendentals=0
        ),
        name="place",
    )(*operands, *targets)


def exchange(array, axis, bit):
    return lax.ppermute(array, axis, [(i, i ^ bit) for i in range(lax.axis_size(axis))])


def shift(array, axis, step):
    count = lax.axis_size(axis)
    return lax.ppermute(array, axis, [(i, (i + step) % count) for i in range(count)])


def gather_blocks(array, axis):
    count = lax.axis_size(axis)
    if count & (count - 1):
        gathered = lax.all_gather(array, axis)
        return [gathered[i] for i in range(count)]
    blocks = [array]
    bit = count // 2
    while bit:
        blocks += [exchange(block, axis, bit) for block in blocks]
        bit //= 2
    return blocks


def table_lookup(table_row, wanted, length):
    entries = jnp.arange(length, dtype=jnp.int32)
    return jnp.sum(jnp.where(wanted[..., None] == entries, table_row, 0), axis=-1)


def send_owners(frame_rows, inverse, my_start, windows, capacity):
    slot_index = jnp.arange(capacity, dtype=jnp.int32)
    position_in = (inverse[:, None] - my_start) % windows + slot_index[None, :] * windows
    is_valid = (position_in < WF).reshape(-1)
    picked = jnp.take(frame_rows, jnp.minimum(position_in, WF - 1).reshape(-1), axis=0)
    picked = jnp.where(is_valid[:, None, None], picked, jnp.zeros_like(picked))
    packed = picked.reshape(windows, capacity, frame_rows.shape[1], frame_rows.shape[2])
    return lax.all_to_all(packed, "win", split_axis=0, concat_axis=0, tiled=True)


def combine_owned(received, window_start, blend_weight, my_phase, windows, frames_total, capacity):
    slot_index = jnp.arange(capacity, dtype=jnp.int32)
    source_pos = (my_phase - window_start[:, None]) % windows + slot_index[None, :] * windows
    arrived = source_pos < WF
    slot_at = (window_start[:, None] + source_pos) % frames_total // windows
    factor = table_lookup(blend_weight[:, None, :], source_pos, WF)
    owned_range = jnp.arange(FR, dtype=jnp.int32)
    mixing = jnp.where(
        (slot_at[None] == owned_range[:, None, None]) & arrived[None], factor[None], 0
    )
    mixing = mixing.reshape(FR, windows * capacity).astype(jnp.float32)
    numerator = jnp.dot(
        mixing.astype(jnp.bfloat16),
        received.reshape(windows * capacity, -1),
        preferred_element_type=jnp.float32,
    )
    denominator = jnp.sum(mixing, axis=1)
    owned = (numerator / denominator[:, None]).astype(jnp.bfloat16)
    return owned.reshape(FR, received.shape[2], received.shape[3])


def blend_by_owners(own_out, window_start, owner_of_phase, blend_weight):
    windows = lax.axis_size("win")
    position = lax.axis_index("win")
    frames_total = FR * windows
    capacity = (WF + windows - 1) // windows
    _, local_tokens, feature_count = own_out.shape
    phases = jnp.arange(windows, dtype=jnp.int32)
    inverse = jnp.sum(
        jnp.where(owner_of_phase[None, :] == phases[:, None], phases[None, :], 0), axis=1
    )
    my_start = window_start[position]
    my_phase = inverse[position]
    frame_range = jnp.arange(WF, dtype=jnp.int32)
    received = send_owners(own_out, inverse, my_start, windows, capacity)
    owned = combine_owned(
        received, window_start, blend_weight, my_phase, windows, frames_total, capacity
    )
    slot_index = jnp.arange(capacity, dtype=jnp.int32)
    target_pos = (my_phase - window_start[:, None] - SHIFT) % windows + slot_index[
        None, :
    ] * windows
    target_valid = (target_pos < WF).reshape(-1)
    target_slot = (
        (window_start[:, None] + SHIFT + target_pos) % frames_total // windows
    ).reshape(-1)
    outgoing = jnp.take(owned, target_slot, axis=0)
    outgoing = jnp.where(target_valid[:, None, None], outgoing, jnp.zeros_like(outgoing))
    outgoing = outgoing.reshape(windows, capacity, local_tokens, feature_count)
    returned = lax.all_to_all(outgoing, "win", split_axis=0, concat_axis=0, tiled=True)
    needed_phase = (my_start + SHIFT + frame_range) % windows
    source_owner = table_lookup(owner_of_phase[None, :], needed_phase, windows)
    flat_index = source_owner * capacity + frame_range // windows
    next_rows = jnp.take(
        returned.reshape(windows * capacity, local_tokens, feature_count), flat_index, axis=0
    )
    return owned, next_rows


def per_device(
    query_rows,
    key_rows,
    value_rows,
    query_gain,
    key_gain,
    window_start,
    owner_of_phase,
    blend_weight,
):
    windows = lax.axis_size("win")
    features = query_rows.shape[-1]
    head_size = features // HEADS
    block_width = 2 * head_size
    widths = [heads * head_size for heads in CHUNK_HEADS]
    packed = pack_keys_values(
        key_rows[0], value_rows[0], key_gain.reshape(1, 1, features), widths
    )
    queries = normalize_queries(query_rows[0], query_gain.reshape(1, 1, features))
    direct = windows >= 3 and FR % windows == 0
    tables = (
        lax.axis_index("win").astype(jnp.int32).reshape(1),
        window_start,
        owner_of_phase,
        blend_weight,
    )
    targets = ()
    whole = []
    base = 0
    for width, own in zip(widths, packed):
        out, first, last = attend(
            queries, gather_blocks(own, "uly"), base, width, head_size, block_width
        )
        if direct:
            before = shift(last, "win", 1)
            after = shift(first, "win", -1)
            home, *sent = blend(tables, out, before, after, windows, block_width)
            received = [shift(array, "win", step) for step, array in enumerate(sent, 1)]
            targets = place(tables, home, received, base, features, targets, windows, block_width)
        else:
            whole.append(out)
        base += width
    if direct:
        owned, next_rows = targets
    else:
        owned, next_rows = blend_by_owners(
            jnp.concatenate(whole, axis=-1), window_start, owner_of_phase, blend_weight
        )
    return (owned, next_rows[None])


def solution(mesh):
    placed = (
        P(("grp", "win"), None, "uly", None),
        P(("grp", "win"), None, "uly", None),
        P(("grp", "win"), None, "uly", None),
        P(),
        P(),
        P("grp"),
        P("grp"),
        P("grp", None),
    )
    return jax.shard_map(
        per_device,
        mesh=mesh,
        in_specs=placed,
        out_specs=(P(("grp", "win"), "uly", None), P(("grp", "win"), None, "uly", None)),
        check_vma=False,
    )
```

time: 382 us -> 271 us (0.71)
  waiting for transfers between devices: 203 us -> 122 us
  Pallas kernels: 0 us -> 62.7 us
  local copies, waits for them, and re-layouts: 71.6 us -> 13.5 us
  matrix products: 46.2 us -> 0 us
  starting transfers between devices: 27 us -> 71.5 us
  other arithmetic: 31.1 us -> 0 us
    all_to_all x6 -> x0, waiting for transfers between devices: 203 us -> none  [the longest x1 58.3 us: send_owners(): lax.all_to_all(packed, 'win', split_axis=0, concat_axis=0, tiled=True)]
    ppermute x0 -> x40, waiting for transfers between devices: none -> 122 us  [the longest x15 102 us: exchange(): lax.ppermute(array, axis, [(i, i ^ bit) for i in range(lax.axis_size(axis...]
    ppermute x0 -> x40, starting transfers between devices: none -> 71.5 us  [the longest x25 61.1 us: shift(): lax.ppermute(array, axis, [(i, (i + step) % count) for i in range(count)])]
    pallas_call x0 -> x17, Pallas kernels: none -> 62.7 us  [the longest x5 36.6 us: attend(): pl.pallas_call(functools.partial(attention_kernel, head_size), grid=(widt...]
    dot_general x21 -> x0, matrix products: 46.2 us -> none  [the longest x10 28.7 us: head_attention(): jnp.dot(weights, value_head, preferred_element_type=jnp.float32)]
    all_to_all x6 -> x0, starting transfers between devices: 27 us -> none  [the longest x1 5.85 us: send_owners(): lax.all_to_all(packed, 'win', split_axis=0, concat_axis=0, tiled=True)]
    convert_element_type x4 -> x0, local copies, waits for them, and re-layouts: 22.6 us -> none  [the longest x2 13.5 us: normalize(): floats = row_block.astype(jnp.float32)]
    all_to_all x5 -> x0, local copies, waits for them, and re-layouts: 14.1 us -> none  [the longest x2 5.28 us: per_device(): lax.all_to_all(attended, 'uly', split_axis=1, concat_axis=2, tiled=True)]
  transfers between devices with their start and end apart: 6 -> 40, of which waited for: 6 -> 8; matrix products, arithmetic and copies ran while one was open for 10% -> 0% of each run, Pallas kernels for 0% -> 21%
where the time goes in v1:
time: 271 us
  waiting for transfers between devices  122 us (45%)
  starting transfers between devices  71.5 us (26%)
  Pallas kernels  62.7 us (23%)
  local copies, waits for them, and re-layouts  13.5 us (5%)
    ppermute x15, waiting for transfers between devices, exchange(): lax.ppermute(array, axis, [(i, i ^ bit) for i in range(lax.axis_size(axis...  102 us
    ppermute x25, starting transfers between devices, shift(): lax.ppermute(array, axis, [(i, (i + step) % count) for i in range(count)])  61.1 us
    pallas_call x5, Pallas kernels, attend(): pl.pallas_call(functools.partial(attention_kernel, head_size), grid=(widt...  36.6 us
    ppermute x25, waiting for transfers between devices, shift(): lax.ppermute(array, axis, [(i, (i + step) % count) for i in range(count)])  19.9 us
    unnamed x46, local copies, waits for them, and re-layouts  13.5 us
    pallas_call x5, Pallas kernels, place(): pl.pallas_call(functools.partial(place_kernel, windows), grid=(width // b...  11.8 us
    ppermute x15, starting transfers between devices, exchange(): lax.ppermute(array, axis, [(i, i ^ bit) for i in range(lax.axis_size(axis...  10.4 us
    pallas_call x5, Pallas kernels, blend(): pl.pallas_call(functools.partial(blend_kernel, windows), grid=(width // b...  8.36 us
  transfers between devices with their start and end apart: 40, of which 8 were waited for; matrix products, arithmetic and copies ran while one was open for 0% of the time, Pallas kernels for 21%

profile of v1, /device:TPU:0, one launch (start us, length us, event | category | flops | bytes accessed | tf_op | source)
XLA Modules:
  0.0 270.7 jit_solution(6283051473102086036)
XLA Ops:
  1.4 4.4 %key_norm_pack.1 = (bf16[2,16,16,1024]{3,2,1,0:T(8,128)(2,1)S(1)}, bf16[2,16,16,1024]{3,2,1,0:T(8,128)(2,1)S(1)}, bf16[2,16,16,1024]{3,2,1,0:T(8,128)(2,1)S(1)},...) custom-call(bf16[16,16,5120]{2,1,0:T(8,128)(2,1)} %bitcast.11, bf16[16,16,5120]{2,1,0:T(8,128)(2,1)} %bitcast.12, ...), custom_call_target="tpu_custom_call" | custom-call | flops 7864320 | bytes 10485760 | tf_op jit(solution)/shard_map/key_norm_pack/pallas_call | solution.py:68
  5.8 3.0 %collective-permute-start = (bf16[2,16,16,1024]{3,2,1,0:T(8,128)(2,1)S(1)}, bf16[2,16,16,1024]{3,2,1,0:T(8,128)(2,1)S(1)}, u32[]{:S(2)}, u32[]{:S(2)}) collective-permute-start(bf16[2,16,16,1024]{3,2,1,0:T(8,128)(2,1)S(1)} %get-tuple-element.52.refs_0_), channel_id=1, source_target_pairs={{0,2},{1,3},{2,0},{3,1},{4,6},{5,7},{6,4},{7,5},{8,10},{9,11},{10,... | collective-permute-start | bytes 3145736 | tf_op jit(solution)/shard_map/ppermute | solution.py:311
  9.3 1.7 collective-permute-start.16
  11.0 21.7 %collective-permute-done.refs_1_ = bf16[2,16,16,1024]{3,2,1,0:T(8,128)(2,1)S(1)} collective-permute-done((bf16[2,16,16,1024]{3,2,1,0:T(8,128)(2,1)S(1)}, bf16[2,16,16,1024]{3,2,1,0:T(8,128)(2,1)S(1)}, u32[]{:S(2)}, u32[]{:S(2)}) %collective-permute-start) | collective-permute-done | bytes 1048608 | tf_op jit(solution)/shard_map/ppermute | solution.py:311
  32.8 2.1 collective-permute-start.24
  35.8 19.4 %collective-permute-done.8.refs_1_ = bf16[2,16,16,1024]{3,2,1,0:T(8,128)(2,1)S(1)} collective-permute-done((bf16[2,16,16,1024]{3,2,1,0:T(8,128)(2,1)S(1)}, bf16[2,16,16,1024]{3,2,1,0:T(8,128)(2,1)S(1)}, u32[]{:S(2)}, u32[]{:S(2)}) %collective-permute-start.8) | collective-permute-done | bytes 1048608 | tf_op jit(solution)/shard_map/ppermute | solution.py:311
  55.2 2.1 collective-permute-start.32
  58.3 19.4 %collective-permute-done.16.refs_1_ = bf16[2,16,16,1024]{3,2,1,0:T(8,128)(2,1)S(1)} collective-permute-done((bf16[2,16,16,1024]{3,2,1,0:T(8,128)(2,1)S(1)}, bf16[2,16,16,1024]{3,2,1,0:T(8,128)(2,1)S(1)}, u32[]{:S(2)}, u32[]{:S(2)}) %collective-permute-start.16) | collective-permute-done | bytes 1048608 | tf_op jit(solution)/shard_map/ppermute | solution.py:311
  78.7 21.5 %collective-permute-done.24.refs_1_ = bf16[2,16,16,1024]{3,2,1,0:T(8,128)(2,1)S(1)} collective-permute-done((bf16[2,16,16,1024]{3,2,1,0:T(8,128)(2,1)S(1)}, bf16[2,16,16,1024]{3,2,1,0:T(8,128)(2,1)S(1)}, u32[]{:S(2)}, u32[]{:S(2)}) %collective-permute-start.24) | collective-permute-done | bytes 1048608 | tf_op jit(solution)/shard_map/ppermute | solution.py:311
  100.2 1.0 copy-done.6
  101.7 20.1 %collective-permute-done.32.refs_1_ = bf16[2,16,16,1024]{3,2,1,0:T(8,128)(2,1)S(1)} collective-permute-done((bf16[2,16,16,1024]{3,2,1,0:T(8,128)(2,1)S(1)}, bf16[2,16,16,1024]{3,2,1,0:T(8,128)(2,1)S(1)}, u32[]{:S(2)}, u32[]{:S(2)}) %collective-permute-start.32) | collective-permute-done | bytes 1048608 | tf_op jit(solution)/shard_map/ppermute | solution.py:311
  123.3 1.1 copy-done.10
  124.4 1.5 query_norm.1.query_ref
  125.9 1.5 copy-done
  127.4 1.2 copy-done.3
  128.6 1.2 copy-done.13
  129.9 7.0 %attention.6 = (bf16[16,16,1024]{2,1,0:T(8,128)(2,1)S(1)}, bf16[4,16,1024]{2,1,0:T(8,128)(2,1)S(1)}, bf16[4,16,1024]{2,1,0:T(8,128)(2,1)S(1)}) custom-call(bf16[16,16,5120]{2,1,0:T(8,128)(2,1)} %copy-done, bf16[2,16,16,1024]{3,2,1,0:T(8,128)(2,1)S(1)} %get-tuple-element.60.refs_0_, bf16[2,16,16,1024]{3,2,1,0:T(8,128)(2,1)S(1)} %collective-permute-done.8.refs_1_, ...), custom_call_target="tpu_custom_call" | custom-call | flops 1073741824 | bytes 5242880 | tf_op jit(solution)/shard_map/attention/pallas_call | solution.py:138
  136.9 1.2 copy-done.11
  138.1 7.0 %attention.7 = (bf16[16,16,1024]{2,1,0:T(8,128)(2,1)S(1)}, bf16[4,16,1024]{2,1,0:T(8,128)(2,1)S(1)}, bf16[4,16,1024]{2,1,0:T(8,128)(2,1)S(1)}) custom-call(bf16[16,16,5120]{2,1,0:T(8,128)(2,1)} %copy-done, bf16[2,16,16,1024]{3,2,1,0:T(8,128)(2,1)S(1)} %get-tuple-element.68.refs_0_, bf16[2,16,16,1024]{3,2,1,0:T(8,128)(2,1)S(1)} %copy-done.9, ...), custom_call_target="tpu_custom_call" | custom-call | flops 1073741824 | bytes 5242880 | tf_op jit(solution)/shard_map/attention/pallas_call | solution.py:138
  145.2 1.9 collective-permute-start.11
  147.1 7.5 %attention.8 = (bf16[16,16,1024]{2,1,0:T(8,128)(2,1)S(1)}, bf16[4,16,1024]{2,1,0:T(8,128)(2,1)}, bf16[4,16,1024]{2,1,0:T(8,128)(2,1)S(1)}) custom-call(bf16[16,16,5120]{2,1,0:T(8,128)(2,1)} %copy-done, bf16[2,16,16,1024]{3,2,1,0:T(8,128)(2,1)S(1)} %get-tuple-element.76.refs_0_, bf16[2,16,16,1024]{3,2,1,0:T(8,128)(2,1)S(1)} %collective-permute-done.24.refs_1_, ...), custom_call_target="tpu_custom_call" | custom-call | flops 1073741824 | bytes 5242880 | tf_op jit(solution)/shard_map/attention/pallas_call | solution.py:138
  154.6 2.1 collective-permute-start.12
  156.6 3.8 %collective-permute-start.20 = (bf16[4,16,1024]{2,1,0:T(8,128)(2,1)S(1)}, bf16[4,16,1024]{2,1,0:T(8,128)(2,1)S(1)}, u32[]{:S(2)}, u32[]{:S(2)}) collective-permute-start(bf16[4,16,1024]{2,1,0:T(8,128)(2,1)S(1)} %get-tuple-element.71), channel_id=1, source_target_pairs={{0,12},{4,0},{8,4},{12,8},{1,13},{5,1},{9,5},{13,9},{2,14},{6,2},{... | collective-permute-start | bytes 393224 | tf_op jit(solution)/shard_map/ppermute | solution.py:316
  160.5 7.5 %attention.5 = (bf16[16,16,1024]{2,1,0:T(8,128)(2,1)S(1)}, bf16[4,16,1024]{2,1,0:T(8,128)(2,1)}, bf16[4,16,1024]{2,1,0:T(8,128)(2,1)}) custom-call(bf16[16,16,5120]{2,1,0:T(8,128)(2,1)} %copy-done, bf16[2,16,16,1024]{3,2,1,0:T(8,128)(2,1)S(1)} %get-tuple-element.52.refs_0_, bf16[2,16,16,1024]{3,2,1,0:T(8,128)(2,1)S(1)} %collective-permute-done.refs_1_, ...), custom_call_target="tpu_custom_call" | custom-call | flops 1073741824 | bytes 5242880 | tf_op jit(solution)/shard_map/attention/pallas_call | solution.py:138
  168.1 3.9 %collective-permute-start.28 = (bf16[4,16,1024]{2,1,0:T(8,128)(2,1)}, bf16[4,16,1024]{2,1,0:T(8,128)(2,1)}, u32[]{:S(2)}, u32[]{:S(2)}) collective-permute-start(bf16[4,16,1024]{2,1,0:T(8,128)(2,1)} %get-tuple-element.79), channel_id=1, source_target_pairs={{0,12},{4,0},{8,4},{12,8},{1,13},{5,1},{9,5},{13,9},{2,14},{6,2},{... | collective-permute-start | bytes 393224 | tf_op jit(solution)/shard_map/ppermute | solution.py:316
  171.9 7.5 %attention.9 = (bf16[16,16,1024]{2,1,0:T(8,128)(2,1)S(1)}, bf16[4,16,1024]{2,1,0:T(8,128)(2,1)}, bf16[4,16,1024]{2,1,0:T(8,128)(2,1)}) custom-call(bf16[16,16,5120]{2,1,0:T(8,128)(2,1)} %copy-done, bf16[2,16,16,1024]{3,2,1,0:T(8,128)(2,1)S(1)} %get-tuple-element.84.refs_0_, bf16[2,16,16,1024]{3,2,1,0:T(8,128)(2,1)S(1)} %collective-permute-done.32.refs_1_, ...), custom_call_target="tpu_custom_call" | custom-call | flops 1073741824 | bytes 5242880 | tf_op jit(solution)/shard_map/attention/pallas_call | solution.py:138
  179.5 3.8 %collective-permute-start.4 = (bf16[4,16,1024]{2,1,0:T(8,128)(2,1)}, bf16[4,16,1024]{2,1,0:T(8,128)(2,1)S(1)}, u32[]{:S(2)}, u32[]{:S(2)}) collective-permute-start(bf16[4,16,1024]{2,1,0:T(8,128)(2,1)} %get-tuple-element.55), channel_id=1, source_target_pairs={{0,12},{4,0},{8,4},{12,8},{1,13},{5,1},{9,5},{13,9},{2,14},{6,2},{... | collective-permute-start | bytes 393224 | tf_op jit(solution)/shard_map/ppermute | solution.py:316
  183.9 3.8 %collective-permute-start.36 = (bf16[4,16,1024]{2,1,0:T(8,128)(2,1)}, bf16[4,16,1024]{2,1,0:T(8,128)(2,1)}, u32[]{:S(2)}, u32[]{:S(2)}) collective-permute-start(bf16[4,16,1024]{2,1,0:T(8,128)(2,1)} %get-tuple-element.87), channel_id=1, source_target_pairs={{0,12},{4,0},{8,4},{12,8},{1,13},{5,1},{9,5},{13,9},{2,14},{6,2},{... | collective-permute-start | bytes 393224 | tf_op jit(solution)/shard_map/ppermute | solution.py:316
  187.8 1.4 blend.6
  190.1 1.4 blend.7
  191.5 2.1 blend.8
  193.8 4.3 %collective-permute-start.22 = (bf16[3,16,1024]{2,1,0:T(8,128)(2,1)S(1)}, bf16[3,16,1024]{2,1,0:T(8,128)(2,1)S(1)}, u32[]{:S(2)}, u32[]{:S(2)}) collective-permute-start(bf16[3,16,1024]{2,1,0:T(8,128)(2,1)S(1)} %get-tuple-element.74), channel_id=1, source_target_pairs={{0,8},{4,12},{8,0},{12,4},{1,9},{5,13},{9,1},{13,5},{2,10},{6,14},... | collective-permute-start | bytes 294920 | tf_op jit(solution)/shard_map/ppermute | solution.py:316
  198.3 2.1 blend.9
  200.4 3.7 %collective-permute-start.23 = (bf16[11,16,1024]{2,1,0:T(8,128)(2,1)S(1)}, bf16[11,16,1024]{2,1,0:T(8,128)(2,1)S(1)}, u32[]{:S(2)}, u32[]{:S(2)}) collective-permute-start(bf16[11,16,1024]{2,1,0:T(8,128)(2,1)S(1)} %get-tuple-element.75), channel_id=1, source_target_pairs={{0,12},{4,0},{8,4},{12,8},{1,13},{5,1},{9,5},{13,9},{2,14},{6,2},{... | collective-permute-start | bytes 1081352 | tf_op jit(solution)/shard_map/ppermute | solution.py:316
  204.8 3.1 %collective-permute-done.22.refs_1_ = bf16[3,16,1024]{2,1,0:T(8,128)(2,1)S(1)} collective-permute-done((bf16[3,16,1024]{2,1,0:T(8,128)(2,1)S(1)}, bf16[3,16,1024]{2,1,0:T(8,128)(2,1)S(1)}, u32[]{:S(2)}, u32[]{:S(2)}) %collective-permute-start.22) | collective-permute-done | bytes 98336 | tf_op jit(solution)/shard_map/ppermute | solution.py:316
  207.8 5.2 %collective-permute-start.31 = (bf16[11,16,1024]{2,1,0:T(8,128)(2,1)S(1)}, bf16[11,16,1024]{2,1,0:T(8,128)(2,1)S(1)}, u32[]{:S(2)}, u32[]{:S(2)}) collective-permute-start(bf16[11,16,1024]{2,1,0:T(8,128)(2,1)S(1)} %get-tuple-element.83), channel_id=1, source_target_pairs={{0,12},{4,0},{8,4},{12,8},{1,13},{5,1},{9,5},{13,9},{2,14},{6,2},{... | collective-permute-start | bytes 1081352 | tf_op jit(solution)/shard_map/ppermute | solution.py:316
  213.1 19.8 %collective-permute-start.38 = (bf16[3,16,1024]{2,1,0:T(8,128)(2,1)S(1)}, bf16[3,16,1024]{2,1,0:T(8,128)(2,1)S(1)}, u32[]{:S(2)}, u32[]{:S(2)}) collective-permute-start(bf16[3,16,1024]{2,1,0:T(8,128)(2,1)S(1)} %get-tuple-element.90), channel_id=1, source_target_pairs={{0,8},{4,12},{8,0},{12,4},{1,9},{5,13},{9,1},{13,5},{2,10},{6,14},... | collective-permute-start | bytes 294920 | tf_op jit(solution)/shard_map/ppermute | solution.py:316
  232.9 2.8 %collective-permute-start.15 = (bf16[11,16,1024]{2,1,0:T(8,128)(2,1)S(1)}, bf16[11,16,1024]{2,1,0:T(8,128)(2,1)S(1)}, u32[]{:S(2)}, u32[]{:S(2)}) collective-permute-start(bf16[11,16,1024]{2,1,0:T(8,128)(2,1)S(1)} %get-tuple-element.67), channel_id=1, source_target_pairs={{0,12},{4,0},{8,4},{12,8},{1,13},{5,1},{9,5},{13,9},{2,14},{6,2},{... | collective-permute-start | bytes 1081352 | tf_op jit(solution)/shard_map/ppermute | solution.py:316
  235.6 1.4 blend.5
  237.0 8.5 %collective-permute-done.38.refs_1_ = bf16[3,16,1024]{2,1,0:T(8,128)(2,1)S(1)} collective-permute-done((bf16[3,16,1024]{2,1,0:T(8,128)(2,1)S(1)}, bf16[3,16,1024]{2,1,0:T(8,128)(2,1)S(1)}, u32[]{:S(2)}, u32[]{:S(2)}) %collective-permute-start.38) | collective-permute-done | bytes 98336 | tf_op jit(solution)/shard_map/ppermute | solution.py:316
  245.5 2.1 collective-permute-start.7
  248.1 2.4 collective-permute-start.6
  250.6 2.3 place.5
  252.9 2.4 place.6
  255.3 2.4 place.7
  257.6 8.3 %collective-permute-done.14.refs_1_ = bf16[3,16,1024]{2,1,0:T(8,128)(2,1)S(1)} collective-permute-done((bf16[3,16,1024]{2,1,0:T(8,128)(2,1)S(1)}, bf16[3,16,1024]{2,1,0:T(8,128)(2,1)S(1)}, u32[]{:S(2)}, u32[]{:S(2)}) %collective-permute-start.14) | collective-permute-done | bytes 98336 | tf_op jit(solution)/shard_map/ppermute | solution.py:316
  265.9 2.4 place.8
  268.3 2.4 place.9
  (95 shorter events, 9.4 us)
Async XLA Ops:
  1.4 123.0 %copy-start.1 = (bf16[1,16,16,5120]{3,2,1,0:T(8,128)(2,1)S(1)}, bf16[1,16,16,5120]{3,2,1,0:T(8,128)(2,1)}, u32[]{:S(2)}) copy-start(bf16[1,16,16,5120]{3,2,1,0:T(8,128)(2,1)} %param.8) | copy-start | bytes 7864324
  1.4 123.0 %copy-start.22 = (f32[5120]{0:T(1024)S(1)}, f32[5120]{0:T(1024)}, u32[]{:S(2)}) copy-start(f32[5120]{0:T(1024)} %param.11) | copy-start | bytes 61444
  5.8 27.0 %collective-permute-start = (bf16[2,16,16,1024]{3,2,1,0:T(8,128)(2,1)S(1)}, bf16[2,16,16,1024]{3,2,1,0:T(8,128)(2,1)S(1)}, u32[]{:S(2)}, u32[]{:S(2)}) collective-permute-start(bf16[2,16,16,1024]{3,2,1,0:T(8,128)(2,1)S(1)} %get-tuple-element.52.refs_0_), channel_id=1, source_target_pairs={{0,2},{1,3},{2,0},{3,1},{4,6},{5,7},{6,4},{7,5},{8,10},{9,11},{10,... | collective-permute-start | bytes 3145736 | tf_op jit(solution)/shard_map/ppermute | solution.py:311
  8.8 26.0 %collective-permute-start.9 = (bf16[2,16,16,1024]{3,2,1,0:T(8,128)(2,1)S(1)}, bf16[2,16,16,1024]{3,2,1,0:T(8,128)(2,1)S(1)}, u32[]{:S(2)}, u32[]{:S(2)}) collective-permute-start(bf16[2,16,16,1024]{3,2,1,0:T(8,128)(2,1)S(1)} %get-tuple-element.60.refs_0_), channel_id=1, source_target_pairs={{0,1},{1,0},{2,3},{3,2},{4,5},{5,4},{6,7},{7,6},{8,9},{9,8},{10,11... | collective-permute-start | bytes 3145736 | tf_op jit(solution)/shard_map/ppermute | solution.py:311
  8.8 46.5 %collective-permute-start.8 = (bf16[2,16,16,1024]{3,2,1,0:T(8,128)(2,1)S(1)}, bf16[2,16,16,1024]{3,2,1,0:T(8,128)(2,1)S(1)}, u32[]{:S(2)}, u32[]{:S(2)}) collective-permute-start(bf16[2,16,16,1024]{3,2,1,0:T(8,128)(2,1)S(1)} %get-tuple-element.60.refs_0_), channel_id=1, source_target_pairs={{0,2},{1,3},{2,0},{3,1},{4,6},{5,7},{6,4},{7,5},{8,10},{9,11},{10,... | collective-permute-start | bytes 3145736 | tf_op jit(solution)/shard_map/ppermute | solution.py:311
  8.9 48.4 %collective-permute-start.17 = (bf16[2,16,16,1024]{3,2,1,0:T(8,128)(2,1)S(1)}, bf16[2,16,16,1024]{3,2,1,0:T(8,128)(2,1)S(1)}, u32[]{:S(2)}, u32[]{:S(2)}) collective-permute-start(bf16[2,16,16,1024]{3,2,1,0:T(8,128)(2,1)S(1)} %get-tuple-element.68.refs_0_), channel_id=1, source_target_pairs={{0,1},{1,0},{2,3},{3,2},{4,5},{5,4},{6,7},{7,6},{8,9},{9,8},{10,11... | collective-permute-start | bytes 3145736 | tf_op jit(solution)/shard_map/ppermute | solution.py:311
  9.3 68.4 %collective-permute-start.16 = (bf16[2,16,16,1024]{3,2,1,0:T(8,128)(2,1)S(1)}, bf16[2,16,16,1024]{3,2,1,0:T(8,128)(2,1)S(1)}, u32[]{:S(2)}, u32[]{:S(2)}) collective-permute-start(bf16[2,16,16,1024]{3,2,1,0:T(8,128)(2,1)S(1)} %get-tuple-element.68.refs_0_), channel_id=1, source_target_pairs={{0,2},{1,3},{2,0},{3,1},{4,6},{5,7},{6,4},{7,5},{8,10},{9,11},{10,... | collective-permute-start | bytes 3145736 | tf_op jit(solution)/shard_map/ppermute | solution.py:311
  32.8 67.4 %collective-permute-start.24 = (bf16[2,16,16,1024]{3,2,1,0:T(8,128)(2,1)S(1)}, bf16[2,16,16,1024]{3,2,1,0:T(8,128)(2,1)S(1)}, u32[]{:S(2)}, u32[]{:S(2)}) collective-permute-start(bf16[2,16,16,1024]{3,2,1,0:T(8,128)(2,1)S(1)} %get-tuple-element.76.refs_0_), channel_id=1, source_target_pairs={{0,2},{1,3},{2,0},{3,1},{4,6},{5,7},{6,4},{7,5},{8,10},{9,11},{10,... | collective-permute-start | bytes 3145736 | tf_op jit(solution)/shard_map/ppermute | solution.py:311
  35.8 64.4 %collective-permute-start.25 = (bf16[2,16,16,1024]{3,2,1,0:T(8,128)(2,1)S(1)}, bf16[2,16,16,1024]{3,2,1,0:T(8,128)(2,1)S(1)}, u32[]{:S(2)}, u32[]{:S(2)}) collective-permute-start(bf16[2,16,16,1024]{3,2,1,0:T(8,128)(2,1)S(1)} %get-tuple-element.76.refs_0_), channel_id=1, source_target_pairs={{0,1},{1,0},{2,3},{3,2},{4,5},{5,4},{6,7},{7,6},{8,9},{9,8},{10,11... | collective-permute-start | bytes 3145736 | tf_op jit(solution)/shard_map/ppermute | solution.py:311
  55.2 66.6 %collective-permute-start.32 = (bf16[2,16,16,1024]{3,2,1,0:T(8,128)(2,1)S(1)}, bf16[2,16,16,1024]{3,2,1,0:T(8,128)(2,1)S(1)}, u32[]{:S(2)}, u32[]{:S(2)}) collective-permute-start(bf16[2,16,16,1024]{3,2,1,0:T(8,128)(2,1)S(1)} %get-tuple-element.84.refs_0_), channel_id=1, source_target_pairs={{0,2},{1,3},{2,0},{3,1},{4,6},{5,7},{6,4},{7,5},{8,10},{9,11},{10,... | collective-permute-start | bytes 3145736 | tf_op jit(solution)/shard_map/ppermute | solution.py:311
  58.3 63.5 %collective-permute-start.10 = (bf16[2,16,16,1024]{3,2,1,0:T(8,128)(2,1)S(1)}, bf16[2,16,16,1024]{3,2,1,0:T(8,128)(2,1)S(1)}, u32[]{:S(2)}, u32[]{:S(2)}) collective-permute-start(bf16[2,16,16,1024]{3,2,1,0:T(8,128)(2,1)S(1)} %collective-permute-done.8.refs_1_), channel_id=1, source_target_pairs={{0,1},{1,0},{2,3},{3,2},{4,5},{5,4},{6,7},{7,6},{8,9},{9,8},{10,11... | collective-permute-start | bytes 3145736 | tf_op jit(solution)/shard_map/ppermute | solution.py:311
  77.7 45.6 %collective-permute-start.18 = (bf16[2,16,16,1024]{3,2,1,0:T(8,128)(2,1)S(1)}, bf16[2,16,16,1024]{3,2,1,0:T(8,128)(2,1)S(1)}, u32[]{:S(2)}, u32[]{:S(2)}) collective-permute-start(bf16[2,16,16,1024]{3,2,1,0:T(8,128)(2,1)S(1)} %collective-permute-done.16.refs_1_), channel_id=1, source_target_pairs={{0,1},{1,0},{2,3},{3,2},{4,5},{5,4},{6,7},{7,6},{8,9},{9,8},{10,11... | collective-permute-start | bytes 3145736 | tf_op jit(solution)/shard_map/ppermute | solution.py:311
  100.2 45.0 %collective-permute-start.26 = (bf16[2,16,16,1024]{3,2,1,0:T(8,128)(2,1)S(1)}, bf16[2,16,16,1024]{3,2,1,0:T(8,128)(2,1)}, u32[]{:S(2)}, u32[]{:S(2)}) collective-permute-start(bf16[2,16,16,1024]{3,2,1,0:T(8,128)(2,1)S(1)} %collective-permute-done.24.refs_1_), channel_id=1, source_target_pairs={{0,1},{1,0},{2,3},{3,2},{4,5},{5,4},{6,7},{7,6},{8,9},{9,8},{10,11... | collective-permute-start | bytes 3145736 | tf_op jit(solution)/shard_map/ppermute | solution.py:311
  101.2 53.4 %collective-permute-start.1 = (bf16[2,16,16,1024]{3,2,1,0:T(8,128)(2,1)S(1)}, bf16[2,16,16,1024]{3,2,1,0:T(8,128)(2,1)}, u32[]{:S(2)}, u32[]{:S(2)}) collective-permute-start(bf16[2,16,16,1024]{3,2,1,0:T(8,128)(2,1)S(1)} %get-tuple-element.52.refs_0_), channel_id=1, source_target_pairs={{0,1},{1,0},{2,3},{3,2},{4,5},{5,4},{6,7},{7,6},{8,9},{9,8},{10,11... | collective-permute-start | bytes 3145736 | tf_op jit(solution)/shard_map/ppermute | solution.py:311
  121.8 34.8 %collective-permute-start.33 = (bf16[2,16,16,1024]{3,2,1,0:T(8,128)(2,1)S(1)}, bf16[2,16,16,1024]{3,2,1,0:T(8,128)(2,1)S(1)}, u32[]{:S(2)}, u32[]{:S(2)}) collective-permute-start(bf16[2,16,16,1024]{3,2,1,0:T(8,128)(2,1)S(1)} %get-tuple-element.84.refs_0_), channel_id=1, source_target_pairs={{0,1},{1,0},{2,3},{3,2},{4,5},{5,4},{6,7},{7,6},{8,9},{9,8},{10,11... | collective-permute-start | bytes 3145736 | tf_op jit(solution)/shard_map/ppermute | solution.py:311
  122.8 33.9 %collective-permute-start.2 = (bf16[2,16,16,1024]{3,2,1,0:T(8,128)(2,1)S(1)}, bf16[2,16,16,1024]{3,2,1,0:T(8,128)(2,1)}, u32[]{:S(2)}, u32[]{:S(2)}) collective-permute-start(bf16[2,16,16,1024]{3,2,1,0:T(8,128)(2,1)S(1)} %collective-permute-done.refs_1_), channel_id=1, source_target_pairs={{0,1},{1,0},{2,3},{3,2},{4,5},{5,4},{6,7},{7,6},{8,9},{9,8},{10,11... | collective-permute-start | bytes 3145736 | tf_op jit(solution)/shard_map/ppermute | solution.py:311
  124.4 36.1 %collective-permute-start.34 = (bf16[2,16,16,1024]{3,2,1,0:T(8,128)(2,1)S(1)}, bf16[2,16,16,1024]{3,2,1,0:T(8,128)(2,1)}, u32[]{:S(2)}, u32[]{:S(2)}) collective-permute-start(bf16[2,16,16,1024]{3,2,1,0:T(8,128)(2,1)S(1)} %collective-permute-done.32.refs_1_), channel_id=1, source_target_pairs={{0,1},{1,0},{2,3},{3,2},{4,5},{5,4},{6,7},{7,6},{8,9},{9,8},{10,11... | collective-permute-start | bytes 3145736 | tf_op jit(solution)/shard_map/ppermute | solution.py:311
  138.1 7.1 %copy-start.14 = (bf16[16,16,1024]{2,1,0:T(8,128)(2,1)}, bf16[16,16,1024]{2,1,0:T(8,128)(2,1)S(1)}, u32[]{:S(2)}) copy-start(bf16[16,16,1024]{2,1,0:T(8,128)(2,1)S(1)} %get-tuple-element.61.out_ref) | copy-start | bytes 1572868
  138.1 8.9 %copy-start.7 = (bf16[2,16,16,1024]{3,2,1,0:T(8,128)(2,1)S(1)}, bf16[2,16,16,1024]{3,2,1,0:T(8,128)(2,1)}, u32[]{:S(2)}) copy-start(bf16[2,16,16,1024]{3,2,1,0:T(8,128)(2,1)} %copy-done.6) | copy-start | bytes 3145732
  145.2 22.8 %collective-permute-start.11 = (bf16[4,16,1024]{2,1,0:T(8,128)(2,1)S(1)}, bf16[4,16,1024]{2,1,0:T(8,128)(2,1)S(1)}, u32[]{:S(2)}, u32[]{:S(2)}) collective-permute-start(bf16[4,16,1024]{2,1,0:T(8,128)(2,1)S(1)} %get-tuple-element.62), channel_id=1, source_target_pairs={{0,4},{4,8},{8,12},{12,0},{1,5},{5,9},{9,13},{13,1},{2,6},{6,10},{... | collective-permute-start | bytes 393224 | tf_op jit(solution)/shard_map/ppermute | solution.py:316
  154.6 24.9 %collective-permute-start.12 = (bf16[4,16,1024]{2,1,0:T(8,128)(2,1)S(1)}, bf16[4,16,1024]{2,1,0:T(8,128)(2,1)S(1)}, u32[]{:S(2)}, u32[]{:S(2)}) collective-permute-start(bf16[4,16,1024]{2,1,0:T(8,128)(2,1)S(1)} %get-tuple-element.63), channel_id=1, source_target_pairs={{0,12},{4,0},{8,4},{12,8},{1,13},{5,1},{9,5},{13,9},{2,14},{6,2},{... | collective-permute-start | bytes 393224 | tf_op jit(solution)/shard_map/ppermute | solution.py:316
  156.6 22.8 %collective-permute-start.19 = (bf16[4,16,1024]{2,1,0:T(8,128)(2,1)S(1)}, bf16[4,16,1024]{2,1,0:T(8,128)(2,1)S(1)}, u32[]{:S(2)}, u32[]{:S(2)}) collective-permute-start(bf16[4,16,1024]{2,1,0:T(8,128)(2,1)S(1)} %get-tuple-element.70), channel_id=1, source_target_pairs={{0,4},{4,8},{8,12},{12,0},{1,5},{5,9},{9,13},{13,1},{2,6},{6,10},{... | collective-permute-start | bytes 393224 | tf_op jit(solution)/shard_map/ppermute | solution.py:316
  156.6 26.6 %collective-permute-start.20 = (bf16[4,16,1024]{2,1,0:T(8,128)(2,1)S(1)}, bf16[4,16,1024]{2,1,0:T(8,128)(2,1)S(1)}, u32[]{:S(2)}, u32[]{:S(2)}) collective-permute-start(bf16[4,16,1024]{2,1,0:T(8,128)(2,1)S(1)} %get-tuple-element.71), channel_id=1, source_target_pairs={{0,12},{4,0},{8,4},{12,8},{1,13},{5,1},{9,5},{13,9},{2,14},{6,2},{... | collective-permute-start | bytes 393224 | tf_op jit(solution)/shard_map/ppermute | solution.py:316
  160.5 23.5 %collective-permute-start.27 = (bf16[4,16,1024]{2,1,0:T(8,128)(2,1)S(1)}, bf16[4,16,1024]{2,1,0:T(8,128)(2,1)S(1)}, u32[]{:S(2)}, u32[]{:S(2)}) collective-permute-start(bf16[4,16,1024]{2,1,0:T(8,128)(2,1)S(1)} %get-tuple-element.78), channel_id=1, source_target_pairs={{0,4},{4,8},{8,12},{12,0},{1,5},{5,9},{9,13},{13,1},{2,6},{6,10},{... | collective-permute-start | bytes 393224 | tf_op jit(solution)/shard_map/ppermute | solution.py:316
  168.0 19.7 %copy-start.15 = (bf16[16,16,1024]{2,1,0:T(8,128)(2,1)S(1)}, bf16[16,16,1024]{2,1,0:T(8,128)(2,1)}, u32[]{:S(2)}) copy-start(bf16[16,16,1024]{2,1,0:T(8,128)(2,1)} %copy-done.14) | copy-start | bytes 1572868
  168.0 19.7 %copy-start.16 = (s32[4,16]{1,0:T(4,128)S(1)}, s32[4,16]{1,0:T(4,128)}, u32[]{:S(2)}) copy-start(s32[4,16]{1,0:T(4,128)} %weight_ref.19) | copy-start | bytes 772
  168.0 19.7 %copy-start.19 = (s32[4]{0:T(128)S(1)}, s32[4]{0:T(128)}, u32[]{:S(2)}) copy-start(s32[4]{0:T(128)} %start_ref.19) | copy-start | bytes 52
  168.1 19.7 %copy-start.20 = (s32[4]{0:T(128)S(1)}, s32[4]{0:T(128)}, u32[]{:S(2)}) copy-start(s32[4]{0:T(128)} %owner_ref.19) | copy-start | bytes 52
  168.1 23.4 %collective-permute-start.28 = (bf16[4,16,1024]{2,1,0:T(8,128)(2,1)}, bf16[4,16,1024]{2,1,0:T(8,128)(2,1)}, u32[]{:S(2)}, u32[]{:S(2)}) collective-permute-start(bf16[4,16,1024]{2,1,0:T(8,128)(2,1)} %get-tuple-element.79), channel_id=1, source_target_pairs={{0,12},{4,0},{8,4},{12,8},{1,13},{5,1},{9,5},{13,9},{2,14},{6,2},{... | collective-permute-start | bytes 393224 | tf_op jit(solution)/shard_map/ppermute | solution.py:316
  179.4 14.2 %collective-permute-start.3 = (bf16[4,16,1024]{2,1,0:T(8,128)(2,1)}, bf16[4,16,1024]{2,1,0:T(8,128)(2,1)S(1)}, u32[]{:S(2)}, u32[]{:S(2)}) collective-permute-start(bf16[4,16,1024]{2,1,0:T(8,128)(2,1)} %get-tuple-element.54), channel_id=1, source_target_pairs={{0,4},{4,8},{8,12},{12,0},{1,5},{5,9},{9,13},{13,1},{2,6},{6,10},{... | collective-permute-start | bytes 393224 | tf_op jit(solution)/shard_map/ppermute | solution.py:316
  179.5 14.3 %collective-permute-start.4 = (bf16[4,16,1024]{2,1,0:T(8,128)(2,1)}, bf16[4,16,1024]{2,1,0:T(8,128)(2,1)S(1)}, u32[]{:S(2)}, u32[]{:S(2)}) collective-permute-start(bf16[4,16,1024]{2,1,0:T(8,128)(2,1)} %get-tuple-element.55), channel_id=1, source_target_pairs={{0,12},{4,0},{8,4},{12,8},{1,13},{5,1},{9,5},{13,9},{2,14},{6,2},{... | collective-permute-start | bytes 393224 | tf_op jit(solution)/shard_map/ppermute | solution.py:316
  183.9 14.2 %collective-permute-start.35 = (bf16[4,16,1024]{2,1,0:T(8,128)(2,1)}, bf16[4,16,1024]{2,1,0:T(8,128)(2,1)}, u32[]{:S(2)}, u32[]{:S(2)}) collective-permute-start(bf16[4,16,1024]{2,1,0:T(8,128)(2,1)} %get-tuple-element.86), channel_id=1, source_target_pairs={{0,4},{4,8},{8,12},{12,0},{1,5},{5,9},{9,13},{13,1},{2,6},{6,10},{... | collective-permute-start | bytes 393224 | tf_op jit(solution)/shard_map/ppermute | solution.py:316
  183.9 14.2 %collective-permute-start.36 = (bf16[4,16,1024]{2,1,0:T(8,128)(2,1)}, bf16[4,16,1024]{2,1,0:T(8,128)(2,1)}, u32[]{:S(2)}, u32[]{:S(2)}) collective-permute-start(bf16[4,16,1024]{2,1,0:T(8,128)(2,1)} %get-tuple-element.87), channel_id=1, source_target_pairs={{0,12},{4,0},{8,4},{12,8},{1,13},{5,1},{9,5},{13,9},{2,14},{6,2},{... | collective-permute-start | bytes 393224 | tf_op jit(solution)/shard_map/ppermute | solution.py:316
  191.5 8.9 %collective-permute-start.13 = (bf16[3,16,1024]{2,1,0:T(8,128)(2,1)S(1)}, bf16[3,16,1024]{2,1,0:T(8,128)(2,1)S(1)}, u32[]{:S(2)}, u32[]{:S(2)}) collective-permute-start(bf16[3,16,1024]{2,1,0:T(8,128)(2,1)S(1)} %get-tuple-element.65), channel_id=1, source_target_pairs={{0,4},{4,8},{8,12},{12,0},{1,5},{5,9},{9,13},{13,1},{2,6},{6,10},{... | collective-permute-start | bytes 294920 | tf_op jit(solution)/shard_map/ppermute | solution.py:316
  193.7 10.5 %collective-permute-start.21 = (bf16[3,16,1024]{2,1,0:T(8,128)(2,1)S(1)}, bf16[3,16,1024]{2,1,0:T(8,128)(2,1)S(1)}, u32[]{:S(2)}, u32[]{:S(2)}) collective-permute-start(bf16[3,16,1024]{2,1,0:T(8,128)(2,1)S(1)} %get-tuple-element.73), channel_id=1, source_target_pairs={{0,4},{4,8},{8,12},{12,0},{1,5},{5,9},{9,13},{13,1},{2,6},{6,10},{... | collective-permute-start | bytes 294920 | tf_op jit(solution)/shard_map/ppermute | solution.py:316
  193.8 14.1 %collective-permute-start.22 = (bf16[3,16,1024]{2,1,0:T(8,128)(2,1)S(1)}, bf16[3,16,1024]{2,1,0:T(8,128)(2,1)S(1)}, u32[]{:S(2)}, u32[]{:S(2)}) collective-permute-start(bf16[3,16,1024]{2,1,0:T(8,128)(2,1)S(1)} %get-tuple-element.74), channel_id=1, source_target_pairs={{0,8},{4,12},{8,0},{12,4},{1,9},{5,13},{9,1},{13,5},{2,10},{6,14},... | collective-permute-start | bytes 294920 | tf_op jit(solution)/shard_map/ppermute | solution.py:316
  198.1 14.9 %collective-permute-start.29 = (bf16[3,16,1024]{2,1,0:T(8,128)(2,1)S(1)}, bf16[3,16,1024]{2,1,0:T(8,128)(2,1)S(1)}, u32[]{:S(2)}, u32[]{:S(2)}) collective-permute-start(bf16[3,16,1024]{2,1,0:T(8,128)(2,1)S(1)} %get-tuple-element.81), channel_id=1, source_target_pairs={{0,4},{4,8},{8,12},{12,0},{1,5},{5,9},{9,13},{13,1},{2,6},{6,10},{... | collective-permute-start | bytes 294920 | tf_op jit(solution)/shard_map/ppermute | solution.py:316
  198.2 14.9 %collective-permute-start.30 = (bf16[3,16,1024]{2,1,0:T(8,128)(2,1)S(1)}, bf16[3,16,1024]{2,1,0:T(8,128)(2,1)S(1)}, u32[]{:S(2)}, u32[]{:S(2)}) collective-permute-start(bf16[3,16,1024]{2,1,0:T(8,128)(2,1)S(1)} %get-tuple-element.82), channel_id=1, source_target_pairs={{0,8},{4,12},{8,0},{12,4},{1,9},{5,13},{9,1},{13,5},{2,10},{6,14},... | collective-permute-start | bytes 294920 | tf_op jit(solution)/shard_map/ppermute | solution.py:316
  200.4 47.2 %collective-permute-start.23 = (bf16[11,16,1024]{2,1,0:T(8,128)(2,1)S(1)}, bf16[11,16,1024]{2,1,0:T(8,128)(2,1)S(1)}, u32[]{:S(2)}, u32[]{:S(2)}) collective-permute-start(bf16[11,16,1024]{2,1,0:T(8,128)(2,1)S(1)} %get-tuple-element.75), channel_id=1, source_target_pairs={{0,12},{4,0},{8,4},{12,8},{1,13},{5,1},{9,5},{13,9},{2,14},{6,2},{... | collective-permute-start | bytes 1081352 | tf_op jit(solution)/shard_map/ppermute | solution.py:316
  204.1 28.7 %collective-permute-start.37 = (bf16[3,16,1024]{2,1,0:T(8,128)(2,1)S(1)}, bf16[3,16,1024]{2,1,0:T(8,128)(2,1)S(1)}, u32[]{:S(2)}, u32[]{:S(2)}) collective-permute-start(bf16[3,16,1024]{2,1,0:T(8,128)(2,1)S(1)} %get-tuple-element.89), channel_id=1, source_target_pairs={{0,4},{4,8},{8,12},{12,0},{1,5},{5,9},{9,13},{13,1},{2,6},{6,10},{... | collective-permute-start | bytes 294920 | tf_op jit(solution)/shard_map/ppermute | solution.py:316
  207.8 39.7 %collective-permute-start.31 = (bf16[11,16,1024]{2,1,0:T(8,128)(2,1)S(1)}, bf16[11,16,1024]{2,1,0:T(8,128)(2,1)S(1)}, u32[]{:S(2)}, u32[]{:S(2)}) collective-permute-start(bf16[11,16,1024]{2,1,0:T(8,128)(2,1)S(1)} %get-tuple-element.83), channel_id=1, source_target_pairs={{0,12},{4,0},{8,4},{12,8},{1,13},{5,1},{9,5},{13,9},{2,14},{6,2},{... | collective-permute-start | bytes 1081352 | tf_op jit(solution)/shard_map/ppermute | solution.py:316
  213.0 35.1 %collective-permute-start.39 = (bf16[11,16,1024]{2,1,0:T(8,128)(2,1)S(1)}, bf16[11,16,1024]{2,1,0:T(8,128)(2,1)S(1)}, u32[]{:S(2)}, u32[]{:S(2)}) collective-permute-start(bf16[11,16,1024]{2,1,0:T(8,128)(2,1)S(1)} %get-tuple-element.91), channel_id=1, source_target_pairs={{0,12},{4,0},{8,4},{12,8},{1,13},{5,1},{9,5},{13,9},{2,14},{6,2},{... | collective-permute-start | bytes 1081352 | tf_op jit(solution)/shard_map/ppermute | solution.py:316
  213.1 32.4 %collective-permute-start.38 = (bf16[3,16,1024]{2,1,0:T(8,128)(2,1)S(1)}, bf16[3,16,1024]{2,1,0:T(8,128)(2,1)S(1)}, u32[]{:S(2)}, u32[]{:S(2)}) collective-permute-start(bf16[3,16,1024]{2,1,0:T(8,128)(2,1)S(1)} %get-tuple-element.90), channel_id=1, source_target_pairs={{0,8},{4,12},{8,0},{12,4},{1,9},{5,13},{9,1},{13,5},{2,10},{6,14},... | collective-permute-start | bytes 294920 | tf_op jit(solution)/shard_map/ppermute | solution.py:316
  232.9 33.1 %collective-permute-start.15 = (bf16[11,16,1024]{2,1,0:T(8,128)(2,1)S(1)}, bf16[11,16,1024]{2,1,0:T(8,128)(2,1)S(1)}, u32[]{:S(2)}, u32[]{:S(2)}) collective-permute-start(bf16[11,16,1024]{2,1,0:T(8,128)(2,1)S(1)} %get-tuple-element.67), channel_id=1, source_target_pairs={{0,12},{4,0},{8,4},{12,8},{1,13},{5,1},{9,5},{13,9},{2,14},{6,2},{... | collective-permute-start | bytes 1081352 | tf_op jit(solution)/shard_map/ppermute | solution.py:316
  245.5 22.8 %collective-permute-start.7 = (bf16[11,16,1024]{2,1,0:T(8,128)(2,1)S(1)}, bf16[11,16,1024]{2,1,0:T(8,128)(2,1)S(1)}, u32[]{:S(2)}, u32[]{:S(2)}) collective-permute-start(bf16[11,16,1024]{2,1,0:T(8,128)(2,1)S(1)} %get-tuple-element.59), channel_id=1, source_target_pairs={{0,12},{4,0},{8,4},{12,8},{1,13},{5,1},{9,5},{13,9},{2,14},{6,2},{... | collective-permute-start | bytes 1081352 | tf_op jit(solution)/shard_map/ppermute | solution.py:316
  247.6 18.4 %collective-permute-start.14 = (bf16[3,16,1024]{2,1,0:T(8,128)(2,1)S(1)}, bf16[3,16,1024]{2,1,0:T(8,128)(2,1)S(1)}, u32[]{:S(2)}, u32[]{:S(2)}) collective-permute-start(bf16[3,16,1024]{2,1,0:T(8,128)(2,1)S(1)} %get-tuple-element.66), channel_id=1, source_target_pairs={{0,8},{4,12},{8,0},{12,4},{1,9},{5,13},{9,1},{13,5},{2,10},{6,14},... | collective-permute-start | bytes 294920 | tf_op jit(solution)/shard_map/ppermute | solution.py:316
  247.6 20.7 %collective-permute-start.5 = (bf16[3,16,1024]{2,1,0:T(8,128)(2,1)S(1)}, bf16[3,16,1024]{2,1,0:T(8,128)(2,1)S(1)}, u32[]{:S(2)}, u32[]{:S(2)}) collective-permute-start(bf16[3,16,1024]{2,1,0:T(8,128)(2,1)S(1)} %get-tuple-element.57), channel_id=1, source_target_pairs={{0,4},{4,8},{8,12},{12,0},{1,5},{5,9},{9,13},{13,1},{2,6},{6,10},{... | collective-permute-start | bytes 294920 | tf_op jit(solution)/shard_map/ppermute | solution.py:316
  248.1 20.1 %collective-permute-start.6 = (bf16[3,16,1024]{2,1,0:T(8,128)(2,1)S(1)}, bf16[3,16,1024]{2,1,0:T(8,128)(2,1)S(1)}, u32[]{:S(2)}, u32[]{:S(2)}) collective-permute-start(bf16[3,16,1024]{2,1,0:T(8,128)(2,1)S(1)} %get-tuple-element.58), channel_id=1, source_target_pairs={{0,8},{4,12},{8,0},{12,4},{1,9},{5,13},{9,1},{13,5},{2,10},{6,14},... | collective-permute-start | bytes 294920 | tf_op jit(solution)/shard_map/ppermute | solution.py:316
  (15 other events, 27.5 us)

commit v2 on v0

--- a/solution.py
+++ b/solution.py
@@ -1,13 +1,471 @@
+import functools
 import math
 
 import jax
 import jax.numpy as jnp
 from jax import lax
+from jax.experimental import pallas as pl
+from jax.experimental.pallas import tpu as pltpu
 from jax.sharding import PartitionSpec as P
 
 HEADS = 40
 WF = 16
 FR = 12
+MARGIN = WF - FR
+SHIFT = FR // 2
+HOME_BASE = 2 * MARGIN
+FROM_BEFORE = HOME_BASE - SHIFT
+FROM_AFTER = SHIFT + WF + MARGIN - HOME_BASE - FR
+NEAR = 2
+CHUNKS = (2, 4, 4, 4, 4, 2)
+STEP_HEADS = 2
+VMEM_LIMIT = 64 * 1024 * 1024
+
+
+def params():
+    return pltpu.CompilerParams(vmem_limit_bytes=VMEM_LIMIT)
+
+
+def like(*shape):
+    return jax.ShapeDtypeStruct(shape, jnp.bfloat16)
+
+
+FILLER = pl.CostEstimate(flops=10**10, bytes_accessed=0, transcendentals=0)
+NO_COST = pl.CostEstimate(flops=0, bytes_accessed=0, transcendentals=0)
+SMEM = pl.BlockSpec(memory_space=pltpu.SMEM)
+
+
+def normalized(rows, gain):
+    floats = rows.astype(jnp.float32)
+    mean_square = jnp.mean(floats * floats, axis=-1, keepdims=True)
+    return (floats * lax.rsqrt(mean_square + 1e-06) * gain).astype(jnp.bfloat16)
+
+
+def split_heads(near, rows, gain, counts, plain=(), frames_per_step=4):
+    frames, tokens, features = rows.shape
+    head_size = features // HEADS
+    kinds = (2,) * len(plain)
+
+    def kernel(near_ref, rows_ref, gain_ref, *refs):
+        scratch = refs[-1]
+        plain_refs, out_refs = refs[: len(plain)], refs[len(plain) : -1]
+        heads = HEADS // NEAR
+        scratch[...] = normalized(rows_ref[...], gain_ref[...])
+        here = near_ref[0]
+
+        def put(out_ref, slot, half, head):
+            column = pl.multiple_of((half * heads + head) * head_size, head_size)
+            columns = pl.ds(column, head_size)
+            if plain:
+                out_ref[slot, 0] = scratch[:, :, columns]
+                out_ref[slot, 1] = plain_refs[0][:, :, columns]
+            else:
+                out_ref[slot] = scratch[:, :, columns]
+
+        for head in range(heads):
+            put(out_refs[0], head, here, head)
+        head = 0
+        for out_ref in out_refs[1:]:
+            for slot in range(out_ref.shape[0]):
+                put(out_ref, slot, NEAR - 1 - here, head)
+                head += 1
+
+    block = pl.BlockSpec((frames_per_step, tokens, features), lambda i: (i, 0, 0))
+
+    def out_spec(count):
+        zeros = (0,) * (1 + len(kinds))
+        return pl.BlockSpec(
+            (count, *kinds, frames_per_step, tokens, head_size), lambda i: (*zeros, i, 0, 0)
+        )
+
+    return pl.pallas_call(
+        kernel,
+        grid=(frames // frames_per_step,),
+        in_specs=[SMEM, block, pl.BlockSpec((1, 1, features), lambda i: (0, 0, 0))]
+        + [block for _ in plain],
+        out_specs=[out_spec(count) for count in (sum(counts), *counts)],
+        out_shape=[
+            like(count, *kinds, frames, tokens, head_size) for count in (sum(counts), *counts)
+        ],
+        scratch_shapes=[pltpu.VMEM((frames_per_step, tokens, features), jnp.bfloat16)],
+        compiler_params=params(),
+        cost_estimate=FILLER,
+        name="norm_split",
+    )(near, rows, gain, *plain)
+
+
+def join_halves(own, base, other, counts):
+    _, kinds, frames, tokens, head_size = own.shape
+    bases = [sum(counts[:i]) for i in range(len(counts))]
+
+    def out_spec(first, count):
+        return pl.BlockSpec(
+            (STEP_HEADS, kinds, NEAR, frames, tokens, head_size),
+            lambda i: (jnp.clip(i - first // STEP_HEADS, 0, count // STEP_HEADS - 1),) + (0,) * 5,
+        )
+
+    def kernel(own_ref, other_ref, *out_refs):
+        step = pl.program_id(0) * STEP_HEADS
+        for out_ref, first, count in zip(out_refs, bases, counts):
+
+            @pl.when((step >= first) & (step < first + count))
+            def _():
+                out_ref[:, :, 0] = own_ref[...]
+                out_ref[:, :, 1] = other_ref[...]
+
+    block = (STEP_HEADS, kinds, frames, tokens, head_size)
+    return pl.pallas_call(
+        kernel,
+        grid=(sum(counts) // STEP_HEADS,),
+        in_specs=[
+            pl.BlockSpec(block, lambda i: (base // STEP_HEADS + i, 0, 0, 0, 0)),
+            pl.BlockSpec(block, lambda i: (i, 0, 0, 0, 0)),
+        ],
+        out_specs=[out_spec(first, count) for first, count in zip(bases, counts)],
+        out_shape=[
+            like(count, kinds, NEAR, frames, tokens, head_size) for count in counts
+        ],
+        compiler_params=params(),
+        cost_estimate=FILLER,
+        name="join_halves",
+    )(own, other)
+
+
+def attention_body(tables, in_refs, out_refs, left_ref, left_base):
+    (out_ref,) = out_refs
+    query_refs, sources = in_refs[:NEAR], in_refs[NEAR:]
+    _, frames, tokens, head_size = query_refs[0].shape
+    rows = frames * tokens
+    factor = math.log2(math.e) / math.sqrt(head_size)
+    contract = (((1,), (1,)), ((), ()))
+    step = pl.program_id(0)
+    for half in range(NEAR):
+        query = query_refs[half][0].reshape(rows, head_size)
+        scores = [
+            lax.dot_general(
+                query,
+                source[0, 0].reshape(NEAR * rows, head_size),
+                contract,
+                preferred_element_type=jnp.float32,
+            )
+            for source in sources
+        ]
+        row_max = functools.reduce(jnp.maximum, scores)
+        row_max = jnp.max(row_max, axis=-1, keepdims=True)
+        exponents = [jnp.exp2((score - row_max) * factor) for score in scores]
+        total = jnp.sum(functools.reduce(jnp.add, exponents), axis=-1, keepdims=True)
+        inverse = 1.0 / total
+        result = jnp.zeros((rows, head_size), jnp.float32)
+        for exponent, source in zip(exponents, sources):
+            weights = (exponent * inverse).astype(jnp.bfloat16)
+            result += jnp.dot(
+                weights,
+                source[0, 1].reshape(NEAR * rows, head_size),
+                preferred_element_type=jnp.float32,
+            )
+        result = result.astype(jnp.bfloat16).reshape(frames, tokens, head_size)
+        out_ref[0, half] = result
+        left_ref[left_base + step, half] = result[:HOME_BASE]
+
+
+def phase_of(owner_ref, wanted, windows):
+    phase = jnp.int32(0)
+    for index in range(windows):
+        phase = jnp.where(owner_ref[index] == wanted, index, phase)
+    return phase
+
+
+def first_owned(phase, windows):
+    return lax.rem(phase + (windows - 1) * HOME_BASE, windows)
+
+
+def extra_owned(windows):
+    return [i for i in range(FR // windows) if windows * (i + 1) > FROM_AFTER]
+
+
+def left_count(windows):
+    return FROM_AFTER + len(extra_owned(windows))
+
+
+def blend_body(windows, tables, in_refs, out_refs, left_ref, left_base):
+    place_ref, start_ref, owner_ref, weight_ref, _ = tables
+    out_ref, after_ref = in_refs
+    home_ref, *sent_refs = out_refs
+    here = place_ref[0]
+    after = lax.rem(here + 1, windows)
+    offset = start_ref[here] - here * FR
+    offset_after = start_ref[after] - after * FR
+    step = pl.program_id(0)
+    for frame in range(FR):
+        place = frame + HOME_BASE - offset
+        if frame + HOME_BASE < WF:
+            weight = weight_ref[here, place].astype(jnp.float32)
+        else:
+            valid = place < WF
+            place = jnp.minimum(place, WF - 1)
+            weight = jnp.where(valid, weight_ref[here, place], 0).astype(jnp.float32)
+        numerator = out_ref[0, :, place].astype(jnp.float32) * weight
+        denominator = weight
+        if frame + HOME_BASE >= FR:
+            slot = frame + HOME_BASE - FR - offset_after
+            valid = slot >= 0
+            slot = jnp.maximum(slot, 0)
+            weight = jnp.where(valid, weight_ref[after, slot], 0).astype(jnp.float32)
+            numerator += after_ref[0, :, slot].astype(jnp.float32) * weight
+            denominator += weight
+        home_ref[0, :, frame] = (numerator / denominator).astype(jnp.bfloat16)
+    for distance in range(1, windows):
+        target = lax.rem(here + distance, windows)
+        first = first_owned(phase_of(owner_ref, target, windows), windows)
+        if distance == windows - 1:
+            left_ref[left_base + step, :, :FROM_AFTER] = home_ref[0, :, :FROM_AFTER]
+            for slot, index in enumerate(extra_owned(windows)):
+                left_ref[left_base + step, :, FROM_AFTER + slot] = home_ref[
+                    0, :, first + index * windows
+                ]
+            continue
+        sent_ref = sent_refs[distance - 1]
+        for index in range(FR // windows):
+            sent_ref[0, :, index] = home_ref[0, :, first + index * windows]
+        if distance == 1:
+            sent_ref[0, :, FR // windows :] = home_ref[0, :, FR - FROM_BEFORE :]
+
+
+def place_body(windows, tables, in_refs, out_refs):
+    place_ref, start_ref, owner_ref = tables[:3]
+    home_ref, *received = in_refs
+    owned_ref, next_ref, other_ref = out_refs
+    here = place_ref[0]
+    first = first_owned(phase_of(owner_ref, here, windows), windows)
+    slot_base = (first + HOME_BASE) // windows
+    count = FR // windows
+    extra = extra_owned(windows)
+    heads, _, _, _, head_size = home_ref.shape
+    offset = start_ref[here] - here * FR + SHIFT - HOME_BASE
+    from_before, from_after = received[0], received[-1]
+    for head in range(heads):
+        columns = slice(head * head_size, (head + 1) * head_size)
+        for distance in range(windows):
+            source = lax.rem(here + windows - distance, windows)
+            for index in range(count):
+                slot = lax.rem(source * count + slot_base + index, FR)
+                if distance == 0:
+                    row = home_ref[head, :, first + index * windows]
+                elif distance < windows - 1:
+                    row = received[distance - 1][head, :, index]
+                elif index in extra:
+                    row = received[distance - 1][head, :, FROM_AFTER + extra.index(index)]
+                else:
+                    row = received[distance - 1][head, :, first + index * windows]
+                owned_ref[slot, :, columns] = row[0]
+                other_ref[slot, :, columns] = row[1]
+        for frame in range(WF):
+            wanted = offset + frame
+            row = home_ref[head, :, jnp.clip(wanted, 0, FR - 1)]
+            if frame < FROM_BEFORE:
+                slot = jnp.clip(wanted + FROM_BEFORE, 0, FROM_BEFORE - 1)
+                row = jnp.where(wanted < 0, from_before[head, :, count + slot], row)
+            if frame + MARGIN + SHIFT - HOME_BASE >= FR:
+                slot = jnp.clip(wanted - FR, 0, FROM_AFTER - 1)
+                row = jnp.where(wanted >= FR, from_after[head, :, slot], row)
+            next_ref[frame, :, columns] = row[0]
+            other_ref[FR + frame, :, columns] = row[1]
+
+
+def block_spec(array, blocks, base=0):
+    shape = (1,) + array.shape[1:]
+    zeros = (0,) * (len(shape) - 1)
+    return pl.BlockSpec(shape, lambda i, *_: (base + jnp.minimum(i, blocks - 1),) + zeros)
+
+
+class Task:
+    def __init__(self, blocks, operands, in_specs, out_shape, out_specs, body):
+        self.blocks, self.body = blocks, body
+        self.operands, self.in_specs = operands, in_specs
+        self.out_shape, self.out_specs = out_shape, out_specs
+
+
+def attention_task(queries, sources, base):
+    blocks = sources[0].shape[0]
+    frames, tokens, head_size = queries[0].shape[1:]
+    shape = like(blocks, NEAR, frames, tokens, head_size)
+    return Task(
+        blocks,
+        [*queries, *sources],
+        [block_spec(query, blocks, base) for query in queries]
+        + [block_spec(source, blocks) for source in sources],
+        [shape],
+        [block_spec(shape, blocks)],
+        attention_body,
+    )
+
+
+def blend_task(out, after, after_base, windows):
+    blocks, halves, _, tokens, head_size = out.shape
+    owned = FR // windows
+    counts = [FR, owned + FROM_BEFORE] + [owned] * (windows - 3)
+    shapes = [like(blocks, halves, count, tokens, head_size) for count in counts]
+    return Task(
+        blocks,
+        [out, after],
+        [block_spec(out, blocks), block_spec(after, blocks, after_base)],
+        shapes,
+        [block_spec(shape, blocks) for shape in shapes],
+        functools.partial(blend_body, windows),
+    )
+
+
+def run_stage(tables, tasks, merged=True):
+    steps = max(task.blocks for task in tasks)
+    operands = [operand for task in tasks for operand in task.operands]
+    shapes = [shape for task in tasks for shape in task.out_shape]
+    windows = lax.axis_size("win")
+    assert left_count(windows) == HOME_BASE
+    _, halves, _, tokens, head_size = shapes[0].shape
+    blocks = [task.blocks for task in tasks]
+    lefts = [
+        like(count, halves, HOME_BASE, tokens, head_size)
+        for count in ([sum(blocks)] if merged else blocks)
+    ]
+
+    def kernel(*refs):
+        table_refs, refs = refs[: len(tables)], refs[len(tables) :]
+        in_refs, refs = refs[: len(operands)], refs[len(operands) :]
+        out_refs, left_refs = refs[: len(shapes)], refs[len(shapes) :]
+        step = pl.program_id(0)
+        for index, task in enumerate(tasks):
+            task_in, in_refs = in_refs[: len(task.operands)], in_refs[len(task.operands) :]
+            task_out, out_refs = out_refs[: len(task.out_shape)], out_refs[len(task.out_shape) :]
+            body = functools.partial(
+                task.body,
+                table_refs,
+                task_in,
+                task_out,
+                left_refs[0 if merged else index],
+                sum(blocks[:index]) if merged else 0,
+            )
+            if task.blocks == steps:
+                body()
+            else:
+                pl.when(step < task.blocks)(body)
+
+    outputs = pl.pallas_call(
+        kernel,
+        grid=(steps,),
+        in_specs=[SMEM for _ in tables] + [spec for task in tasks for spec in task.in_specs],
+        out_specs=[spec for task in tasks for spec in task.out_specs]
+        + [pl.BlockSpec(left.shape, lambda i: (0,) * 5) for left in lefts],
+        out_shape=shapes + lefts,
+        compiler_params=params(),
+        cost_estimate=NO_COST,
+        name="stage",
+    )(*tables, *operands)
+    results = []
+    for task in tasks:
+        results.append(outputs[: len(task.out_shape)])
+        outputs = outputs[len(task.out_shape) :]
+    return results, outputs
+
+
+def result_columns(half, base, width):
+    head_size = width[1]
+    column = (half * (HEADS // NEAR) + base) * head_size
+    return pl.ds(pl.multiple_of(column, head_size), width[0] * head_size)
+
+
+def place(tables, home, received, base, features, windows, targets):
+    heads, halves, _, tokens, head_size = home.shape
+    operands = [home, *received]
+
+    def first_heads(operand):
+        return pl.BlockSpec((heads,) + operand.shape[1:], lambda i: (0,) * len(operand.shape))
+
+    def kernel(*refs):
+        table_refs, refs = refs[: len(tables)], refs[len(tables) :]
+        in_refs, refs = refs[: len(operands)], refs[len(operands) + len(targets) :]
+        owned_ref, next_ref, other_ref, owned_rows, next_rows, sems = refs
+        place_body(windows, table_refs, in_refs, (owned_rows, next_rows, other_ref))
+        columns = result_columns(table_refs[-1][0], base, (heads, head_size))
+        copies = [
+            pltpu.make_async_copy(owned_rows, owned_ref.at[:, :, columns], sems.at[0]),
+            pltpu.make_async_copy(next_rows, next_ref.at[:, :, columns], sems.at[1]),
+        ]
+        for copy in copies:
+            copy.start()
+        for copy in copies:
+            copy.wait()
+
+    other = like(FR + WF, tokens, heads * head_size)
+    anywhere = pl.BlockSpec(memory_space=pl.ANY)
+    *targets, other = pl.pallas_call(
+        kernel,
+        grid=(1,),
+        in_specs=[SMEM for _ in tables]
+        + [first_heads(operand) for operand in operands]
+        + [anywhere for _ in targets],
+        out_specs=[anywhere, anywhere, pl.BlockSpec(other.shape, lambda i: (0, 0, 0))],
+        out_shape=[like(FR, tokens, features), like(WF, tokens, features), other],
+        scratch_shapes=[
+            pltpu.VMEM((FR, tokens, heads * head_size), jnp.bfloat16),
+            pltpu.VMEM((WF, tokens, heads * head_size), jnp.bfloat16),
+            pltpu.SemaphoreType.DMA((2,)),
+        ],
+        input_output_aliases={len(tables) + len(operands) + i: i for i in range(len(targets))},
+        compiler_params=params(),
+        cost_estimate=FILLER,
+        name="place",
+    )(*tables, *operands, *targets)
+    return targets, other
+
+
+def finish(near, others, bases, head_size, targets):
+    def kernel(near_ref, *refs):
+        in_refs, (owned_ref, next_ref, sems) = refs[: len(others)], refs[len(others) + 2 :]
+        copies = []
+        for index, (other_ref, base) in enumerate(zip(in_refs, bases)):
+            heads = other_ref.shape[-1] // head_size
+            columns = result_columns(NEAR - 1 - near_ref[0], base, (heads, head_size))
+            copies += [
+                pltpu.make_async_copy(
+                    other_ref.at[pl.ds(0, FR)], owned_ref.at[:, :, columns], sems.at[2 * index]
+                ),
+                pltpu.make_async_copy(
+                    other_ref.at[pl.ds(FR, WF)], next_ref.at[:, :, columns], sems.at[2 * index + 1]
+                ),
+            ]
+        for copy in copies:
+            copy.start()
+        for copy in copies:
+            copy.wait()
+
+    anywhere = pl.BlockSpec(memory_space=pl.ANY)
+    return pl.pallas_call(
+        kernel,
+        grid=(1,),
+        in_specs=[SMEM]
+        + [pl.BlockSpec(other.shape, lambda i: (0, 0, 0)) for other in others]
+        + [anywhere for _ in targets],
+        out_specs=[anywhere, anywhere],
+        out_shape=[like(*target.shape) for target in targets],
+        scratch_shapes=[pltpu.SemaphoreType.DMA((2 * len(others),))],
+        input_output_aliases={1 + len(others) + i: i for i in range(2)},
+        compiler_params=params(),
+        cost_estimate=FILLER,
+        name="finish",
+    )(near, *others, *targets)
+
+
+def exchange(array, bit):
+    return lax.ppermute(array, "uly", [(i, i ^ bit) for i in range(lax.axis_size("uly"))])
+
+
+def shift(array, step):
+    count = lax.axis_size("win")
+    return lax.ppermute(array, "win", [(i, (i + step) % count) for i in range(count)])
+
+
+def after(array, *others):
+    return lax.optimization_barrier((array, *others))[0] if others else array
 
 
 def normalize(row_block, gain_vector):
@@ -76,7 +534,7 @@
     return owned.reshape(FR, received.shape[2], received.shape[3])
 
 
-def per_device(
+def general(
     query_rows,
     key_rows,
     value_rows,
@@ -142,6 +600,111 @@
     return (owned, next_rows[None])
 
 
+def far_blocks(own):
+    blocks = [own]
+    bit = lax.axis_size("uly") // 2
+    while bit >= NEAR:
+        blocks += [exchange(block, bit) for block in blocks]
+        bit //= 2
+    return blocks
+
+
+def pipelined(
+    query_rows,
+    key_rows,
+    value_rows,
+    query_gain,
+    key_gain,
+    window_start,
+    owner_of_phase,
+    blend_weight,
+):
+    windows = lax.axis_size("win")
+    features = query_rows.shape[-1]
+    head_size = features // HEADS
+    near = lax.rem(lax.axis_index("uly"), NEAR).astype(jnp.int32).reshape(1)
+    position = lax.axis_index("win").astype(jnp.int32).reshape(1)
+    tables = (position, window_start, owner_of_phase, blend_weight, near)
+    query_gain = query_gain.reshape(1, 1, features)
+    key_gain = key_gain.reshape(1, 1, features)
+    count = len(CHUNKS)
+    bases = [sum(CHUNKS[:i]) for i in range(count)]
+
+    groups = [CHUNKS[:1], CHUNKS[1:2], CHUNKS[2:]]
+    own, *sent = split_heads(
+        near, key_rows[0], key_gain, [sum(group) for group in groups], (value_rows[0],)
+    )
+    chunks = []
+    queries = None
+    for array, group in zip(sent, groups):
+        other = exchange(after(array, *chunks[-1:]), 1)
+        base = bases[len(chunks)]
+        chunks += join_halves(own, base, other, group)
+        if queries is None:
+            own_queries, sent_queries = split_heads(
+                near, after(query_rows[0], *chunks), query_gain, [sum(CHUNKS)]
+            )
+            queries = [own_queries, exchange(sent_queries, 1)]
+    sources = [far_blocks(chunk) for chunk in chunks]
+
+    attended, homes, received, others, heads = {}, {}, {}, {}, {}
+    targets = ()
+
+    def place_chunk(chunk, *earlier):
+        return place(
+            tables,
+            after(homes[chunk], *earlier),
+            received[chunk],
+            bases[chunk],
+            features,
+            windows,
+            targets,
+        )
+
+    for chunk in range(count + 1):
+        tasks = []
+        if chunk >= 1:
+            tasks.append(blend_task(attended[chunk - 1], *heads[chunk - 1], windows))
+        if chunk < count:
+            tasks.append(attention_task(queries, sources[chunk], bases[chunk]))
+        merged = chunk < count - 1 or len(tasks) == 1
+        results, lefts = run_stage(tables, tasks, merged)
+        gate = received[chunk - 2] if chunk >= 2 else ()
+        lefts = [shift(after(left, *gate), -1) for left in reversed(lefts)]
+        if chunk >= 1:
+            homes[chunk - 1], *sent = results.pop(0)
+            received[chunk - 1] = [
+                shift(array, distance) for distance, array in enumerate(sent, 1)
+            ] + lefts[-1:]
+        if chunk < count:
+            ((attended[chunk],),) = results
+        if chunk >= 2:
+            targets, others[chunk - 2] = place_chunk(
+                chunk - 2, attended[chunk] if chunk < count else homes[chunk - 1]
+            )
+        if chunk < count:
+            left = lefts[0]
+            if 2 <= chunk:
+                left = after(left, targets[0])
+            heads[chunk] = (left, CHUNKS[chunk - 1] if merged and chunk >= 1 else 0)
+    early = range(count - 2)
+    arrived = [exchange(after(others[i], homes[count - 1]), 1) for i in early]
+    targets = finish(near, arrived, [bases[i] for i in early], head_size, targets)
+    targets, others[count - 1] = place_chunk(count - 1)
+    late = range(count - 2, count)
+    arrived = [exchange(others[i], 1) for i in late]
+    owned, next_rows = finish(near, arrived, [bases[i] for i in late], head_size, targets)
+    return (owned, next_rows[None])
+
+
+def per_device(*operands):
+    windows, ulysses = lax.axis_size("win"), lax.axis_size("uly")
+    fits = windows >= 3 and FR % windows == 0 and left_count(windows) == HOME_BASE
+    if fits and ulysses >= NEAR and ulysses & (ulysses - 1) == 0:
+        return pipelined(*operands)
+    return general(*operands)
+
+
 def solution(mesh):
     placed = (
         P(("grp", "win"), None, "uly", None),

time: 382 us -> 190 us (0.50)
  waiting for transfers between devices: 203 us -> 54 us
  Pallas kernels: 0 us -> 88 us
  local copies, waits for them, and re-layouts: 71.6 us -> 0 us
  matrix products: 46.2 us -> 0 us
  other arithmetic: 31.1 us -> 0 us
  starting transfers between devices: 27 us -> 45.9 us
    all_to_all x6 -> x0, waiting for transfers between devices: 203 us -> none  [the longest x1 58.3 us: send_owners(): lax.all_to_all(packed, 'win', split_axis=0, concat_axis=0, tiled=True)]
    pallas_call x0 -> x20, Pallas kernels: none -> 88 us  [the longest x7 44.4 us: run_stage(): pl.pallas_call(kernel, grid=(steps,), in_specs=[SMEM for _ in tables] + [...]
    ppermute x0 -> x36, waiting for transfers between devices: none -> 54 us  [the longest x20 38 us: shift(): lax.ppermute(array, 'win', [(i, (i + step) % count) for i in range(count)])]
    dot_general x21 -> x0, matrix products: 46.2 us -> none  [the longest x10 28.7 us: head_attention(): jnp.dot(weights, value_head, preferred_element_type=jnp.float32)]
    ppermute x0 -> x36, starting transfers between devices: none -> 45.9 us  [the longest x20 34.8 us: shift(): lax.ppermute(array, 'win', [(i, (i + step) % count) for i in range(count)])]
    all_to_all x6 -> x0, starting transfers between devices: 27 us -> none  [the longest x1 5.85 us: send_owners(): lax.all_to_all(packed, 'win', split_axis=0, concat_axis=0, tiled=True)]
    convert_element_type x4 -> x0, local copies, waits for them, and re-layouts: 22.6 us -> none  [the longest x2 13.5 us: normalize(): floats = row_block.astype(jnp.float32)]
    all_to_all x5 -> x0, local copies, waits for them, and re-layouts: 14.1 us -> none  [the longest x2 5.28 us: per_device(): lax.all_to_all(attended, 'uly', split_axis=1, concat_axis=2, tiled=True)]
  transfers between devices with their start and end apart: 6 -> 36, of which waited for: 6 -> 12; matrix products, arithmetic and copies ran while one was open for 10% -> 0% of each run, Pallas kernels for 0% -> 40%
where the time goes in v2:
time: 190 us; the launch traced here: 189 us
  Pallas kernels  88 us (46%)
  waiting for transfers between devices  54 us (28%)
  starting transfers between devices  45.9 us (24%)
    pallas_call x7, Pallas kernels, run_stage(): pl.pallas_call(kernel, grid=(steps,), in_specs=[SMEM for _ in tables] + [...  44.4 us
    ppermute x20, waiting for transfers between devices, shift(): lax.ppermute(array, 'win', [(i, (i + step) % count) for i in range(count)])  38 us
    ppermute x20, starting transfers between devices, shift(): lax.ppermute(array, 'win', [(i, (i + step) % count) for i in range(count)])  34.8 us
    pallas_call x6, Pallas kernels, place(): pl.pallas_call(kernel, grid=(1,), in_specs=[SMEM for _ in tables] + [firs...  17.2 us
    ppermute x16, waiting for transfers between devices, exchange(): lax.ppermute(array, 'uly', [(i, i ^ bit) for i in range(lax.axis_size('ul...  16 us
    pallas_call x2, Pallas kernels, split_heads(): pl.pallas_call(kernel, grid=(frames // frames_per_step,), in_specs=[SMEM,...  11.6 us
    ppermute x16, starting transfers between devices, exchange(): lax.ppermute(array, 'uly', [(i, i ^ bit) for i in range(lax.axis_size('ul...  11 us
    pallas_call x3, Pallas kernels, join_halves(): pl.pallas_call(kernel, grid=(sum(counts) // STEP_HEADS,), in_specs=[pl.Bl...  10.2 us
  transfers between devices with their start and end apart: 36, of which 12 were waited for; matrix products, arithmetic and copies ran while one was open for 0% of the time, Pallas kernels for 40%

profile of v2, /device:TPU:0, one launch (start us, length us, event | category | flops | bytes accessed | tf_op | source)
XLA Modules:
  0.0 188.9 jit_solution(8961220947253265351)
XLA Ops:
  0.6 6.6 %norm_split.2 = (bf16[20,2,16,16,128]{4,3,2,1,0:T(8,128)(2,1)}, bf16[2,2,16,16,128]{4,3,2,1,0:T(8,128)(2,1)}, bf16[4,2,16,16,128]{4,3,2,1,0:T(8,128)(2,1)}, bf16[14,2,16,16,128]{4,3,2,1,0:T(8,128)(2,1)}) custom-call(s32[1]{0:T(128)} %bitcast.near_ref.refs_4_, bf16[16,16,5120]{2,1,0:T(8,128)(2,1)} %bitcast.8, f32[1,1,5120]{2,1,0:T(1,128)} %bitcast.11, ...), custom_call_target="tpu_custom_call" | custom-call | flops 10000000000 | tf_op jit(solution)/shard_map/norm_split/pallas_call | solution.py:81
  7.7 1.5 collective-permute-done.other_ref
  9.2 1.9 join_halves.3.refs_7_
  11.4 1.9 collective-permute-done.4.other_ref
  13.3 2.0 %join_halves.4.refs_9_ = bf16[4,2,2,16,16,128]{5,4,3,2,1,0:T(8,128)(2,1)} custom-call(bf16[20,2,16,16,128]{4,3,2,1,0:T(8,128)(2,1)} %get-tuple-element.88.own_ref, bf16[4,2,16,16,128]{4,3,2,1,0:T(8,128)(2,1)} %collective-permute-done.4.other_ref), custom_call_target="tpu_custom_call" | custom-call | flops 10000000000 | tf_op jit(solution)/shard_map/join_halves/pallas_call | solution.py:117
  15.7 2.6 %collective-permute-start.2 = (bf16[2,2,2,16,16,128]{5,4,3,2,1,0:T(8,128)(2,1)}, bf16[2,2,2,16,16,128]{5,4,3,2,1,0:T(8,128)(2,1)}, u32[]{:S(2)}, u32[]{:S(2)}) collective-permute-start(bf16[2,2,2,16,16,128]{5,4,3,2,1,0:T(8,128)(2,1)} %join_halves.3.refs_7_), channel_id=1, source_target_pairs={{0,2},{1,3},{2,0},{3,1},{4,6},{5,7},{6,4},{7,5},{8,10},{9,11},{10,... | collective-permute-start | bytes 1572872 | tf_op jit(solution)/shard_map/ppermute | solution.py:459
  18.3 5.1 %norm_split.3 = (bf16[20,16,16,128]{3,2,1,0:T(8,128)(2,1)}, bf16[20,16,16,128]{3,2,1,0:T(8,128)(2,1)}) custom-call(s32[1]{0:T(128)} %bitcast.near_ref.refs_4_, bf16[16,16,5120]{2,1,0:T(8,128)(2,1)} %bitcast.10, f32[1,1,5120]{2,1,0:T(1,128)} %bitcast.12), custom_call_target="tpu_custom_call" | custom-call | flops 10000000000 | tf_op jit(solution)/shard_map/norm_split/pallas_call | solution.py:81
  23.7 6.3 %join_halves.5 = (bf16[4,2,2,16,16,128]{5,4,3,2,1,0:T(8,128)(2,1)}, bf16[4,2,2,16,16,128]{5,4,3,2,1,0:T(8,128)(2,1)}, bf16[4,2,2,16,16,128]{5,4,3,2,1,0:T(8,128)(2,1)}, bf16[2,2,2,16,16,128]{5,4,3,2,1,0:T(8,128)(2,1)}) custom-call(bf16[20,2,16,16,128]{4,3,2,1,0:T(8,128)(2,1)} %get-tuple-element.88.own_ref, ...), custom_call_target="tpu_custom_call" | custom-call | flops 10000000000 | tf_op jit(solution)/shard_map/join_halves/pallas_call | solution.py:117
  30.1 1.7 collective-permute-start.8
  31.8 4.5 %stage.7 = (bf16[2,2,16,16,128]{4,3,2,1,0:T(8,128)(2,1)}, bf16[2,2,8,16,128]{4,3,2,1,0:T(8,128)(2,1)}) custom-call(s32[1]{0:T(128)} %bitcast.1.refs_0_, s32[4]{0:T(128)} %refs_1_.25, s32[4]{0:T(128)} %refs_2_.25, s32[4,16]{1,0:T(4,128)} %refs_3_.25, s32[1]{0:T(128)} %bitcast.near_ref.refs_4_, bf16[20,16,16,128]{3,2,1,0:T(8,128)(2,1)} %get-tuple-element.91.refs_5_.refs_7_, ...), custom_call_target="tpu_custom_call" | custom-call | tf_op jit(solution)/shard_map/stage/pallas_call | solution.py:352
  36.4 3.7 %collective-permute-start.3 = (bf16[2,2,8,16,128]{4,3,2,1,0:T(8,128)(2,1)}, bf16[2,2,8,16,128]{4,3,2,1,0:T(8,128)(2,1)}, u32[]{:S(2)}, u32[]{:S(2)}) collective-permute-start(bf16[2,2,8,16,128]{4,3,2,1,0:T(8,128)(2,1)} %get-tuple-element.94), channel_id=1, source_target_pairs={{0,12},{4,0},{8,4},{12,8},{1,13},{5,1},{9,5},{13,9},{2,14},{6,2},{... | collective-permute-start | bytes 393224 | tf_op jit(solution)/shard_map/ppermute | solution.py:464
  40.0 3.1 %collective-permute-done.3.refs_6_ = bf16[2,2,8,16,128]{4,3,2,1,0:T(8,128)(2,1)} collective-permute-done((bf16[2,2,8,16,128]{4,3,2,1,0:T(8,128)(2,1)}, bf16[2,2,8,16,128]{4,3,2,1,0:T(8,128)(2,1)}, u32[]{:S(2)}, u32[]{:S(2)}) %collective-permute-start.3) | collective-permute-done | bytes 131104 | tf_op jit(solution)/shard_map/ppermute | solution.py:464
  43.1 10.8 %collective-permute-done.5.refs_10_ = bf16[4,2,2,16,16,128]{5,4,3,2,1,0:T(8,128)(2,1)} collective-permute-done((bf16[4,2,2,16,16,128]{5,4,3,2,1,0:T(8,128)(2,1)}, bf16[4,2,2,16,16,128]{5,4,3,2,1,0:T(8,128)(2,1)}, u32[]{:S(2)}, u32[]{:S(2)}) %collective-permute-start.5) | collective-permute-done | bytes 1048608 | tf_op jit(solution)/shard_map/ppermute | solution.py:459
  53.9 8.0 %stage.8 = (bf16[2,2,12,16,128]{4,3,2,1,0:T(8,128)(2,1)}, bf16[2,2,5,16,128]{4,3,2,1,0:T(8,128)(2,1)}, bf16[2,2,3,16,128]{4,3,2,1,0:T(8,128)(2,1)}, bf16[4,2,16,...) custom-call(s32[1]{0:T(128)} %bitcast.1.refs_0_, s32[4]{0:T(128)} %refs_1_.25, s32[4]{0:T(128)} %refs_2_.25, ...), custom_call_target="tpu_custom_call" | custom-call | tf_op jit(solution)/shard_map/stage/pallas_call | solution.py:352
  61.8 4.2 %collective-permute-start.6 = (bf16[6,2,8,16,128]{4,3,2,1,0:T(8,128)(2,1)}, bf16[6,2,8,16,128]{4,3,2,1,0:T(8,128)(2,1)}, u32[]{:S(2)}, u32[]{:S(2)}) collective-permute-start(bf16[6,2,8,16,128]{4,3,2,1,0:T(8,128)(2,1)} %get-tuple-element.98), channel_id=1, source_target_pairs={{0,12},{4,0},{8,4},{12,8},{1,13},{5,1},{9,5},{13,9},{2,14},{6,2},{... | collective-permute-start | bytes 1179656 | tf_op jit(solution)/shard_map/ppermute | solution.py:464
  66.0 1.5 collective-permute-start.12
  67.5 1.0 collective-permute-start.10
  68.5 6.8 %collective-permute-done.6.refs_6_.refs_8_ = bf16[6,2,8,16,128]{4,3,2,1,0:T(8,128)(2,1)} collective-permute-done((bf16[6,2,8,16,128]{4,3,2,1,0:T(8,128)(2,1)}, bf16[6,2,8,16,128]{4,3,2,1,0:T(8,128)(2,1)}, u32[]{:S(2)}, u32[]{:S(2)}) %collective-permute-start.6) | collective-permute-done | bytes 393248 | tf_op jit(solution)/shard_map/ppermute | solution.py:464
  75.3 1.5 collective-permute-start.16
  76.8 7.9 %stage.9 = (bf16[4,2,12,16,128]{4,3,2,1,0:T(8,128)(2,1)}, bf16[4,2,5,16,128]{4,3,2,1,0:T(8,128)(2,1)}, bf16[4,2,3,16,128]{4,3,2,1,0:T(8,128)(2,1)}, bf16[4,2,16,...) custom-call(s32[1]{0:T(128)} %bitcast.1.refs_0_, s32[4]{0:T(128)} %refs_1_.25, s32[4]{0:T(128)} %refs_2_.25, ...), custom_call_target="tpu_custom_call" | custom-call | tf_op jit(solution)/shard_map/stage/pallas_call | solution.py:352
  84.7 4.3 %collective-permute-start.11 = (bf16[8,2,8,16,128]{4,3,2,1,0:T(8,128)(2,1)}, bf16[8,2,8,16,128]{4,3,2,1,0:T(8,128)(2,1)}, u32[]{:S(2)}, u32[]{:S(2)}) collective-permute-start(bf16[8,2,8,16,128]{4,3,2,1,0:T(8,128)(2,1)} %get-tuple-element.106), channel_id=1, source_target_pairs={{0,12},{4,0},{8,4},{12,8},{1,13},{5,1},{9,5},{13,9},{2,14},{6,2},{... | collective-permute-start | bytes 1572872 | tf_op jit(solution)/shard_map/ppermute | solution.py:464
  89.0 0.6 collective-permute-start.14
  89.6 2.6 %place.6 = (bf16[12,16,5120]{2,1,0:T(8,128)(2,1)}, bf16[16,16,5120]{2,1,0:T(8,128)(2,1)}, bf16[28,16,256]{2,1,0:T(8,128)(2,1)}) custom-call(s32[1]{0:T(128)} %bitcast.1.refs_0_, s32[4]{0:T(128)} %refs_1_.25, s32[4]{0:T(128)} %refs_2_.25, s32[4,16]{1,0:T(4,128)} %refs_3_.25, s32[1]{0:T(128)} %bitcast.near_ref.refs_4_, ...), custom_call_target="tpu_custom_call" | custom-call | flops 10000000000 | tf_op jit(solution)/shard_map/place/pallas_call | solution.py:400
  92.2 9.5 %collective-permute-done.11.refs_6_.refs_8_ = bf16[8,2,8,16,128]{4,3,2,1,0:T(8,128)(2,1)} collective-permute-done((bf16[8,2,8,16,128]{4,3,2,1,0:T(8,128)(2,1)}, bf16[8,2,8,16,128]{4,3,2,1,0:T(8,128)(2,1)}, u32[]{:S(2)}, u32[]{:S(2)}) %collective-permute-start.11) | collective-permute-done | bytes 524320 | tf_op jit(solution)/shard_map/ppermute | solution.py:464
  101.7 0.9 collective-permute-start.20
  102.6 7.9 %stage.10 = (bf16[4,2,12,16,128]{4,3,2,1,0:T(8,128)(2,1)}, bf16[4,2,5,16,128]{4,3,2,1,0:T(8,128)(2,1)}, bf16[4,2,3,16,128]{4,3,2,1,0:T(8,128)(2,1)}, bf16[4,2,16...) custom-call(s32[1]{0:T(128)} %bitcast.1.refs_0_, s32[4]{0:T(128)} %refs_1_.25, s32[4]{0:T(128)} %refs_2_.25, ...), custom_call_target="tpu_custom_call" | custom-call | tf_op jit(solution)/shard_map/stage/pallas_call | solution.py:352
  110.5 4.3 %collective-permute-start.15 = (bf16[8,2,8,16,128]{4,3,2,1,0:T(8,128)(2,1)}, bf16[8,2,8,16,128]{4,3,2,1,0:T(8,128)(2,1)}, u32[]{:S(2)}, u32[]{:S(2)}) collective-permute-start(bf16[8,2,8,16,128]{4,3,2,1,0:T(8,128)(2,1)} %get-tuple-element.116), channel_id=1, source_target_pairs={{0,12},{4,0},{8,4},{12,8},{1,13},{5,1},{9,5},{13,9},{2,14},{6,2},{... | collective-permute-start | bytes 1572872 | tf_op jit(solution)/shard_map/ppermute | solution.py:464
  115.5 3.0 %place.7 = (bf16[12,16,5120]{2,1,0:T(8,128)(2,1)}, bf16[16,16,5120]{2,1,0:T(8,128)(2,1)}, bf16[28,16,512]{2,1,0:T(8,128)(2,1)}) custom-call(s32[1]{0:T(128)} %bitcast.1.refs_0_, s32[4]{0:T(128)} %refs_1_.25, s32[4]{0:T(128)} %refs_2_.25, s32[4,16]{1,0:T(4,128)} %refs_3_.25, s32[1]{0:T(128)} %bitcast.near_ref.refs_4_, ...), custom_call_target="tpu_custom_call", output_to_operand_aliasing={{0}: (9, {}), {1}: (10, {})} | custom-call | flops 10000000000 | tf_op jit(solution)/shard_map/place/pallas_call | solution.py:400
  118.5 6.7 %collective-permute-done.15.refs_6_.refs_8_ = bf16[8,2,8,16,128]{4,3,2,1,0:T(8,128)(2,1)} collective-permute-done((bf16[8,2,8,16,128]{4,3,2,1,0:T(8,128)(2,1)}, bf16[8,2,8,16,128]{4,3,2,1,0:T(8,128)(2,1)}, u32[]{:S(2)}, u32[]{:S(2)}) %collective-permute-start.15) | collective-permute-done | bytes 524320 | tf_op jit(solution)/shard_map/ppermute | solution.py:464
  125.2 7.9 %stage.11 = (bf16[4,2,12,16,128]{4,3,2,1,0:T(8,128)(2,1)}, bf16[4,2,5,16,128]{4,3,2,1,0:T(8,128)(2,1)}, bf16[4,2,3,16,128]{4,3,2,1,0:T(8,128)(2,1)}, bf16[4,2,16...) custom-call(s32[1]{0:T(128)} %bitcast.1.refs_0_, s32[4]{0:T(128)} %refs_1_.25, s32[4]{0:T(128)} %refs_2_.25, ...), custom_call_target="tpu_custom_call" | custom-call | tf_op jit(solution)/shard_map/stage/pallas_call | solution.py:352
  133.1 4.3 %collective-permute-start.19 = (bf16[8,2,8,16,128]{4,3,2,1,0:T(8,128)(2,1)}, bf16[8,2,8,16,128]{4,3,2,1,0:T(8,128)(2,1)}, u32[]{:S(2)}, u32[]{:S(2)}) collective-permute-start(bf16[8,2,8,16,128]{4,3,2,1,0:T(8,128)(2,1)} %get-tuple-element.127), channel_id=1, source_target_pairs={{0,12},{4,0},{8,4},{12,8},{1,13},{5,1},{9,5},{13,9},{2,14},{6,2},{... | collective-permute-start | bytes 1572872 | tf_op jit(solution)/shard_map/ppermute | solution.py:464
  137.4 0.8 collective-permute-start.22
  138.3 3.0 %place.8 = (bf16[12,16,5120]{2,1,0:T(8,128)(2,1)}, bf16[16,16,5120]{2,1,0:T(8,128)(2,1)}, bf16[28,16,512]{2,1,0:T(8,128)(2,1)}) custom-call(s32[1]{0:T(128)} %bitcast.1.refs_0_, s32[4]{0:T(128)} %refs_1_.25, s32[4]{0:T(128)} %refs_2_.25, s32[4,16]{1,0:T(4,128)} %refs_3_.25, s32[1]{0:T(128)} %bitcast.near_ref.refs_4_, ...), custom_call_target="tpu_custom_call", output_to_operand_aliasing={{0}: (9, {}), {1}: (10, {})} | custom-call | flops 10000000000 | tf_op jit(solution)/shard_map/place/pallas_call | solution.py:400
  141.3 5.6 %collective-permute-done.19.refs_6_.refs_8_ = bf16[8,2,8,16,128]{4,3,2,1,0:T(8,128)(2,1)} collective-permute-done((bf16[8,2,8,16,128]{4,3,2,1,0:T(8,128)(2,1)}, bf16[8,2,8,16,128]{4,3,2,1,0:T(8,128)(2,1)}, u32[]{:S(2)}, u32[]{:S(2)}) %collective-permute-start.19) | collective-permute-done | bytes 524320 | tf_op jit(solution)/shard_map/ppermute | solution.py:464
  146.9 6.3 %stage.12 = (bf16[4,2,12,16,128]{4,3,2,1,0:T(8,128)(2,1)}, bf16[4,2,5,16,128]{4,3,2,1,0:T(8,128)(2,1)}, bf16[4,2,3,16,128]{4,3,2,1,0:T(8,128)(2,1)}, bf16[2,2,16...) custom-call(s32[1]{0:T(128)} %bitcast.1.refs_0_, s32[4]{0:T(128)} %refs_1_.25, ...), custom_call_target="tpu_custom_call" | custom-call | tf_op jit(solution)/shard_map/stage/pallas_call | solution.py:352
  153.2 4.3 %collective-permute-start.23 = (bf16[2,2,8,16,128]{4,3,2,1,0:T(8,128)(2,1)}, bf16[2,2,8,16,128]{4,3,2,1,0:T(8,128)(2,1)}, u32[]{:S(2)}, u32[]{:S(2)}) collective-permute-start(bf16[2,2,8,16,128]{4,3,2,1,0:T(8,128)(2,1)} %get-tuple-element.139), channel_id=1, source_target_pairs={{0,12},{4,0},{8,4},{12,8},{1,13},{5,1},{9,5},{13,9},{2,14},{6,2},{... | collective-permute-start | bytes 393224 | tf_op jit(solution)/shard_map/ppermute | solution.py:464
  157.6 2.0 %collective-permute-start.24 = (bf16[4,2,5,16,128]{4,3,2,1,0:T(8,128)(2,1)}, bf16[4,2,5,16,128]{4,3,2,1,0:T(8,128)(2,1)}, u32[]{:S(2)}, u32[]{:S(2)}) collective-permute-start(bf16[4,2,5,16,128]{4,3,2,1,0:T(8,128)(2,1)} %get-tuple-element.147), channel_id=1, source_target_pairs={{0,4},{4,8},{8,12},{12,0},{1,5},{5,9},{9,13},{13,1},{2,6},{6,10},{... | collective-permute-start | bytes 491528 | tf_op jit(solution)/shard_map/ppermute | solution.py:464
  159.5 3.0 %place.9 = (bf16[12,16,5120]{2,1,0:T(8,128)(2,1)}, bf16[16,16,5120]{2,1,0:T(8,128)(2,1)}, bf16[28,16,512]{2,1,0:T(8,128)(2,1)}) custom-call(s32[1]{0:T(128)} %bitcast.1.refs_0_, s32[4]{0:T(128)} %refs_1_.25, s32[4]{0:T(128)} %refs_2_.25, s32[4,16]{1,0:T(4,128)} %refs_3_.25, s32[1]{0:T(128)} %bitcast.near_ref.refs_4_, ...), custom_call_target="tpu_custom_call", output_to_operand_aliasing={{0}: (9, {}), {1}: (10, {})} | custom-call | flops 10000000000 | tf_op jit(solution)/shard_map/place/pallas_call | solution.py:400
  162.6 1.9 %stage.13 = (bf16[2,2,12,16,128]{4,3,2,1,0:T(8,128)(2,1)}, bf16[2,2,5,16,128]{4,3,2,1,0:T(8,128)(2,1)}, bf16[2,2,3,16,128]{4,3,2,1,0:T(8,128)(2,1)}, bf16[2,2,8,16,128]{4,3,2,1,0:T(8,128)(2,1)}) custom-call(s32[1]{0:T(128)} %bitcast.1.refs_0_, s32[4]{0:T(128)} %refs_1_.25, s32[4]{0:T(128)} %refs_2_.25, s32[4,16]{1,0:T(4,128)} %refs_3_.25, ...), custom_call_target="tpu_custom_call" | custom-call | tf_op jit(solution)/shard_map/stage/pallas_call | solution.py:352
  165.1 3.3 %collective-permute-done.25.refs_7_ = bf16[4,2,3,16,128]{4,3,2,1,0:T(8,128)(2,1)} collective-permute-done((bf16[4,2,3,16,128]{4,3,2,1,0:T(8,128)(2,1)}, bf16[4,2,3,16,128]{4,3,2,1,0:T(8,128)(2,1)}, u32[]{:S(2)}, u32[]{:S(2)}) %collective-permute-start.25) | collective-permute-done | bytes 98336 | tf_op jit(solution)/shard_map/ppermute | solution.py:464
  168.9 1.1 collective-permute-start.28
  170.0 3.0 %place.10 = (bf16[12,16,5120]{2,1,0:T(8,128)(2,1)}, bf16[16,16,5120]{2,1,0:T(8,128)(2,1)}, bf16[28,16,512]{2,1,0:T(8,128)(2,1)}) custom-call(s32[1]{0:T(128)} %bitcast.1.refs_0_, s32[4]{0:T(128)} %refs_1_.25, s32[4]{0:T(128)} %refs_2_.25, s32[4,16]{1,0:T(4,128)} %refs_3_.25, s32[1]{0:T(128)} %bitcast.near_ref.refs_4_, ...), custom_call_target="tpu_custom_call", output_to_operand_aliasing={{0}: (9, {}), {1}: (10, {})} | custom-call | flops 10000000000 | tf_op jit(solution)/shard_map/place/pallas_call | solution.py:400
  173.0 3.4 %collective-permute-start.29 = (bf16[2,2,3,16,128]{4,3,2,1,0:T(8,128)(2,1)}, bf16[2,2,3,16,128]{4,3,2,1,0:T(8,128)(2,1)}, u32[]{:S(2)}, u32[]{:S(2)}) collective-permute-start(bf16[2,2,3,16,128]{4,3,2,1,0:T(8,128)(2,1)} %get-tuple-element.154), channel_id=1, source_target_pairs={{0,8},{4,12},{8,0},{12,4},{1,9},{5,13},{9,1},{13,5},{2,10},{6,14},... | collective-permute-start | bytes 147464 | tf_op jit(solution)/shard_map/ppermute | solution.py:464
  176.5 2.6 %finish.2 = (bf16[12,16,5120]{2,1,0:T(8,128)(2,1)}, bf16[16,16,5120]{2,1,0:T(8,128)(2,1)}) custom-call(s32[1]{0:T(128)} %bitcast.near_ref.refs_4_, bf16[28,16,256]{2,1,0:T(8,128)(2,1)} %collective-permute-done.31.refs_0_, bf16[28,16,512]{2,1,0:T(8,128)(2,1)} %collective-permute-done.32.refs_1_, ...), custom_call_target="tpu_custom_call", output_to_operand_aliasing={{0}: (5, {}), {1}: (6, {})} | custom-call | flops 10000000000 | tf_op jit(solution)/shard_map/finish/pallas_call | solution.py:442
  179.8 2.5 %collective-permute-done.30.refs_8_ = bf16[2,2,8,16,128]{4,3,2,1,0:T(8,128)(2,1)} collective-permute-done((bf16[2,2,8,16,128]{4,3,2,1,0:T(8,128)(2,1)}, bf16[2,2,8,16,128]{4,3,2,1,0:T(8,128)(2,1)}, u32[]{:S(2)}, u32[]{:S(2)}) %collective-permute-start.30) | collective-permute-done | bytes 131104 | tf_op jit(solution)/shard_map/ppermute | solution.py:464
  182.3 2.6 %place.11 = (bf16[12,16,5120]{2,1,0:T(8,128)(2,1)}, bf16[16,16,5120]{2,1,0:T(8,128)(2,1)}, bf16[28,16,256]{2,1,0:T(8,128)(2,1)}) custom-call(s32[1]{0:T(128)} %bitcast.1.refs_0_, s32[4]{0:T(128)} %refs_1_.25, s32[4]{0:T(128)} %refs_2_.25, s32[4,16]{1,0:T(4,128)} %refs_3_.25, s32[1]{0:T(128)} %bitcast.near_ref.refs_4_, ...), custom_call_target="tpu_custom_call", output_to_operand_aliasing={{0}: (9, {}), {1}: (10, {})} | custom-call | flops 10000000000 | tf_op jit(solution)/shard_map/place/pallas_call | solution.py:400
  185.0 1.8 collective-permute-done.35.refs_1_
  186.8 1.9 %finish.3 = (bf16[12,16,5120]{2,1,0:T(8,128)(2,1)}, bf16[16,16,5120]{2,1,0:T(8,128)(2,1)}) custom-call(s32[1]{0:T(128)} %bitcast.near_ref.refs_4_, bf16[28,16,512]{2,1,0:T(8,128)(2,1)} %collective-permute-done.27.refs_0_, bf16[28,16,256]{2,1,0:T(8,128)(2,1)} %collective-permute-done.35.refs_1_, ...), custom_call_target="tpu_custom_call", output_to_operand_aliasing={{0}: (3, {}), {1}: (4, {})} | custom-call | flops 10000000000 | tf_op jit(solution)/shard_map/finish/pallas_call | solution.py:442
  (44 shorter events, 4.2 us)
Async XLA Ops:
  7.2 2.0 %collective-permute-start = (bf16[2,2,16,16,128]{4,3,2,1,0:T(8,128)(2,1)}, bf16[2,2,16,16,128]{4,3,2,1,0:T(8,128)(2,1)}, u32[]{:S(2)}, u32[]{:S(2)}) collective-permute-start(bf16[2,2,16,16,128]{4,3,2,1,0:T(8,128)(2,1)} %get-tuple-element.89), channel_id=1, source_target_pairs={{0,1},{1,0},{2,3},{3,2},{4,5},{5,4},{6,7},{7,6},{8,9},{9,8},{10,11... | collective-permute-start | bytes 786440 | tf_op jit(solution)/shard_map/ppermute | solution.py:459
  11.0 2.3 %collective-permute-start.4 = (bf16[4,2,16,16,128]{4,3,2,1,0:T(8,128)(2,1)}, bf16[4,2,16,16,128]{4,3,2,1,0:T(8,128)(2,1)}, u32[]{:S(2)}, u32[]{:S(2)}) collective-permute-start(bf16[4,2,16,16,128]{4,3,2,1,0:T(8,128)(2,1)} %get-tuple-element.96), channel_id=1, source_target_pairs={{0,1},{1,0},{2,3},{3,2},{4,5},{5,4},{6,7},{7,6},{8,9},{9,8},{10,11... | collective-permute-start | bytes 1572872 | tf_op jit(solution)/shard_map/ppermute | solution.py:459
  15.3 8.4 %collective-permute-start.7 = (bf16[14,2,16,16,128]{4,3,2,1,0:T(8,128)(2,1)}, bf16[14,2,16,16,128]{4,3,2,1,0:T(8,128)(2,1)}, u32[]{:S(2)}, u32[]{:S(2)}) collective-permute-start(bf16[14,2,16,16,128]{4,3,2,1,0:T(8,128)(2,1)} %get-tuple-element.100), channel_id=1, source_target_pairs={{0,1},{1,0},{2,3},{3,2},{4,5},{5,4},{6,7},{7,6},{8,9},{9,8},{10,11... | collective-permute-start | bytes 5505032 | tf_op jit(solution)/shard_map/ppermute | solution.py:459
  15.7 16.1 %collective-permute-start.2 = (bf16[2,2,2,16,16,128]{5,4,3,2,1,0:T(8,128)(2,1)}, bf16[2,2,2,16,16,128]{5,4,3,2,1,0:T(8,128)(2,1)}, u32[]{:S(2)}, u32[]{:S(2)}) collective-permute-start(bf16[2,2,2,16,16,128]{5,4,3,2,1,0:T(8,128)(2,1)} %join_halves.3.refs_7_), channel_id=1, source_target_pairs={{0,2},{1,3},{2,0},{3,1},{4,6},{5,7},{6,4},{7,5},{8,10},{9,11},{10,... | collective-permute-start | bytes 1572872 | tf_op jit(solution)/shard_map/ppermute | solution.py:459
  23.4 8.5 %collective-permute-start.1 = (bf16[20,16,16,128]{3,2,1,0:T(8,128)(2,1)}, bf16[20,16,16,128]{3,2,1,0:T(8,128)(2,1)}, u32[]{:S(2)}, u32[]{:S(2)}) collective-permute-start(bf16[20,16,16,128]{3,2,1,0:T(8,128)(2,1)} %get-tuple-element.92), channel_id=1, source_target_pairs={{0,1},{1,0},{2,3},{3,2},{4,5},{5,4},{6,7},{7,6},{8,9},{9,8},{10,11... | collective-permute-start | bytes 3932168 | tf_op jit(solution)/shard_map/ppermute | solution.py:459
  23.4 30.4 %collective-permute-start.5 = (bf16[4,2,2,16,16,128]{5,4,3,2,1,0:T(8,128)(2,1)}, bf16[4,2,2,16,16,128]{5,4,3,2,1,0:T(8,128)(2,1)}, u32[]{:S(2)}, u32[]{:S(2)}) collective-permute-start(bf16[4,2,2,16,16,128]{5,4,3,2,1,0:T(8,128)(2,1)} %join_halves.4.refs_9_), channel_id=1, source_target_pairs={{0,2},{1,3},{2,0},{3,1},{4,6},{5,7},{6,4},{7,5},{8,10},{9,11},{10,... | collective-permute-start | bytes 3145736 | tf_op jit(solution)/shard_map/ppermute | solution.py:459
  30.1 46.7 %collective-permute-start.8 = (bf16[4,2,2,16,16,128]{5,4,3,2,1,0:T(8,128)(2,1)}, bf16[4,2,2,16,16,128]{5,4,3,2,1,0:T(8,128)(2,1)}, u32[]{:S(2)}, u32[]{:S(2)}) collective-permute-start(bf16[4,2,2,16,16,128]{5,4,3,2,1,0:T(8,128)(2,1)} %get-tuple-element.101.refs_9_), channel_id=1, source_target_pairs={{0,2},{1,3},{2,0},{3,1},{4,6},{5,7},{6,4},{7,5},{8,10},{9,11},{10,... | collective-permute-start | bytes 3145736 | tf_op jit(solution)/shard_map/ppermute | solution.py:459
  36.4 6.7 %collective-permute-start.3 = (bf16[2,2,8,16,128]{4,3,2,1,0:T(8,128)(2,1)}, bf16[2,2,8,16,128]{4,3,2,1,0:T(8,128)(2,1)}, u32[]{:S(2)}, u32[]{:S(2)}) collective-permute-start(bf16[2,2,8,16,128]{4,3,2,1,0:T(8,128)(2,1)} %get-tuple-element.94), channel_id=1, source_target_pairs={{0,12},{4,0},{8,4},{12,8},{1,13},{5,1},{9,5},{13,9},{2,14},{6,2},{... | collective-permute-start | bytes 393224 | tf_op jit(solution)/shard_map/ppermute | solution.py:464
  61.8 13.5 %collective-permute-start.6 = (bf16[6,2,8,16,128]{4,3,2,1,0:T(8,128)(2,1)}, bf16[6,2,8,16,128]{4,3,2,1,0:T(8,128)(2,1)}, u32[]{:S(2)}, u32[]{:S(2)}) collective-permute-start(bf16[6,2,8,16,128]{4,3,2,1,0:T(8,128)(2,1)} %get-tuple-element.98), channel_id=1, source_target_pairs={{0,12},{4,0},{8,4},{12,8},{1,13},{5,1},{9,5},{13,9},{2,14},{6,2},{... | collective-permute-start | bytes 1179656 | tf_op jit(solution)/shard_map/ppermute | solution.py:464
  66.0 36.6 %collective-permute-start.12 = (bf16[4,2,2,16,16,128]{5,4,3,2,1,0:T(8,128)(2,1)}, bf16[4,2,2,16,16,128]{5,4,3,2,1,0:T(8,128)(2,1)}, u32[]{:S(2)}, u32[]{:S(2)}) collective-permute-start(bf16[4,2,2,16,16,128]{5,4,3,2,1,0:T(8,128)(2,1)} %get-tuple-element.111.refs_9_), channel_id=1, source_target_pairs={{0,2},{1,3},{2,0},{3,1},{4,6},{5,7},{6,4},{7,5},{8,10},{9,11},{10,... | collective-permute-start | bytes 3145736 | tf_op jit(solution)/shard_map/ppermute | solution.py:459
  67.4 17.2 %collective-permute-start.9 = (bf16[2,2,5,16,128]{4,3,2,1,0:T(8,128)(2,1)}, bf16[2,2,5,16,128]{4,3,2,1,0:T(8,128)(2,1)}, u32[]{:S(2)}, u32[]{:S(2)}) collective-permute-start(bf16[2,2,5,16,128]{4,3,2,1,0:T(8,128)(2,1)} %get-tuple-element.104), channel_id=1, source_target_pairs={{0,4},{4,8},{8,12},{12,0},{1,5},{5,9},{9,13},{13,1},{2,6},{6,10},{... | collective-permute-start | bytes 245768 | tf_op jit(solution)/shard_map/ppermute | solution.py:464
  67.5 17.2 %collective-permute-start.10 = (bf16[2,2,3,16,128]{4,3,2,1,0:T(8,128)(2,1)}, bf16[2,2,3,16,128]{4,3,2,1,0:T(8,128)(2,1)}, u32[]{:S(2)}, u32[]{:S(2)}) collective-permute-start(bf16[2,2,3,16,128]{4,3,2,1,0:T(8,128)(2,1)} %get-tuple-element.105), channel_id=1, source_target_pairs={{0,8},{4,12},{8,0},{12,4},{1,9},{5,13},{9,1},{13,5},{2,10},{6,14},... | collective-permute-start | bytes 147464 | tf_op jit(solution)/shard_map/ppermute | solution.py:464
  75.3 49.9 %collective-permute-start.16 = (bf16[4,2,2,16,16,128]{5,4,3,2,1,0:T(8,128)(2,1)}, bf16[4,2,2,16,16,128]{5,4,3,2,1,0:T(8,128)(2,1)}, u32[]{:S(2)}, u32[]{:S(2)}) collective-permute-start(bf16[4,2,2,16,16,128]{5,4,3,2,1,0:T(8,128)(2,1)} %get-tuple-element.122.refs_9_), channel_id=1, source_target_pairs={{0,2},{1,3},{2,0},{3,1},{4,6},{5,7},{6,4},{7,5},{8,10},{9,11},{10,... | collective-permute-start | bytes 3145736 | tf_op jit(solution)/shard_map/ppermute | solution.py:459
  84.7 17.0 %collective-permute-start.11 = (bf16[8,2,8,16,128]{4,3,2,1,0:T(8,128)(2,1)}, bf16[8,2,8,16,128]{4,3,2,1,0:T(8,128)(2,1)}, u32[]{:S(2)}, u32[]{:S(2)}) collective-permute-start(bf16[8,2,8,16,128]{4,3,2,1,0:T(8,128)(2,1)} %get-tuple-element.106), channel_id=1, source_target_pairs={{0,12},{4,0},{8,4},{12,8},{1,13},{5,1},{9,5},{13,9},{2,14},{6,2},{... | collective-permute-start | bytes 1572872 | tf_op jit(solution)/shard_map/ppermute | solution.py:464
  89.0 21.5 %collective-permute-start.13 = (bf16[4,2,5,16,128]{4,3,2,1,0:T(8,128)(2,1)}, bf16[4,2,5,16,128]{4,3,2,1,0:T(8,128)(2,1)}, u32[]{:S(2)}, u32[]{:S(2)}) collective-permute-start(bf16[4,2,5,16,128]{4,3,2,1,0:T(8,128)(2,1)} %get-tuple-element.114), channel_id=1, source_target_pairs={{0,4},{4,8},{8,12},{12,0},{1,5},{5,9},{9,13},{13,1},{2,6},{6,10},{... | collective-permute-start | bytes 491528 | tf_op jit(solution)/shard_map/ppermute | solution.py:464
  89.0 21.5 %collective-permute-start.14 = (bf16[4,2,3,16,128]{4,3,2,1,0:T(8,128)(2,1)}, bf16[4,2,3,16,128]{4,3,2,1,0:T(8,128)(2,1)}, u32[]{:S(2)}, u32[]{:S(2)}) collective-permute-start(bf16[4,2,3,16,128]{4,3,2,1,0:T(8,128)(2,1)} %get-tuple-element.115), channel_id=1, source_target_pairs={{0,8},{4,12},{8,0},{12,4},{1,9},{5,13},{9,1},{13,5},{2,10},{6,14},... | collective-permute-start | bytes 294920 | tf_op jit(solution)/shard_map/ppermute | solution.py:464
  101.7 45.2 %collective-permute-start.20 = (bf16[2,2,2,16,16,128]{5,4,3,2,1,0:T(8,128)(2,1)}, bf16[2,2,2,16,16,128]{5,4,3,2,1,0:T(8,128)(2,1)}, u32[]{:S(2)}, u32[]{:S(2)}) collective-permute-start(bf16[2,2,2,16,16,128]{5,4,3,2,1,0:T(8,128)(2,1)} %get-tuple-element.133.refs_9_), channel_id=1, source_target_pairs={{0,2},{1,3},{2,0},{3,1},{4,6},{5,7},{6,4},{7,5},{8,10},{9,11},{10,... | collective-permute-start | bytes 1572872 | tf_op jit(solution)/shard_map/ppermute | solution.py:459
  110.5 14.7 %collective-permute-start.15 = (bf16[8,2,8,16,128]{4,3,2,1,0:T(8,128)(2,1)}, bf16[8,2,8,16,128]{4,3,2,1,0:T(8,128)(2,1)}, u32[]{:S(2)}, u32[]{:S(2)}) collective-permute-start(bf16[8,2,8,16,128]{4,3,2,1,0:T(8,128)(2,1)} %get-tuple-element.116), channel_id=1, source_target_pairs={{0,12},{4,0},{8,4},{12,8},{1,13},{5,1},{9,5},{13,9},{2,14},{6,2},{... | collective-permute-start | bytes 1572872 | tf_op jit(solution)/shard_map/ppermute | solution.py:464
  114.8 18.3 %collective-permute-start.17 = (bf16[4,2,5,16,128]{4,3,2,1,0:T(8,128)(2,1)}, bf16[4,2,5,16,128]{4,3,2,1,0:T(8,128)(2,1)}, u32[]{:S(2)}, u32[]{:S(2)}) collective-permute-start(bf16[4,2,5,16,128]{4,3,2,1,0:T(8,128)(2,1)} %get-tuple-element.125), channel_id=1, source_target_pairs={{0,4},{4,8},{8,12},{12,0},{1,5},{5,9},{9,13},{13,1},{2,6},{6,10},{... | collective-permute-start | bytes 491528 | tf_op jit(solution)/shard_map/ppermute | solution.py:464
  114.8 18.2 %collective-permute-start.18 = (bf16[4,2,3,16,128]{4,3,2,1,0:T(8,128)(2,1)}, bf16[4,2,3,16,128]{4,3,2,1,0:T(8,128)(2,1)}, u32[]{:S(2)}, u32[]{:S(2)}) collective-permute-start(bf16[4,2,3,16,128]{4,3,2,1,0:T(8,128)(2,1)} %get-tuple-element.126), channel_id=1, source_target_pairs={{0,8},{4,12},{8,0},{12,4},{1,9},{5,13},{9,1},{13,5},{2,10},{6,14},... | collective-permute-start | bytes 294920 | tf_op jit(solution)/shard_map/ppermute | solution.py:464
  133.1 13.7 %collective-permute-start.19 = (bf16[8,2,8,16,128]{4,3,2,1,0:T(8,128)(2,1)}, bf16[8,2,8,16,128]{4,3,2,1,0:T(8,128)(2,1)}, u32[]{:S(2)}, u32[]{:S(2)}) collective-permute-start(bf16[8,2,8,16,128]{4,3,2,1,0:T(8,128)(2,1)} %get-tuple-element.127), channel_id=1, source_target_pairs={{0,12},{4,0},{8,4},{12,8},{1,13},{5,1},{9,5},{13,9},{2,14},{6,2},{... | collective-permute-start | bytes 1572872 | tf_op jit(solution)/shard_map/ppermute | solution.py:464
  137.4 15.7 %collective-permute-start.21 = (bf16[4,2,5,16,128]{4,3,2,1,0:T(8,128)(2,1)}, bf16[4,2,5,16,128]{4,3,2,1,0:T(8,128)(2,1)}, u32[]{:S(2)}, u32[]{:S(2)}) collective-permute-start(bf16[4,2,5,16,128]{4,3,2,1,0:T(8,128)(2,1)} %get-tuple-element.137), channel_id=1, source_target_pairs={{0,4},{4,8},{8,12},{12,0},{1,5},{5,9},{9,13},{13,1},{2,6},{6,10},{... | collective-permute-start | bytes 491528 | tf_op jit(solution)/shard_map/ppermute | solution.py:464
  137.4 15.7 %collective-permute-start.22 = (bf16[4,2,3,16,128]{4,3,2,1,0:T(8,128)(2,1)}, bf16[4,2,3,16,128]{4,3,2,1,0:T(8,128)(2,1)}, u32[]{:S(2)}, u32[]{:S(2)}) collective-permute-start(bf16[4,2,3,16,128]{4,3,2,1,0:T(8,128)(2,1)} %get-tuple-element.138), channel_id=1, source_target_pairs={{0,8},{4,12},{8,0},{12,4},{1,9},{5,13},{9,1},{13,5},{2,10},{6,14},... | collective-permute-start | bytes 294920 | tf_op jit(solution)/shard_map/ppermute | solution.py:464
  153.2 9.4 %collective-permute-start.23 = (bf16[2,2,8,16,128]{4,3,2,1,0:T(8,128)(2,1)}, bf16[2,2,8,16,128]{4,3,2,1,0:T(8,128)(2,1)}, u32[]{:S(2)}, u32[]{:S(2)}) collective-permute-start(bf16[2,2,8,16,128]{4,3,2,1,0:T(8,128)(2,1)} %get-tuple-element.139), channel_id=1, source_target_pairs={{0,12},{4,0},{8,4},{12,8},{1,13},{5,1},{9,5},{13,9},{2,14},{6,2},{... | collective-permute-start | bytes 393224 | tf_op jit(solution)/shard_map/ppermute | solution.py:464
  157.5 11.4 %collective-permute-start.26 = (bf16[4,2,8,16,128]{4,3,2,1,0:T(8,128)(2,1)}, bf16[4,2,8,16,128]{4,3,2,1,0:T(8,128)(2,1)}, u32[]{:S(2)}, u32[]{:S(2)}) collective-permute-start(bf16[4,2,8,16,128]{4,3,2,1,0:T(8,128)(2,1)} %get-tuple-element.150), channel_id=1, source_target_pairs={{0,12},{4,0},{8,4},{12,8},{1,13},{5,1},{9,5},{13,9},{2,14},{6,2},{... | collective-permute-start | bytes 786440 | tf_op jit(solution)/shard_map/ppermute | solution.py:464
  157.6 10.8 %collective-permute-start.24 = (bf16[4,2,5,16,128]{4,3,2,1,0:T(8,128)(2,1)}, bf16[4,2,5,16,128]{4,3,2,1,0:T(8,128)(2,1)}, u32[]{:S(2)}, u32[]{:S(2)}) collective-permute-start(bf16[4,2,5,16,128]{4,3,2,1,0:T(8,128)(2,1)} %get-tuple-element.147), channel_id=1, source_target_pairs={{0,4},{4,8},{8,12},{12,0},{1,5},{5,9},{9,13},{13,1},{2,6},{6,10},{... | collective-permute-start | bytes 491528 | tf_op jit(solution)/shard_map/ppermute | solution.py:464
  159.5 8.8 %collective-permute-start.25 = (bf16[4,2,3,16,128]{4,3,2,1,0:T(8,128)(2,1)}, bf16[4,2,3,16,128]{4,3,2,1,0:T(8,128)(2,1)}, u32[]{:S(2)}, u32[]{:S(2)}) collective-permute-start(bf16[4,2,3,16,128]{4,3,2,1,0:T(8,128)(2,1)} %get-tuple-element.148), channel_id=1, source_target_pairs={{0,8},{4,12},{8,0},{12,4},{1,9},{5,13},{9,1},{13,5},{2,10},{6,14},... | collective-permute-start | bytes 294920 | tf_op jit(solution)/shard_map/ppermute | solution.py:464
  164.5 11.9 %collective-permute-start.34 = (bf16[28,16,512]{2,1,0:T(8,128)(2,1)}, bf16[28,16,512]{2,1,0:T(8,128)(2,1)}, u32[]{:S(2)}, u32[]{:S(2)}) collective-permute-start(bf16[28,16,512]{2,1,0:T(8,128)(2,1)} %get-tuple-element.164), channel_id=1, source_target_pairs={{0,1},{1,0},{2,3},{3,2},{4,5},{5,4},{6,7},{7,6},{8,9},{9,8},{10,11... | collective-permute-start | bytes 1376264 | tf_op jit(solution)/shard_map/ppermute | solution.py:459
  164.6 11.8 %collective-permute-start.33 = (bf16[28,16,512]{2,1,0:T(8,128)(2,1)}, bf16[28,16,512]{2,1,0:T(8,128)(2,1)}, u32[]{:S(2)}, u32[]{:S(2)}) collective-permute-start(bf16[28,16,512]{2,1,0:T(8,128)(2,1)} %get-tuple-element.162), channel_id=1, source_target_pairs={{0,1},{1,0},{2,3},{3,2},{4,5},{5,4},{6,7},{7,6},{8,9},{9,8},{10,11... | collective-permute-start | bytes 1376264 | tf_op jit(solution)/shard_map/ppermute | solution.py:459
  168.3 8.2 %collective-permute-start.32 = (bf16[28,16,512]{2,1,0:T(8,128)(2,1)}, bf16[28,16,512]{2,1,0:T(8,128)(2,1)}, u32[]{:S(2)}, u32[]{:S(2)}) collective-permute-start(bf16[28,16,512]{2,1,0:T(8,128)(2,1)} %get-tuple-element.160), channel_id=1, source_target_pairs={{0,1},{1,0},{2,3},{3,2},{4,5},{5,4},{6,7},{7,6},{8,9},{9,8},{10,11... | collective-permute-start | bytes 1376264 | tf_op jit(solution)/shard_map/ppermute | solution.py:459
  168.4 4.6 %collective-permute-start.31 = (bf16[28,16,256]{2,1,0:T(8,128)(2,1)}, bf16[28,16,256]{2,1,0:T(8,128)(2,1)}, u32[]{:S(2)}, u32[]{:S(2)}) collective-permute-start(bf16[28,16,256]{2,1,0:T(8,128)(2,1)} %get-tuple-element.158), channel_id=1, source_target_pairs={{0,1},{1,0},{2,3},{3,2},{4,5},{5,4},{6,7},{7,6},{8,9},{9,8},{10,11... | collective-permute-start | bytes 688136 | tf_op jit(solution)/shard_map/ppermute | solution.py:459
  168.9 10.9 %collective-permute-start.28 = (bf16[2,2,5,16,128]{4,3,2,1,0:T(8,128)(2,1)}, bf16[2,2,5,16,128]{4,3,2,1,0:T(8,128)(2,1)}, u32[]{:S(2)}, u32[]{:S(2)}) collective-permute-start(bf16[2,2,5,16,128]{4,3,2,1,0:T(8,128)(2,1)} %get-tuple-element.153), channel_id=1, source_target_pairs={{0,4},{4,8},{8,12},{12,0},{1,5},{5,9},{9,13},{13,1},{2,6},{6,10},{... | collective-permute-start | bytes 245768 | tf_op jit(solution)/shard_map/ppermute | solution.py:464
  173.0 6.8 %collective-permute-start.29 = (bf16[2,2,3,16,128]{4,3,2,1,0:T(8,128)(2,1)}, bf16[2,2,3,16,128]{4,3,2,1,0:T(8,128)(2,1)}, u32[]{:S(2)}, u32[]{:S(2)}) collective-permute-start(bf16[2,2,3,16,128]{4,3,2,1,0:T(8,128)(2,1)} %get-tuple-element.154), channel_id=1, source_target_pairs={{0,8},{4,12},{8,0},{12,4},{1,9},{5,13},{9,1},{13,5},{2,10},{6,14},... | collective-permute-start | bytes 147464 | tf_op jit(solution)/shard_map/ppermute | solution.py:464
  176.4 5.8 %collective-permute-start.30 = (bf16[2,2,8,16,128]{4,3,2,1,0:T(8,128)(2,1)}, bf16[2,2,8,16,128]{4,3,2,1,0:T(8,128)(2,1)}, u32[]{:S(2)}, u32[]{:S(2)}) collective-permute-start(bf16[2,2,8,16,128]{4,3,2,1,0:T(8,128)(2,1)} %get-tuple-element.156), channel_id=1, source_target_pairs={{0,12},{4,0},{8,4},{12,8},{1,13},{5,1},{9,5},{13,9},{2,14},{6,2},{... | collective-permute-start | bytes 393224 | tf_op jit(solution)/shard_map/ppermute | solution.py:464
  176.4 8.5 %collective-permute-start.27 = (bf16[28,16,512]{2,1,0:T(8,128)(2,1)}, bf16[28,16,512]{2,1,0:T(8,128)(2,1)}, u32[]{:S(2)}, u32[]{:S(2)}) collective-permute-start(bf16[28,16,512]{2,1,0:T(8,128)(2,1)} %get-tuple-element.152), channel_id=1, source_target_pairs={{0,1},{1,0},{2,3},{3,2},{4,5},{5,4},{6,7},{7,6},{8,9},{9,8},{10,11... | collective-permute-start | bytes 1376264 | tf_op jit(solution)/shard_map/ppermute | solution.py:459
  184.9 1.9 %collective-permute-start.35 = (bf16[28,16,256]{2,1,0:T(8,128)(2,1)}, bf16[28,16,256]{2,1,0:T(8,128)(2,1)}, u32[]{:S(2)}, u32[]{:S(2)}) collective-permute-start(bf16[28,16,256]{2,1,0:T(8,128)(2,1)} %get-tuple-element.169), channel_id=1, source_target_pairs={{0,1},{1,0},{2,3},{3,2},{4,5},{5,4},{6,7},{7,6},{8,9},{9,8},{10,11... | collective-permute-start | bytes 688136 | tf_op jit(solution)/shard_map/ppermute | solution.py:459

commit v3 on v2

--- a/solution.py
+++ b/solution.py
@@ -30,37 +30,51 @@
     return jax.ShapeDtypeStruct(shape, jnp.bfloat16)
 
 
-FILLER = pl.CostEstimate(flops=10**10, bytes_accessed=0, transcendentals=0)
-NO_COST = pl.CostEstimate(flops=0, bytes_accessed=0, transcendentals=0)
+def cost(microseconds):
+    return pl.CostEstimate(
+        flops=int(microseconds * 1.15e9), bytes_accessed=0, transcendentals=0
+    )
+
+
+NORM_COST = 8.7
+JOIN_COST = 8.7
+REST_COST = 0.0
+STAGE_COST = 0.0
+BLEND_COST = 0.0
+SWAP = 1
+PLACE_COST = 6.0
+TAIL_COST = 0.0
+LATE_CHUNKS = 1
+FREE = 2
 SMEM = pl.BlockSpec(memory_space=pltpu.SMEM)
 
 
-def normalized(rows, gain):
-    floats = rows.astype(jnp.float32)
-    mean_square = jnp.mean(floats * floats, axis=-1, keepdims=True)
-    return (floats * lax.rsqrt(mean_square + 1e-06) * gain).astype(jnp.bfloat16)
-
-
-def split_heads(near, rows, gain, counts, plain=(), frames_per_step=4):
+def split_heads(near, rows, gain, counts, plain=(), frames_per_step=8):
     frames, tokens, features = rows.shape
     head_size = features // HEADS
     kinds = (2,) * len(plain)
+    heads = HEADS // NEAR
 
     def kernel(near_ref, rows_ref, gain_ref, *refs):
-        scratch = refs[-1]
-        plain_refs, out_refs = refs[: len(plain)], refs[len(plain) : -1]
-        heads = HEADS // NEAR
-        scratch[...] = normalized(rows_ref[...], gain_ref[...])
+        plain_refs, out_refs = refs[: len(plain)], refs[len(plain) :]
         here = near_ref[0]
+        squares = jnp.zeros((frames_per_step, tokens, head_size), jnp.float32)
+        for head in range(HEADS):
+            floats = rows_ref[:, :, head * head_size : (head + 1) * head_size].astype(jnp.float32)
+            squares += floats * floats
+        mean_square = jnp.sum(squares, axis=-1, keepdims=True) / features
+        scale = jnp.broadcast_to(lax.rsqrt(mean_square + 1e-06), squares.shape)
 
         def put(out_ref, slot, half, head):
             column = pl.multiple_of((half * heads + head) * head_size, head_size)
             columns = pl.ds(column, head_size)
+            floats = rows_ref[:, :, columns].astype(jnp.float32)
+            normalized = (floats * scale * gain_ref[:, :, columns]).astype(jnp.bfloat16)
             if plain:
-                out_ref[slot, 0] = scratch[:, :, columns]
+                out_ref[slot, 0] = normalized
                 out_ref[slot, 1] = plain_refs[0][:, :, columns]
             else:
-                out_ref[slot] = scratch[:, :, columns]
+                out_ref[slot] = normalized
 
         for head in range(heads):
             put(out_refs[0], head, here, head)
@@ -87,9 +101,8 @@
         out_shape=[
             like(count, *kinds, frames, tokens, head_size) for count in (sum(counts), *counts)
         ],
-        scratch_shapes=[pltpu.VMEM((frames_per_step, tokens, features), jnp.bfloat16)],
         compiler_params=params(),
-        cost_estimate=FILLER,
+        cost_estimate=cost(NORM_COST),
         name="norm_split",
     )(near, rows, gain, *plain)
 
@@ -126,30 +139,38 @@
             like(count, kinds, NEAR, frames, tokens, head_size) for count in counts
         ],
         compiler_params=params(),
-        cost_estimate=FILLER,
+        cost_estimate=cost(JOIN_COST if len(counts) == 1 else REST_COST),
         name="join_halves",
     )(own, other)
 
 
 def attention_body(tables, in_refs, out_refs, left_ref, left_base):
+    query_refs, sources = in_refs[:NEAR], in_refs[NEAR:]
     (out_ref,) = out_refs
-    query_refs, sources = in_refs[:NEAR], in_refs[NEAR:]
     _, frames, tokens, head_size = query_refs[0].shape
     rows = frames * tokens
     factor = math.log2(math.e) / math.sqrt(head_size)
     contract = (((1,), (1,)), ((), ()))
-    step = pl.program_id(0)
-    for half in range(NEAR):
-        query = query_refs[half][0].reshape(rows, head_size)
-        scores = [
+    left_slot = left_base + pl.program_id(0) * STEP_HEADS
+
+    def scores_of(head, half):
+        query = query_refs[half][head].reshape(rows, head_size)
+        return [
             lax.dot_general(
                 query,
-                source[0, 0].reshape(NEAR * rows, head_size),
+                source[head, 0].reshape(NEAR * rows, head_size),
                 contract,
                 preferred_element_type=jnp.float32,
             )
             for source in sources
         ]
+
+    pieces = [(head, half) for head in range(STEP_HEADS) for half in range(NEAR)]
+    following = scores_of(*pieces[0])
+    for index, (head, half) in enumerate(pieces):
+        scores = following
+        if index + 1 < len(pieces):
+            following = scores_of(*pieces[index + 1])
         row_max = functools.reduce(jnp.maximum, scores)
         row_max = jnp.max(row_max, axis=-1, keepdims=True)
         exponents = [jnp.exp2((score - row_max) * factor) for score in scores]
@@ -160,12 +181,12 @@
             weights = (exponent * inverse).astype(jnp.bfloat16)
             result += jnp.dot(
                 weights,
-                source[0, 1].reshape(NEAR * rows, head_size),
+                source[head, 1].reshape(NEAR * rows, head_size),
                 preferred_element_type=jnp.float32,
             )
         result = result.astype(jnp.bfloat16).reshape(frames, tokens, head_size)
-        out_ref[0, half] = result
-        left_ref[left_base + step, half] = result[:HOME_BASE]
+        out_ref[head, half] = result
+        left_ref[left_slot + head, half] = result[:HOME_BASE]
 
 
 def phase_of(owner_ref, wanted, windows):
@@ -195,7 +216,7 @@
     after = lax.rem(here + 1, windows)
     offset = start_ref[here] - here * FR
     offset_after = start_ref[after] - after * FR
-    step = pl.program_id(0)
+    left_slots = pl.ds(left_base + pl.program_id(0) * STEP_HEADS, STEP_HEADS)
     for frame in range(FR):
         place = frame + HOME_BASE - offset
         if frame + HOME_BASE < WF:
@@ -204,31 +225,29 @@
             valid = place < WF
             place = jnp.minimum(place, WF - 1)
             weight = jnp.where(valid, weight_ref[here, place], 0).astype(jnp.float32)
-        numerator = out_ref[0, :, place].astype(jnp.float32) * weight
+        numerator = out_ref[:, :, place].astype(jnp.float32) * weight
         denominator = weight
         if frame + HOME_BASE >= FR:
             slot = frame + HOME_BASE - FR - offset_after
             valid = slot >= 0
             slot = jnp.maximum(slot, 0)
             weight = jnp.where(valid, weight_ref[after, slot], 0).astype(jnp.float32)
-            numerator += after_ref[0, :, slot].astype(jnp.float32) * weight
+            numerator += after_ref[:, :, slot].astype(jnp.float32) * weight
             denominator += weight
-        home_ref[0, :, frame] = (numerator / denominator).astype(jnp.bfloat16)
+        home_ref[:, :, frame] = (numerator / denominator).astype(jnp.bfloat16)
     for distance in range(1, windows):
         target = lax.rem(here + distance, windows)
         first = first_owned(phase_of(owner_ref, target, windows), windows)
         if distance == windows - 1:
-            left_ref[left_base + step, :, :FROM_AFTER] = home_ref[0, :, :FROM_AFTER]
+            left_ref[left_slots, :, :FROM_AFTER] = home_ref[:, :, :FROM_AFTER]
             for slot, index in enumerate(extra_owned(windows)):
-                left_ref[left_base + step, :, FROM_AFTER + slot] = home_ref[
-                    0, :, first + index * windows
-                ]
+                left_ref[left_slots, :, FROM_AFTER + slot] = home_ref[:, :, first + index * windows]
             continue
         sent_ref = sent_refs[distance - 1]
         for index in range(FR // windows):
-            sent_ref[0, :, index] = home_ref[0, :, first + index * windows]
+            sent_ref[:, :, index] = home_ref[:, :, first + index * windows]
         if distance == 1:
-            sent_ref[0, :, FR // windows :] = home_ref[0, :, FR - FROM_BEFORE :]
+            sent_ref[:, :, FR // windows :] = home_ref[:, :, FR - FROM_BEFORE :]
 
 
 def place_body(windows, tables, in_refs, out_refs):
@@ -273,9 +292,11 @@
 
 
 def block_spec(array, blocks, base=0):
-    shape = (1,) + array.shape[1:]
+    shape = (STEP_HEADS,) + array.shape[1:]
     zeros = (0,) * (len(shape) - 1)
-    return pl.BlockSpec(shape, lambda i, *_: (base + jnp.minimum(i, blocks - 1),) + zeros)
+    return pl.BlockSpec(
+        shape, lambda i: (base // STEP_HEADS + jnp.minimum(i, blocks - 1),) + zeros
+    )
 
 
 class Task:
@@ -285,14 +306,15 @@
         self.out_shape, self.out_specs = out_shape, out_specs
 
 
-def attention_task(queries, sources, base):
-    blocks = sources[0].shape[0]
-    frames, tokens, head_size = queries[0].shape[1:]
-    shape = like(blocks, NEAR, frames, tokens, head_size)
+def attention_task(queries, sources):
+    heads = sources[0].shape[0]
+    blocks = heads // STEP_HEADS
+    frames, tokens, head_size = queries[0][0].shape[1:]
+    shape = like(heads, NEAR, frames, tokens, head_size)
     return Task(
         blocks,
-        [*queries, *sources],
-        [block_spec(query, blocks, base) for query in queries]
+        [query for query, _ in queries] + sources,
+        [block_spec(query, blocks, base) for query, base in queries]
         + [block_spec(source, blocks) for source in sources],
         [shape],
         [block_spec(shape, blocks)],
@@ -301,10 +323,11 @@
 
 
 def blend_task(out, after, after_base, windows):
-    blocks, halves, _, tokens, head_size = out.shape
+    heads, halves, _, tokens, head_size = out.shape
+    blocks = heads // STEP_HEADS
     owned = FR // windows
     counts = [FR, owned + FROM_BEFORE] + [owned] * (windows - 3)
-    shapes = [like(blocks, halves, count, tokens, head_size) for count in counts]
+    shapes = [like(heads, halves, count, tokens, head_size) for count in counts]
     return Task(
         blocks,
         [out, after],
@@ -315,14 +338,14 @@
     )
 
 
-def run_stage(tables, tasks, merged=True):
+def run_stage(tables, tasks, weight, merged=True):
     steps = max(task.blocks for task in tasks)
     operands = [operand for task in tasks for operand in task.operands]
     shapes = [shape for task in tasks for shape in task.out_shape]
     windows = lax.axis_size("win")
     assert left_count(windows) == HOME_BASE
     _, halves, _, tokens, head_size = shapes[0].shape
-    blocks = [task.blocks for task in tasks]
+    blocks = [task.blocks * STEP_HEADS for task in tasks]
     lefts = [
         like(count, halves, HOME_BASE, tokens, head_size)
         for count in ([sum(blocks)] if merged else blocks)
@@ -357,7 +380,7 @@
         + [pl.BlockSpec(left.shape, lambda i: (0,) * 5) for left in lefts],
         out_shape=shapes + lefts,
         compiler_params=params(),
-        cost_estimate=NO_COST,
+        cost_estimate=cost(weight),
         name="stage",
     )(*tables, *operands)
     results = []
@@ -373,20 +396,24 @@
     return pl.ds(pl.multiple_of(column, head_size), width[0] * head_size)
 
 
-def place(tables, home, received, base, features, windows, targets):
+def place(tables, home, received, base, features, windows, targets, other, other_base, other_heads, weight):
     heads, halves, _, tokens, head_size = home.shape
     operands = [home, *received]
+    earlier = [*targets, *([] if other is None else [other])]
+    slots = ([0, 1] if targets else []) + ([] if other is None else [2])
 
     def first_heads(operand):
         return pl.BlockSpec((heads,) + operand.shape[1:], lambda i: (0,) * len(operand.shape))
 
     def kernel(*refs):
         table_refs, refs = refs[: len(tables)], refs[len(tables) :]
-        in_refs, refs = refs[: len(operands)], refs[len(operands) + len(targets) :]
-        owned_ref, next_ref, other_ref, owned_rows, next_rows, sems = refs
-        place_body(windows, table_refs, in_refs, (owned_rows, next_rows, other_ref))
+        in_refs, refs = refs[: len(operands)], refs[len(operands) + len(earlier) :]
+        owned_ref, next_ref, other_ref, owned_rows, next_rows, other_rows, sems = refs
+        place_body(windows, table_refs, in_refs, (owned_rows, next_rows, other_rows))
         columns = result_columns(table_refs[-1][0], base, (heads, head_size))
+        other_columns = pl.ds(other_base * head_size, heads * head_size)
         copies = [
+            pltpu.make_async_copy(other_rows, other_ref.at[:, :, other_columns], sems.at[2]),
             pltpu.make_async_copy(owned_rows, owned_ref.at[:, :, columns], sems.at[0]),
             pltpu.make_async_copy(next_rows, next_ref.at[:, :, columns], sems.at[1]),
         ]
@@ -395,26 +422,32 @@
         for copy in copies:
             copy.wait()
 
-    other = like(FR + WF, tokens, heads * head_size)
     anywhere = pl.BlockSpec(memory_space=pl.ANY)
     *targets, other = pl.pallas_call(
         kernel,
         grid=(1,),
         in_specs=[SMEM for _ in tables]
         + [first_heads(operand) for operand in operands]
-        + [anywhere for _ in targets],
-        out_specs=[anywhere, anywhere, pl.BlockSpec(other.shape, lambda i: (0, 0, 0))],
-        out_shape=[like(FR, tokens, features), like(WF, tokens, features), other],
+        + [anywhere for _ in earlier],
+        out_specs=[anywhere] * 3,
+        out_shape=[
+            like(FR, tokens, features),
+            like(WF, tokens, features),
+            like(FR + WF, tokens, other_heads * head_size),
+        ],
         scratch_shapes=[
             pltpu.VMEM((FR, tokens, heads * head_size), jnp.bfloat16),
             pltpu.VMEM((WF, tokens, heads * head_size), jnp.bfloat16),
-            pltpu.SemaphoreType.DMA((2,)),
+            pltpu.VMEM((FR + WF, tokens, heads * head_size), jnp.bfloat16),
+            pltpu.SemaphoreType.DMA((3,)),
         ],
-        input_output_aliases={len(tables) + len(operands) + i: i for i in range(len(targets))},
+        input_output_aliases={
+            len(tables) + len(operands) + i: slot for i, slot in enumerate(slots)
+        },
         compiler_params=params(),
-        cost_estimate=FILLER,
+        cost_estimate=cost(weight),
         name="place",
-    )(*tables, *operands, *targets)
+    )(*tables, *operands, *earlier)
     return targets, other
 
 
@@ -450,7 +483,7 @@
         scratch_shapes=[pltpu.SemaphoreType.DMA((2 * len(others),))],
         input_output_aliases={1 + len(others) + i: i for i in range(2)},
         compiler_params=params(),
-        cost_estimate=FILLER,
+        cost_estimate=cost(TAIL_COST),
         name="finish",
     )(near, *others, *targets)
 
@@ -634,24 +667,37 @@
     own, *sent = split_heads(
         near, key_rows[0], key_gain, [sum(group) for group in groups], (value_rows[0],)
     )
-    chunks = []
-    queries = None
-    for array, group in zip(sent, groups):
-        other = exchange(after(array, *chunks[-1:]), 1)
-        base = bases[len(chunks)]
-        chunks += join_halves(own, base, other, group)
-        if queries is None:
-            own_queries, sent_queries = split_heads(
-                near, after(query_rows[0], *chunks), query_gain, [sum(CHUNKS)]
-            )
-            queries = [own_queries, exchange(sent_queries, 1)]
-    sources = [far_blocks(chunk) for chunk in chunks]
-
-    attended, homes, received, others, heads = {}, {}, {}, {}, {}
+    chunks, sources = [], {}
+
+    def join_group(index, *earlier):
+        other = exchange(after(sent[index], *chunks[:1]), 1)
+        chunks.extend(
+            join_halves(own, bases[len(chunks)], after(other, *earlier), groups[index])
+        )
+
+    join_group(0)
+    sources[0] = far_blocks(chunks[0])
+    own_queries, *sent_queries = split_heads(
+        near, after(query_rows[0], chunks[0]), query_gain, [CHUNKS[0], sum(CHUNKS[1:])]
+    )
+    first_queries, later_queries = [exchange(array, 1) for array in sent_queries]
+    join_group(1, own_queries)
+    sources[1] = far_blocks(chunks[1])
+
+    attended, homes, received, others = {}, {}, {}, {}
     targets = ()
 
+    def shift_around(arrays, *earlier):
+        return [
+            shift(after(array, *earlier), distance) for distance, array in enumerate(arrays, 1)
+        ]
+
+    early = count - LATE_CHUNKS
+    early_heads = sum(CHUNKS[:early])
+
     def place_chunk(chunk, *earlier):
-        return place(
+        late = chunk >= early
+        targets_now, others[late] = place(
             tables,
             after(homes[chunk], *earlier),
             received[chunk],
@@ -659,41 +705,71 @@
             features,
             windows,
             targets,
+            others.get(late),
+            bases[chunk] - early_heads if late else bases[chunk],
+            sum(CHUNKS) - early_heads if late else early_heads,
+            TAIL_COST if chunk >= count - FREE else PLACE_COST,
         )
-
-    for chunk in range(count + 1):
-        tasks = []
+        return targets_now
+
+    arrived, waiting = {}, {}
+
+    def attend(chunk, *earlier):
+        queries = (after(own_queries, *earlier), bases[chunk]), (
+            (later_queries, bases[chunk] - bases[1]) if chunk else (first_queries, 0)
+        )
+        (((attended[chunk],),), (left,)) = run_stage(
+            tables, [attention_task(queries, sources[chunk])], STAGE_COST
+        )
+        return left
+
+    def mix(chunk, *earlier):
+        ready = after(arrived[chunk], *earlier)
+        (((homes[chunk], *waiting[chunk]),), (left,)) = run_stage(
+            tables, [blend_task(attended[chunk], ready, 0, windows)], BLEND_COST
+        )
+        received[chunk] = [shift(left, -1)]
+
+    def send_around(chunk, *earlier):
+        received[chunk] = [
+            shift(after(array, *earlier), distance)
+            for distance, array in enumerate(waiting[chunk], 1)
+        ] + received[chunk]
+
+    swapped = SWAP if count > 3 else 0
+    for chunk in range(count - swapped):
+        left = attend(chunk, homes[chunk - 1] if chunk else chunks[1])
+        gate = received[chunk - 1] if chunk else []
+        arrived[chunk] = shift(after(left, *gate), -1)
         if chunk >= 1:
-            tasks.append(blend_task(attended[chunk - 1], *heads[chunk - 1], windows))
-        if chunk < count:
-            tasks.append(attention_task(queries, sources[chunk], bases[chunk]))
-        merged = chunk < count - 1 or len(tasks) == 1
-        results, lefts = run_stage(tables, tasks, merged)
-        gate = received[chunk - 2] if chunk >= 2 else ()
-        lefts = [shift(after(left, *gate), -1) for left in reversed(lefts)]
-        if chunk >= 1:
-            homes[chunk - 1], *sent = results.pop(0)
-            received[chunk - 1] = [
-                shift(array, distance) for distance, array in enumerate(sent, 1)
-            ] + lefts[-1:]
-        if chunk < count:
-            ((attended[chunk],),) = results
+            send_around(chunk - 1, attended[chunk])
         if chunk >= 2:
-            targets, others[chunk - 2] = place_chunk(
-                chunk - 2, attended[chunk] if chunk < count else homes[chunk - 1]
-            )
-        if chunk < count:
-            left = lefts[0]
-            if 2 <= chunk:
-                left = after(left, targets[0])
-            heads[chunk] = (left, CHUNKS[chunk - 1] if merged and chunk >= 1 else 0)
-    early = range(count - 2)
-    arrived = [exchange(after(others[i], homes[count - 1]), 1) for i in early]
-    targets = finish(near, arrived, [bases[i] for i in early], head_size, targets)
-    targets, others[count - 1] = place_chunk(count - 1)
-    late = range(count - 2, count)
-    arrived = [exchange(others[i], 1) for i in late]
-    owned, next_rows = finish(near, arrived, [bases[i] for i in late], head_size, targets)
+            targets = place_chunk(chunk - 2, attended[chunk])
+        if chunk == count - 1 - swapped and swapped:
+            break
+        mix(chunk, *targets[:1])
+        if chunk == 0:
+            join_group(2, homes[0])
+            for later in range(2, count):
+                sources[later] = far_blocks(chunks[later])
+    if swapped:
+        left = attend(count - 1, attended[count - 2], targets[0])
+        arrived[count - 1] = shift(left, -1)
+        mix(count - 2, attended[count - 1])
+        send_around(count - 2)
+        targets = place_chunk(count - 3, homes[count - 2])
+        mix(count - 1, homes[count - 2])
+    send_around(count - 1)
+    targets = place_chunk(count - 2, homes[count - 1])
+    if LATE_CHUNKS > 1:
+        arrived = exchange(after(others[False], homes[count - 1]), 1)
+    else:
+        arrived = exchange(others[False], 1)
+    targets = finish(near, [arrived], [0], head_size, targets)
+    targets = place_chunk(count - 1)
+    owned, next_rows = finish(
+        near, [exchange(others[True], 1)], [early_heads], head_size, targets
+    )
     return (owned, next_rows[None])
 
 

time: 190 us -> 174 us (0.916)
  waiting for transfers between devices: 54 us -> 31.1 us
  starting transfers between devices: 45.9 us -> 60.2 us
  Pallas kernels: 88 us -> 81 us
    ppermute x20 -> x24, waiting for transfers between devices: 38 us -> 21.4 us  [shift(): lax.ppermute(array, 'win', [(i, (i + step) % count) for i in range(count)])]
    ppermute x20 -> x24, starting transfers between devices: 34.8 us -> 49.7 us  [shift(): lax.ppermute(array, 'win', [(i, (i + step) % count) for i in range(count)])]
    ppermute x16 -> x13, waiting for transfers between devices: 16 us -> 9.69 us  [exchange(): lax.ppermute(array, 'uly', [(i, i ^ bit) for i in range(lax.axis_size('ul...]
    pallas_call x6, Pallas kernels: 17.2 us -> 13.5 us  [place(): pl.pallas_call(kernel, grid=(1,), in_specs=[SMEM for _ in tables] + [firs...]
    pallas_call x2, Pallas kernels: 11.6 us -> 8.88 us  [split_heads(): pl.pallas_call(kernel, grid=(frames // frames_per_step,), in_specs=[SMEM,...]
    pallas_call x7 -> x12, Pallas kernels: 44.4 us -> 43.7 us  [run_stage(): pl.pallas_call(kernel, grid=(steps,), in_specs=[SMEM for _ in tables] + [...]
    ppermute x16 -> x13, starting transfers between devices: 11 us -> 10.4 us  [exchange(): lax.ppermute(array, 'uly', [(i, i ^ bit) for i in range(lax.axis_size('ul...]
  transfers between devices with their start and end apart: 36 -> 37, of which waited for: 12 -> 14; matrix products, arithmetic and copies ran while one was open for 0% -> 0% of each run, Pallas kernels for 40% -> 39%
where the time goes in v3:
time: 174 us; the launch traced here: 173 us
  Pallas kernels  81 us (47%)
  starting transfers between devices  60.2 us (35%)
  waiting for transfers between devices  31.1 us (18%)
    ppermute x24, starting transfers between devices, shift(): lax.ppermute(array, 'win', [(i, (i + step) % count) for i in range(count)])  49.7 us
    pallas_call x12, Pallas kernels, run_stage(): pl.pallas_call(kernel, grid=(steps,), in_specs=[SMEM for _ in tables] + [...  43.7 us
    ppermute x24, waiting for transfers between devices, shift(): lax.ppermute(array, 'win', [(i, (i + step) % count) for i in range(count)])  21.4 us
    pallas_call x6, Pallas kernels, place(): pl.pallas_call(kernel, grid=(1,), in_specs=[SMEM for _ in tables] + [firs...  13.5 us
    ppermute x13, starting transfers between devices, exchange(): lax.ppermute(array, 'uly', [(i, i ^ bit) for i in range(lax.axis_size('ul...  10.4 us
    pallas_call x3, Pallas kernels, join_halves(): pl.pallas_call(kernel, grid=(sum(counts) // STEP_HEADS,), in_specs=[pl.Bl...  10.4 us
    ppermute x13, waiting for transfers between devices, exchange(): lax.ppermute(array, 'uly', [(i, i ^ bit) for i in range(lax.axis_size('ul...  9.69 us
    pallas_call x2, Pallas kernels, split_heads(): pl.pallas_call(kernel, grid=(frames // frames_per_step,), in_specs=[SMEM,...  8.88 us
  transfers between devices with their start and end apart: 37, of which 14 were waited for; matrix products, arithmetic and copies ran while one was open for 0% of the time, Pallas kernels for 39%

profile of v3, /device:TPU:0, one launch (start us, length us, event | category | flops | bytes accessed | tf_op | source)
XLA Modules:
  0.0 173.2 jit_solution(7583501759302522434)
XLA Ops:
  0.6 5.2 %norm_split.2 = (bf16[20,2,16,16,128]{4,3,2,1,0:T(8,128)(2,1)}, bf16[2,2,16,16,128]{4,3,2,1,0:T(8,128)(2,1)}, bf16[4,2,16,16,128]{4,3,2,1,0:T(8,128)(2,1)}, bf16[14,2,16,16,128]{4,3,2,1,0:T(8,128)(2,1)}) custom-call(s32[1]{0:T(128)} %bitcast.near_ref.refs_4_, bf16[16,16,5120]{2,1,0:T(8,128)(2,1)} %bitcast.9, f32[1,1,5120]{2,1,0:T(1,128)} %bitcast.12, ...), custom_call_target="tpu_custom_call" | custom-call | flops 10005000192 | tf_op jit(solution)/shard_map/norm_split/pallas_call | solution.py:95
  6.3 1.5 collective-permute-done.other_ref
  7.8 1.9 %join_halves.3.refs_7_ = bf16[2,2,2,16,16,128]{5,4,3,2,1,0:T(8,128)(2,1)} custom-call(bf16[20,2,16,16,128]{4,3,2,1,0:T(8,128)(2,1)} %get-tuple-element.103.own_ref, bf16[2,2,16,16,128]{4,3,2,1,0:T(8,128)(2,1)} %collective-permute-done.other_ref), custom_call_target="tpu_custom_call" | custom-call | flops 10005000192 | tf_op jit(solution)/shard_map/join_halves/pallas_call | solution.py:130
  9.7 2.9 %collective-permute-start.3 = (bf16[2,2,2,16,16,128]{5,4,3,2,1,0:T(8,128)(2,1)}, bf16[2,2,2,16,16,128]{5,4,3,2,1,0:T(8,128)(2,1)}, u32[]{:S(2)}, u32[]{:S(2)}) collective-permute-start(bf16[2,2,2,16,16,128]{5,4,3,2,1,0:T(8,128)(2,1)} %join_halves.3.refs_7_), channel_id=1, source_target_pairs={{0,2},{1,3},{2,0},{3,1},{4,6},{5,7},{6,4},{7,5},{8,10},{9,11},{10,... | collective-permute-start | bytes 1572872 | tf_op jit(solution)/shard_map/ppermute | solution.py:492
  13.0 3.7 %norm_split.3 = (bf16[20,16,16,128]{3,2,1,0:T(8,128)(2,1)}, bf16[2,16,16,128]{3,2,1,0:T(8,128)(2,1)}, bf16[18,16,16,128]{3,2,1,0:T(8,128)(2,1)}) custom-call(s32[1]{0:T(128)} %bitcast.near_ref.refs_4_, bf16[16,16,5120]{2,1,0:T(8,128)(2,1)} %bitcast.11, f32[1,1,5120]{2,1,0:T(1,128)} %bitcast.13), custom_call_target="tpu_custom_call" | custom-call | flops 10005000192 | tf_op jit(solution)/shard_map/norm_split/pallas_call | solution.py:95
  16.7 2.2 %join_halves.4.refs_7_ = bf16[4,2,2,16,16,128]{5,4,3,2,1,0:T(8,128)(2,1)} custom-call(bf16[20,2,16,16,128]{4,3,2,1,0:T(8,128)(2,1)} %get-tuple-element.103.own_ref, bf16[4,2,16,16,128]{4,3,2,1,0:T(8,128)(2,1)} %collective-permute-done.1.other_ref), custom_call_target="tpu_custom_call" | custom-call | flops 10005000192 | tf_op jit(solution)/shard_map/join_halves/pallas_call | solution.py:130
  20.7 4.8 %collective-permute-done.3.refs_8_ = bf16[2,2,2,16,16,128]{5,4,3,2,1,0:T(8,128)(2,1)} collective-permute-done((bf16[2,2,2,16,16,128]{5,4,3,2,1,0:T(8,128)(2,1)}, bf16[2,2,2,16,16,128]{5,4,3,2,1,0:T(8,128)(2,1)}, u32[]{:S(2)}, u32[]{:S(2)}) %collective-permute-start.3) | collective-permute-done | bytes 524320 | tf_op jit(solution)/shard_map/ppermute | solution.py:492
  25.5 3.9 %stage.12 = (bf16[2,2,16,16,128]{4,3,2,1,0:T(8,128)(2,1)}, bf16[2,2,8,16,128]{4,3,2,1,0:T(8,128)(2,1)}) custom-call(s32[1]{0:T(128)} %bitcast.1.refs_0_, s32[4]{0:T(128)} %refs_1_.35, s32[4]{0:T(128)} %refs_2_.35, s32[4,16]{1,0:T(4,128)} %refs_3_.35, s32[1]{0:T(128)} %bitcast.near_ref.refs_4_, bf16[20,16,16,128]{3,2,1,0:T(8,128)(2,1)} %get-tuple-element.166.refs_5_, ...), custom_call_target="tpu_custom_call" | custom-call | tf_op jit(solution)/shard_map/stage/pallas_call | solution.py:375
  29.4 4.2 %collective-permute-start.4 = (bf16[2,2,8,16,128]{4,3,2,1,0:T(8,128)(2,1)}, bf16[2,2,8,16,128]{4,3,2,1,0:T(8,128)(2,1)}, u32[]{:S(2)}, u32[]{:S(2)}) collective-permute-start(bf16[2,2,8,16,128]{4,3,2,1,0:T(8,128)(2,1)} %get-tuple-element.113), channel_id=1, source_target_pairs={{0,12},{4,0},{8,4},{12,8},{1,13},{5,1},{9,5},{13,9},{2,14},{6,2},{... | collective-permute-start | bytes 393224 | tf_op jit(solution)/shard_map/ppermute | solution.py:497
  33.6 2.8 %collective-permute-done.4.refs_6_ = bf16[2,2,8,16,128]{4,3,2,1,0:T(8,128)(2,1)} collective-permute-done((bf16[2,2,8,16,128]{4,3,2,1,0:T(8,128)(2,1)}, bf16[2,2,8,16,128]{4,3,2,1,0:T(8,128)(2,1)}, u32[]{:S(2)}, u32[]{:S(2)}) %collective-permute-start.4) | collective-permute-done | bytes 131104 | tf_op jit(solution)/shard_map/ppermute | solution.py:497
  36.4 1.9 %stage.13 = (bf16[2,2,12,16,128]{4,3,2,1,0:T(8,128)(2,1)}, bf16[2,2,5,16,128]{4,3,2,1,0:T(8,128)(2,1)}, bf16[2,2,3,16,128]{4,3,2,1,0:T(8,128)(2,1)}, bf16[2,2,8,16,128]{4,3,2,1,0:T(8,128)(2,1)}) custom-call(s32[1]{0:T(128)} %bitcast.1.refs_0_, s32[4]{0:T(128)} %refs_1_.35, s32[4]{0:T(128)} %refs_2_.35, s32[4,16]{1,0:T(4,128)} %refs_3_.35, ...), custom_call_target="tpu_custom_call" | custom-call | tf_op jit(solution)/shard_map/stage/pallas_call | solution.py:375
  38.3 6.4 %join_halves.5 = (bf16[4,2,2,16,16,128]{5,4,3,2,1,0:T(8,128)(2,1)}, bf16[4,2,2,16,16,128]{5,4,3,2,1,0:T(8,128)(2,1)}, bf16[4,2,2,16,16,128]{5,4,3,2,1,0:T(8,128)(2,1)}, bf16[2,2,2,16,16,128]{5,4,3,2,1,0:T(8,128)(2,1)}) custom-call(bf16[20,2,16,16,128]{4,3,2,1,0:T(8,128)(2,1)} %get-tuple-element.103.own_ref, ...), custom_call_target="tpu_custom_call" | custom-call | tf_op jit(solution)/shard_map/join_halves/pallas_call | solution.py:130
  46.2 4.2 %collective-permute-start.7 = (bf16[2,2,8,16,128]{4,3,2,1,0:T(8,128)(2,1)}, bf16[2,2,8,16,128]{4,3,2,1,0:T(8,128)(2,1)}, u32[]{:S(2)}, u32[]{:S(2)}) collective-permute-start(bf16[2,2,8,16,128]{4,3,2,1,0:T(8,128)(2,1)} %get-tuple-element.119), channel_id=1, source_target_pairs={{0,12},{4,0},{8,4},{12,8},{1,13},{5,1},{9,5},{13,9},{2,14},{6,2},{... | collective-permute-start | bytes 393224 | tf_op jit(solution)/shard_map/ppermute | solution.py:497
  50.4 5.9 %stage.14 = (bf16[4,2,16,16,128]{4,3,2,1,0:T(8,128)(2,1)}, bf16[4,2,8,16,128]{4,3,2,1,0:T(8,128)(2,1)}) custom-call(s32[1]{0:T(128)} %bitcast.1.refs_0_, s32[4]{0:T(128)} %refs_1_.35, s32[4]{0:T(128)} %refs_2_.35, s32[4,16]{1,0:T(4,128)} %refs_3_.35, s32[1]{0:T(128)} %bitcast.near_ref.refs_4_, bf16[20,16,16,128]{3,2,1,0:T(8,128)(2,1)} %get-tuple-element.166.refs_5_, ...), custom_call_target="tpu_custom_call" | custom-call | tf_op jit(solution)/shard_map/stage/pallas_call | solution.py:375
  56.3 1.8 %collective-permute-start.8 = (bf16[4,2,8,16,128]{4,3,2,1,0:T(8,128)(2,1)}, bf16[4,2,8,16,128]{4,3,2,1,0:T(8,128)(2,1)}, u32[]{:S(2)}, u32[]{:S(2)}) collective-permute-start(bf16[4,2,8,16,128]{4,3,2,1,0:T(8,128)(2,1)} %get-tuple-element.120), channel_id=1, source_target_pairs={{0,12},{4,0},{8,4},{12,8},{1,13},{5,1},{9,5},{13,9},{2,14},{6,2},{... | collective-permute-start | bytes 786440 | tf_op jit(solution)/shard_map/ppermute | solution.py:497
  58.1 5.0 %collective-permute-done.8.refs_6_ = bf16[4,2,8,16,128]{4,3,2,1,0:T(8,128)(2,1)} collective-permute-done((bf16[4,2,8,16,128]{4,3,2,1,0:T(8,128)(2,1)}, bf16[4,2,8,16,128]{4,3,2,1,0:T(8,128)(2,1)}, u32[]{:S(2)}, u32[]{:S(2)}) %collective-permute-start.8) | collective-permute-done | bytes 262176 | tf_op jit(solution)/shard_map/ppermute | solution.py:497
  63.1 2.1 %stage.15 = (bf16[4,2,12,16,128]{4,3,2,1,0:T(8,128)(2,1)}, bf16[4,2,5,16,128]{4,3,2,1,0:T(8,128)(2,1)}, bf16[4,2,3,16,128]{4,3,2,1,0:T(8,128)(2,1)}, bf16[4,2,8,16,128]{4,3,2,1,0:T(8,128)(2,1)}) custom-call(s32[1]{0:T(128)} %bitcast.1.refs_0_, s32[4]{0:T(128)} %refs_1_.35, s32[4]{0:T(128)} %refs_2_.35, s32[4,16]{1,0:T(4,128)} %refs_3_.35, ...), custom_call_target="tpu_custom_call" | custom-call | tf_op jit(solution)/shard_map/stage/pallas_call | solution.py:375
  65.2 3.9 %collective-permute-start.11 = (bf16[4,2,8,16,128]{4,3,2,1,0:T(8,128)(2,1)}, bf16[4,2,8,16,128]{4,3,2,1,0:T(8,128)(2,1)}, u32[]{:S(2)}, u32[]{:S(2)}) collective-permute-start(bf16[4,2,8,16,128]{4,3,2,1,0:T(8,128)(2,1)} %get-tuple-element.129), channel_id=1, source_target_pairs={{0,12},{4,0},{8,4},{12,8},{1,13},{5,1},{9,5},{13,9},{2,14},{6,2},{... | collective-permute-start | bytes 786440 | tf_op jit(solution)/shard_map/ppermute | solution.py:497
  71.2 5.9 %stage.16 = (bf16[4,2,16,16,128]{4,3,2,1,0:T(8,128)(2,1)}, bf16[4,2,8,16,128]{4,3,2,1,0:T(8,128)(2,1)}) custom-call(s32[1]{0:T(128)} %bitcast.1.refs_0_, s32[4]{0:T(128)} %refs_1_.35, s32[4]{0:T(128)} %refs_2_.35, s32[4,16]{1,0:T(4,128)} %refs_3_.35, s32[1]{0:T(128)} %bitcast.near_ref.refs_4_, bf16[20,16,16,128]{3,2,1,0:T(8,128)(2,1)} %get-tuple-element.166.refs_5_, ...), custom_call_target="tpu_custom_call" | custom-call | tf_op jit(solution)/shard_map/stage/pallas_call | solution.py:375
  77.1 4.1 %collective-permute-start.12 = (bf16[4,2,8,16,128]{4,3,2,1,0:T(8,128)(2,1)}, bf16[4,2,8,16,128]{4,3,2,1,0:T(8,128)(2,1)}, u32[]{:S(2)}, u32[]{:S(2)}) collective-permute-start(bf16[4,2,8,16,128]{4,3,2,1,0:T(8,128)(2,1)} %get-tuple-element.130), channel_id=1, source_target_pairs={{0,12},{4,0},{8,4},{12,8},{1,13},{5,1},{9,5},{13,9},{2,14},{6,2},{... | collective-permute-start | bytes 786440 | tf_op jit(solution)/shard_map/ppermute | solution.py:497
  81.3 2.0 %place.6 = (bf16[12,16,5120]{2,1,0:T(8,128)(2,1)}, bf16[16,16,5120]{2,1,0:T(8,128)(2,1)}, bf16[28,16,2304]{2,1,0:T(8,128)(2,1)}) custom-call(s32[1]{0:T(128)} %bitcast.1.refs_0_, s32[4]{0:T(128)} %refs_1_.35, s32[4]{0:T(128)} %refs_2_.35, s32[4,16]{1,0:T(4,128)} %refs_3_.35, s32[1]{0:T(128)} %bitcast.near_ref.refs_4_, ...), custom_call_target="tpu_custom_call" | custom-call | flops 6899999744 | tf_op jit(solution)/shard_map/place/pallas_call | solution.py:426
  83.3 2.3 %collective-permute-done.12.refs_6_ = bf16[4,2,8,16,128]{4,3,2,1,0:T(8,128)(2,1)} collective-permute-done((bf16[4,2,8,16,128]{4,3,2,1,0:T(8,128)(2,1)}, bf16[4,2,8,16,128]{4,3,2,1,0:T(8,128)(2,1)}, u32[]{:S(2)}, u32[]{:S(2)}) %collective-permute-start.12) | collective-permute-done | bytes 262176 | tf_op jit(solution)/shard_map/ppermute | solution.py:497
  85.6 2.1 %stage.17 = (bf16[4,2,12,16,128]{4,3,2,1,0:T(8,128)(2,1)}, bf16[4,2,5,16,128]{4,3,2,1,0:T(8,128)(2,1)}, bf16[4,2,3,16,128]{4,3,2,1,0:T(8,128)(2,1)}, bf16[4,2,8,16,128]{4,3,2,1,0:T(8,128)(2,1)}) custom-call(s32[1]{0:T(128)} %bitcast.1.refs_0_, s32[4]{0:T(128)} %refs_1_.35, s32[4]{0:T(128)} %refs_2_.35, s32[4,16]{1,0:T(4,128)} %refs_3_.35, ...), custom_call_target="tpu_custom_call" | custom-call | tf_op jit(solution)/shard_map/stage/pallas_call | solution.py:375
  87.7 4.2 %collective-permute-start.16 = (bf16[4,2,8,16,128]{4,3,2,1,0:T(8,128)(2,1)}, bf16[4,2,8,16,128]{4,3,2,1,0:T(8,128)(2,1)}, u32[]{:S(2)}, u32[]{:S(2)}) collective-permute-start(bf16[4,2,8,16,128]{4,3,2,1,0:T(8,128)(2,1)} %get-tuple-element.143), channel_id=1, source_target_pairs={{0,12},{4,0},{8,4},{12,8},{1,13},{5,1},{9,5},{13,9},{2,14},{6,2},{... | collective-permute-start | bytes 786440 | tf_op jit(solution)/shard_map/ppermute | solution.py:497
  94.3 5.9 %stage.18 = (bf16[4,2,16,16,128]{4,3,2,1,0:T(8,128)(2,1)}, bf16[4,2,8,16,128]{4,3,2,1,0:T(8,128)(2,1)}) custom-call(s32[1]{0:T(128)} %bitcast.1.refs_0_, s32[4]{0:T(128)} %refs_1_.35, s32[4]{0:T(128)} %refs_2_.35, s32[4,16]{1,0:T(4,128)} %refs_3_.35, s32[1]{0:T(128)} %bitcast.near_ref.refs_4_, bf16[20,16,16,128]{3,2,1,0:T(8,128)(2,1)} %get-tuple-element.166.refs_5_, ...), custom_call_target="tpu_custom_call" | custom-call | tf_op jit(solution)/shard_map/stage/pallas_call | solution.py:375
  100.2 3.8 %collective-permute-start.17 = (bf16[4,2,8,16,128]{4,3,2,1,0:T(8,128)(2,1)}, bf16[4,2,8,16,128]{4,3,2,1,0:T(8,128)(2,1)}, u32[]{:S(2)}, u32[]{:S(2)}) collective-permute-start(bf16[4,2,8,16,128]{4,3,2,1,0:T(8,128)(2,1)} %get-tuple-element.144), channel_id=1, source_target_pairs={{0,12},{4,0},{8,4},{12,8},{1,13},{5,1},{9,5},{13,9},{2,14},{6,2},{... | collective-permute-start | bytes 786440 | tf_op jit(solution)/shard_map/ppermute | solution.py:497
  103.9 2.4 %place.7 = (bf16[12,16,5120]{2,1,0:T(8,128)(2,1)}, bf16[16,16,5120]{2,1,0:T(8,128)(2,1)}, bf16[28,16,2304]{2,1,0:T(8,128)(2,1)}) custom-call(s32[1]{0:T(128)} %bitcast.1.refs_0_, s32[4]{0:T(128)} %refs_1_.35, s32[4]{0:T(128)} %refs_2_.35, s32[4,16]{1,0:T(4,128)} %refs_3_.35, ...), custom_call_target="tpu_custom_call", output_to_operand_aliasing={{0}: (9, {}), {1}: (10, {}), {2}: (11, {})} | custom-call | flops 6899999744 | tf_op jit(solution)/shard_map/place/pallas_call | solution.py:426
  106.3 2.4 %collective-permute-done.17.refs_6_ = bf16[4,2,8,16,128]{4,3,2,1,0:T(8,128)(2,1)} collective-permute-done((bf16[4,2,8,16,128]{4,3,2,1,0:T(8,128)(2,1)}, bf16[4,2,8,16,128]{4,3,2,1,0:T(8,128)(2,1)}, u32[]{:S(2)}, u32[]{:S(2)}) %collective-permute-start.17) | collective-permute-done | bytes 262176 | tf_op jit(solution)/shard_map/ppermute | solution.py:497
  108.7 2.1 %stage.19 = (bf16[4,2,12,16,128]{4,3,2,1,0:T(8,128)(2,1)}, bf16[4,2,5,16,128]{4,3,2,1,0:T(8,128)(2,1)}, bf16[4,2,3,16,128]{4,3,2,1,0:T(8,128)(2,1)}, bf16[4,2,8,16,128]{4,3,2,1,0:T(8,128)(2,1)}) custom-call(s32[1]{0:T(128)} %bitcast.1.refs_0_, s32[4]{0:T(128)} %refs_1_.35, s32[4]{0:T(128)} %refs_2_.35, s32[4,16]{1,0:T(4,128)} %refs_3_.35, ...), custom_call_target="tpu_custom_call" | custom-call | tf_op jit(solution)/shard_map/stage/pallas_call | solution.py:375
  110.8 3.8 %collective-permute-start.25 = (bf16[4,2,8,16,128]{4,3,2,1,0:T(8,128)(2,1)}, bf16[4,2,8,16,128]{4,3,2,1,0:T(8,128)(2,1)}, u32[]{:S(2)}, u32[]{:S(2)}) collective-permute-start(bf16[4,2,8,16,128]{4,3,2,1,0:T(8,128)(2,1)} %get-tuple-element.171), channel_id=1, source_target_pairs={{0,12},{4,0},{8,4},{12,8},{1,13},{5,1},{9,5},{13,9},{2,14},{6,2},{... | collective-permute-start | bytes 786440 | tf_op jit(solution)/shard_map/ppermute | solution.py:497
  116.7 5.9 %stage.20 = (bf16[4,2,16,16,128]{4,3,2,1,0:T(8,128)(2,1)}, bf16[4,2,8,16,128]{4,3,2,1,0:T(8,128)(2,1)}) custom-call(s32[1]{0:T(128)} %bitcast.1.refs_0_, s32[4]{0:T(128)} %refs_1_.35, s32[4]{0:T(128)} %refs_2_.35, s32[4,16]{1,0:T(4,128)} %refs_3_.35, s32[1]{0:T(128)} %bitcast.near_ref.refs_4_, bf16[20,16,16,128]{3,2,1,0:T(8,128)(2,1)} %get-tuple-element.166.refs_5_, ...), custom_call_target="tpu_custom_call" | custom-call | tf_op jit(solution)/shard_map/stage/pallas_call | solution.py:375
  122.6 3.8 %collective-permute-start.33 = (bf16[4,2,5,16,128]{4,3,2,1,0:T(8,128)(2,1)}, bf16[4,2,5,16,128]{4,3,2,1,0:T(8,128)(2,1)}, u32[]{:S(2)}, u32[]{:S(2)}) collective-permute-start(bf16[4,2,5,16,128]{4,3,2,1,0:T(8,128)(2,1)} %get-tuple-element.186), channel_id=1, source_target_pairs={{0,4},{4,8},{8,12},{12,0},{1,5},{5,9},{9,13},{13,1},{2,6},{6,10},{... | collective-permute-start | bytes 491528 | tf_op jit(solution)/shard_map/ppermute | solution.py:497
  128.9 2.4 %place.8 = (bf16[12,16,5120]{2,1,0:T(8,128)(2,1)}, bf16[16,16,5120]{2,1,0:T(8,128)(2,1)}, bf16[28,16,2304]{2,1,0:T(8,128)(2,1)}) custom-call(s32[1]{0:T(128)} %bitcast.1.refs_0_, s32[4]{0:T(128)} %refs_1_.35, s32[4]{0:T(128)} %refs_2_.35, s32[4,16]{1,0:T(4,128)} %refs_3_.35, ...), custom_call_target="tpu_custom_call", output_to_operand_aliasing={{0}: (9, {}), {1}: (10, {}), {2}: (11, {})} | custom-call | flops 6899999744 | tf_op jit(solution)/shard_map/place/pallas_call | solution.py:426
  131.2 3.9 %stage.21 = (bf16[2,2,16,16,128]{4,3,2,1,0:T(8,128)(2,1)}, bf16[2,2,8,16,128]{4,3,2,1,0:T(8,128)(2,1)}) custom-call(s32[1]{0:T(128)} %bitcast.1.refs_0_, s32[4]{0:T(128)} %refs_1_.35, s32[4]{0:T(128)} %refs_2_.35, s32[4,16]{1,0:T(4,128)} %refs_3_.35, s32[1]{0:T(128)} %bitcast.near_ref.refs_4_, bf16[20,16,16,128]{3,2,1,0:T(8,128)(2,1)} %get-tuple-element.166.refs_5_, ...), custom_call_target="tpu_custom_call" | custom-call | tf_op jit(solution)/shard_map/stage/pallas_call | solution.py:375
  135.2 1.9 %collective-permute-start.24 = (bf16[2,2,8,16,128]{4,3,2,1,0:T(8,128)(2,1)}, bf16[2,2,8,16,128]{4,3,2,1,0:T(8,128)(2,1)}, u32[]{:S(2)}, u32[]{:S(2)}) collective-permute-start(bf16[2,2,8,16,128]{4,3,2,1,0:T(8,128)(2,1)} %get-tuple-element.169), channel_id=1, source_target_pairs={{0,12},{4,0},{8,4},{12,8},{1,13},{5,1},{9,5},{13,9},{2,14},{6,2},{... | collective-permute-start | bytes 393224 | tf_op jit(solution)/shard_map/ppermute | solution.py:497
  137.7 2.1 %stage.22 = (bf16[4,2,12,16,128]{4,3,2,1,0:T(8,128)(2,1)}, bf16[4,2,5,16,128]{4,3,2,1,0:T(8,128)(2,1)}, bf16[4,2,3,16,128]{4,3,2,1,0:T(8,128)(2,1)}, bf16[4,2,8,16,128]{4,3,2,1,0:T(8,128)(2,1)}) custom-call(s32[1]{0:T(128)} %bitcast.1.refs_0_, s32[4]{0:T(128)} %refs_1_.35, s32[4]{0:T(128)} %refs_2_.35, s32[4,16]{1,0:T(4,128)} %refs_3_.35, ...), custom_call_target="tpu_custom_call" | custom-call | tf_op jit(solution)/shard_map/stage/pallas_call | solution.py:375
  139.9 2.8 %collective-permute-start.30 = (bf16[4,2,5,16,128]{4,3,2,1,0:T(8,128)(2,1)}, bf16[4,2,5,16,128]{4,3,2,1,0:T(8,128)(2,1)}, u32[]{:S(2)}, u32[]{:S(2)}) collective-permute-start(bf16[4,2,5,16,128]{4,3,2,1,0:T(8,128)(2,1)} %get-tuple-element.181), channel_id=1, source_target_pairs={{0,4},{4,8},{8,12},{12,0},{1,5},{5,9},{9,13},{13,1},{2,6},{6,10},{... | collective-permute-start | bytes 491528 | tf_op jit(solution)/shard_map/ppermute | solution.py:497
  142.6 2.4 %collective-permute-start.32 = (bf16[4,2,8,16,128]{4,3,2,1,0:T(8,128)(2,1)}, bf16[4,2,8,16,128]{4,3,2,1,0:T(8,128)(2,1)}, u32[]{:S(2)}, u32[]{:S(2)}) collective-permute-start(bf16[4,2,8,16,128]{4,3,2,1,0:T(8,128)(2,1)} %get-tuple-element.183), channel_id=1, source_target_pairs={{0,12},{4,0},{8,4},{12,8},{1,13},{5,1},{9,5},{13,9},{2,14},{6,2},{... | collective-permute-start | bytes 786440 | tf_op jit(solution)/shard_map/ppermute | solution.py:497
  145.1 2.4 %place.9 = (bf16[12,16,5120]{2,1,0:T(8,128)(2,1)}, bf16[16,16,5120]{2,1,0:T(8,128)(2,1)}, bf16[28,16,2304]{2,1,0:T(8,128)(2,1)}) custom-call(s32[1]{0:T(128)} %bitcast.1.refs_0_, s32[4]{0:T(128)} %refs_1_.35, s32[4]{0:T(128)} %refs_2_.35, s32[4,16]{1,0:T(4,128)} %refs_3_.35, ...), custom_call_target="tpu_custom_call", output_to_operand_aliasing={{0}: (9, {}), {1}: (10, {}), {2}: (11, {})} | custom-call | flops 6899999744 | tf_op jit(solution)/shard_map/place/pallas_call | solution.py:426
  147.5 1.9 %stage.23 = (bf16[2,2,12,16,128]{4,3,2,1,0:T(8,128)(2,1)}, bf16[2,2,5,16,128]{4,3,2,1,0:T(8,128)(2,1)}, bf16[2,2,3,16,128]{4,3,2,1,0:T(8,128)(2,1)}, bf16[2,2,8,16,128]{4,3,2,1,0:T(8,128)(2,1)}) custom-call(s32[1]{0:T(128)} %bitcast.1.refs_0_, s32[4]{0:T(128)} %refs_1_.35, s32[4]{0:T(128)} %refs_2_.35, s32[4,16]{1,0:T(4,128)} %refs_3_.35, ...), custom_call_target="tpu_custom_call" | custom-call | tf_op jit(solution)/shard_map/stage/pallas_call | solution.py:375
  149.3 1.8 %collective-permute-done.31.refs_7_ = bf16[4,2,3,16,128]{4,3,2,1,0:T(8,128)(2,1)} collective-permute-done((bf16[4,2,3,16,128]{4,3,2,1,0:T(8,128)(2,1)}, bf16[4,2,3,16,128]{4,3,2,1,0:T(8,128)(2,1)}, u32[]{:S(2)}, u32[]{:S(2)}) %collective-permute-start.31) | collective-permute-done | bytes 98336 | tf_op jit(solution)/shard_map/ppermute | solution.py:497
  151.7 2.4 %place.10 = (bf16[12,16,5120]{2,1,0:T(8,128)(2,1)}, bf16[16,16,5120]{2,1,0:T(8,128)(2,1)}, bf16[28,16,2304]{2,1,0:T(8,128)(2,1)}) custom-call(s32[1]{0:T(128)} %bitcast.1.refs_0_, s32[4]{0:T(128)} %refs_1_.35, s32[4]{0:T(128)} %refs_2_.35, s32[4,16]{1,0:T(4,128)} %refs_3_.35, ...), custom_call_target="tpu_custom_call", output_to_operand_aliasing={{0}: (9, {}), {1}: (10, {}), {2}: (11, {})} | custom-call | tf_op jit(solution)/shard_map/place/pallas_call | solution.py:426
  154.2 5.2 %collective-permute-start.29 = (bf16[2,2,8,16,128]{4,3,2,1,0:T(8,128)(2,1)}, bf16[2,2,8,16,128]{4,3,2,1,0:T(8,128)(2,1)}, u32[]{:S(2)}, u32[]{:S(2)}) collective-permute-start(bf16[2,2,8,16,128]{4,3,2,1,0:T(8,128)(2,1)} %get-tuple-element.179), channel_id=1, source_target_pairs={{0,12},{4,0},{8,4},{12,8},{1,13},{5,1},{9,5},{13,9},{2,14},{6,2},{... | collective-permute-start | bytes 393224 | tf_op jit(solution)/shard_map/ppermute | solution.py:497
  160.0 2.9 %finish.2 = (bf16[12,16,5120]{2,1,0:T(8,128)(2,1)}, bf16[16,16,5120]{2,1,0:T(8,128)(2,1)}) custom-call(s32[1]{0:T(128)} %bitcast.near_ref.refs_4_, bf16[28,16,2304]{2,1,0:T(8,128)(2,1)} %collective-permute-done.35.refs_0_, bf16[12,16,5120]{2,1,0:T(8,128)(2,1)} %get-tuple-element.195.refs_1_, ...), custom_call_target="tpu_custom_call", output_to_operand_aliasing={{0}: (2, {}), {1}: (3, {})} | custom-call | tf_op jit(solution)/shard_map/finish/pallas_call | solution.py:475
  162.9 4.6 %collective-permute-done.28.refs_7_ = bf16[2,2,3,16,128]{4,3,2,1,0:T(8,128)(2,1)} collective-permute-done((bf16[2,2,3,16,128]{4,3,2,1,0:T(8,128)(2,1)}, bf16[2,2,3,16,128]{4,3,2,1,0:T(8,128)(2,1)}, u32[]{:S(2)}, u32[]{:S(2)}) %collective-permute-start.28) | collective-permute-done | bytes 49184 | tf_op jit(solution)/shard_map/ppermute | solution.py:497
  167.5 2.0 %place.11 = (bf16[12,16,5120]{2,1,0:T(8,128)(2,1)}, bf16[16,16,5120]{2,1,0:T(8,128)(2,1)}, bf16[28,16,256]{2,1,0:T(8,128)(2,1)}) custom-call(s32[1]{0:T(128)} %bitcast.1.refs_0_, s32[4]{0:T(128)} %refs_1_.35, s32[4]{0:T(128)} %refs_2_.35, s32[4,16]{1,0:T(4,128)} %refs_3_.35, s32[1]{0:T(128)} %bitcast.near_ref.refs_4_, ...), custom_call_target="tpu_custom_call", output_to_operand_aliasing={{0}: (9, {}), {1}: (10, {})} | custom-call | tf_op jit(solution)/shard_map/place/pallas_call | solution.py:426
  169.6 1.8 %collective-permute-done.36.refs_0_ = bf16[28,16,256]{2,1,0:T(8,128)(2,1)} collective-permute-done((bf16[28,16,256]{2,1,0:T(8,128)(2,1)}, bf16[28,16,256]{2,1,0:T(8,128)(2,1)}, u32[]{:S(2)}, u32[]{:S(2)}) %collective-permute-start.36) | collective-permute-done | bytes 229408 | tf_op jit(solution)/shard_map/ppermute | solution.py:492
  171.4 1.6 finish.3
  (51 shorter events, 15.3 us)
Async XLA Ops:
  5.8 2.0 %collective-permute-start = (bf16[2,2,16,16,128]{4,3,2,1,0:T(8,128)(2,1)}, bf16[2,2,16,16,128]{4,3,2,1,0:T(8,128)(2,1)}, u32[]{:S(2)}, u32[]{:S(2)}) collective-permute-start(bf16[2,2,16,16,128]{4,3,2,1,0:T(8,128)(2,1)} %get-tuple-element.104), channel_id=1, source_target_pairs={{0,1},{1,0},{2,3},{3,2},{4,5},{5,4},{6,7},{7,6},{8,9},{9,8},{10,11... | collective-permute-start | bytes 786440 | tf_op jit(solution)/shard_map/ppermute | solution.py:492
  9.7 15.9 %collective-permute-start.3 = (bf16[2,2,2,16,16,128]{5,4,3,2,1,0:T(8,128)(2,1)}, bf16[2,2,2,16,16,128]{5,4,3,2,1,0:T(8,128)(2,1)}, u32[]{:S(2)}, u32[]{:S(2)}) collective-permute-start(bf16[2,2,2,16,16,128]{5,4,3,2,1,0:T(8,128)(2,1)} %join_halves.3.refs_7_), channel_id=1, source_target_pairs={{0,2},{1,3},{2,0},{3,1},{4,6},{5,7},{6,4},{7,5},{8,10},{9,11},{10,... | collective-permute-start | bytes 1572872 | tf_op jit(solution)/shard_map/ppermute | solution.py:492
  12.5 4.2 %collective-permute-start.1 = (bf16[4,2,16,16,128]{4,3,2,1,0:T(8,128)(2,1)}, bf16[4,2,16,16,128]{4,3,2,1,0:T(8,128)(2,1)}, u32[]{:S(2)}, u32[]{:S(2)}) collective-permute-start(bf16[4,2,16,16,128]{4,3,2,1,0:T(8,128)(2,1)} %get-tuple-element.108), channel_id=1, source_target_pairs={{0,1},{1,0},{2,3},{3,2},{4,5},{5,4},{6,7},{7,6},{8,9},{9,8},{10,11... | collective-permute-start | bytes 1572872 | tf_op jit(solution)/shard_map/ppermute | solution.py:492
  12.5 25.8 %collective-permute-start.9 = (bf16[14,2,16,16,128]{4,3,2,1,0:T(8,128)(2,1)}, bf16[14,2,16,16,128]{4,3,2,1,0:T(8,128)(2,1)}, u32[]{:S(2)}, u32[]{:S(2)}) collective-permute-start(bf16[14,2,16,16,128]{4,3,2,1,0:T(8,128)(2,1)} %get-tuple-element.124), channel_id=1, source_target_pairs={{0,1},{1,0},{2,3},{3,2},{4,5},{5,4},{6,7},{7,6},{8,9},{9,8},{10,11... | collective-permute-start | bytes 5505032 | tf_op jit(solution)/shard_map/ppermute | solution.py:492
  16.7 33.7 %collective-permute-start.5 = (bf16[18,16,16,128]{3,2,1,0:T(8,128)(2,1)}, bf16[18,16,16,128]{3,2,1,0:T(8,128)(2,1)}, u32[]{:S(2)}, u32[]{:S(2)}) collective-permute-start(bf16[18,16,16,128]{3,2,1,0:T(8,128)(2,1)} %get-tuple-element.116), channel_id=1, source_target_pairs={{0,1},{1,0},{2,3},{3,2},{4,5},{5,4},{6,7},{7,6},{8,9},{9,8},{10,11... | collective-permute-start | bytes 3538952 | tf_op jit(solution)/shard_map/ppermute | solution.py:492
  18.9 31.5 %collective-permute-start.6 = (bf16[4,2,2,16,16,128]{5,4,3,2,1,0:T(8,128)(2,1)}, bf16[4,2,2,16,16,128]{5,4,3,2,1,0:T(8,128)(2,1)}, u32[]{:S(2)}, u32[]{:S(2)}) collective-permute-start(bf16[4,2,2,16,16,128]{5,4,3,2,1,0:T(8,128)(2,1)} %join_halves.4.refs_7_), channel_id=1, source_target_pairs={{0,2},{1,3},{2,0},{3,1},{4,6},{5,7},{6,4},{7,5},{8,10},{9,11},{10,... | collective-permute-start | bytes 3145736 | tf_op jit(solution)/shard_map/ppermute | solution.py:492
  19.0 1.7 collective-permute-start.2
  29.4 7.0 %collective-permute-start.4 = (bf16[2,2,8,16,128]{4,3,2,1,0:T(8,128)(2,1)}, bf16[2,2,8,16,128]{4,3,2,1,0:T(8,128)(2,1)}, u32[]{:S(2)}, u32[]{:S(2)}) collective-permute-start(bf16[2,2,8,16,128]{4,3,2,1,0:T(8,128)(2,1)} %get-tuple-element.113), channel_id=1, source_target_pairs={{0,12},{4,0},{8,4},{12,8},{1,13},{5,1},{9,5},{13,9},{2,14},{6,2},{... | collective-permute-start | bytes 393224 | tf_op jit(solution)/shard_map/ppermute | solution.py:497
  44.7 26.5 %collective-permute-start.10 = (bf16[4,2,2,16,16,128]{5,4,3,2,1,0:T(8,128)(2,1)}, bf16[4,2,2,16,16,128]{5,4,3,2,1,0:T(8,128)(2,1)}, u32[]{:S(2)}, u32[]{:S(2)}) collective-permute-start(bf16[4,2,2,16,16,128]{5,4,3,2,1,0:T(8,128)(2,1)} %get-tuple-element.126.refs_7_), channel_id=1, source_target_pairs={{0,2},{1,3},{2,0},{3,1},{4,6},{5,7},{6,4},{7,5},{8,10},{9,11},{10,... | collective-permute-start | bytes 3145736 | tf_op jit(solution)/shard_map/ppermute | solution.py:492
  46.2 10.1 %collective-permute-start.7 = (bf16[2,2,8,16,128]{4,3,2,1,0:T(8,128)(2,1)}, bf16[2,2,8,16,128]{4,3,2,1,0:T(8,128)(2,1)}, u32[]{:S(2)}, u32[]{:S(2)}) collective-permute-start(bf16[2,2,8,16,128]{4,3,2,1,0:T(8,128)(2,1)} %get-tuple-element.119), channel_id=1, source_target_pairs={{0,12},{4,0},{8,4},{12,8},{1,13},{5,1},{9,5},{13,9},{2,14},{6,2},{... | collective-permute-start | bytes 393224 | tf_op jit(solution)/shard_map/ppermute | solution.py:497
  56.3 6.7 %collective-permute-start.8 = (bf16[4,2,8,16,128]{4,3,2,1,0:T(8,128)(2,1)}, bf16[4,2,8,16,128]{4,3,2,1,0:T(8,128)(2,1)}, u32[]{:S(2)}, u32[]{:S(2)}) collective-permute-start(bf16[4,2,8,16,128]{4,3,2,1,0:T(8,128)(2,1)} %get-tuple-element.120), channel_id=1, source_target_pairs={{0,12},{4,0},{8,4},{12,8},{1,13},{5,1},{9,5},{13,9},{2,14},{6,2},{... | collective-permute-start | bytes 786440 | tf_op jit(solution)/shard_map/ppermute | solution.py:497
  65.2 12.0 %collective-permute-start.11 = (bf16[4,2,8,16,128]{4,3,2,1,0:T(8,128)(2,1)}, bf16[4,2,8,16,128]{4,3,2,1,0:T(8,128)(2,1)}, u32[]{:S(2)}, u32[]{:S(2)}) collective-permute-start(bf16[4,2,8,16,128]{4,3,2,1,0:T(8,128)(2,1)} %get-tuple-element.129), channel_id=1, source_target_pairs={{0,12},{4,0},{8,4},{12,8},{1,13},{5,1},{9,5},{13,9},{2,14},{6,2},{... | collective-permute-start | bytes 786440 | tf_op jit(solution)/shard_map/ppermute | solution.py:497
  69.1 25.2 %collective-permute-start.15 = (bf16[4,2,2,16,16,128]{5,4,3,2,1,0:T(8,128)(2,1)}, bf16[4,2,2,16,16,128]{5,4,3,2,1,0:T(8,128)(2,1)}, u32[]{:S(2)}, u32[]{:S(2)}) collective-permute-start(bf16[4,2,2,16,16,128]{5,4,3,2,1,0:T(8,128)(2,1)} %get-tuple-element.140.refs_7_), channel_id=1, source_target_pairs={{0,2},{1,3},{2,0},{3,1},{4,6},{5,7},{6,4},{7,5},{8,10},{9,11},{10,... | collective-permute-start | bytes 3145736 | tf_op jit(solution)/shard_map/ppermute | solution.py:492
  70.6 10.7 %collective-permute-start.13 = (bf16[2,2,5,16,128]{4,3,2,1,0:T(8,128)(2,1)}, bf16[2,2,5,16,128]{4,3,2,1,0:T(8,128)(2,1)}, u32[]{:S(2)}, u32[]{:S(2)}) collective-permute-start(bf16[2,2,5,16,128]{4,3,2,1,0:T(8,128)(2,1)} %get-tuple-element.133), channel_id=1, source_target_pairs={{0,4},{4,8},{8,12},{12,0},{1,5},{5,9},{9,13},{13,1},{2,6},{6,10},{... | collective-permute-start | bytes 245768 | tf_op jit(solution)/shard_map/ppermute | solution.py:497
  70.6 10.7 %collective-permute-start.14 = (bf16[2,2,3,16,128]{4,3,2,1,0:T(8,128)(2,1)}, bf16[2,2,3,16,128]{4,3,2,1,0:T(8,128)(2,1)}, u32[]{:S(2)}, u32[]{:S(2)}) collective-permute-start(bf16[2,2,3,16,128]{4,3,2,1,0:T(8,128)(2,1)} %get-tuple-element.135), channel_id=1, source_target_pairs={{0,8},{4,12},{8,0},{12,4},{1,9},{5,13},{9,1},{13,5},{2,10},{6,14},... | collective-permute-start | bytes 147464 | tf_op jit(solution)/shard_map/ppermute | solution.py:497
  77.1 8.5 %collective-permute-start.12 = (bf16[4,2,8,16,128]{4,3,2,1,0:T(8,128)(2,1)}, bf16[4,2,8,16,128]{4,3,2,1,0:T(8,128)(2,1)}, u32[]{:S(2)}, u32[]{:S(2)}) collective-permute-start(bf16[4,2,8,16,128]{4,3,2,1,0:T(8,128)(2,1)} %get-tuple-element.130), channel_id=1, source_target_pairs={{0,12},{4,0},{8,4},{12,8},{1,13},{5,1},{9,5},{13,9},{2,14},{6,2},{... | collective-permute-start | bytes 786440 | tf_op jit(solution)/shard_map/ppermute | solution.py:497
  87.7 12.4 %collective-permute-start.16 = (bf16[4,2,8,16,128]{4,3,2,1,0:T(8,128)(2,1)}, bf16[4,2,8,16,128]{4,3,2,1,0:T(8,128)(2,1)}, u32[]{:S(2)}, u32[]{:S(2)}) collective-permute-start(bf16[4,2,8,16,128]{4,3,2,1,0:T(8,128)(2,1)} %get-tuple-element.143), channel_id=1, source_target_pairs={{0,12},{4,0},{8,4},{12,8},{1,13},{5,1},{9,5},{13,9},{2,14},{6,2},{... | collective-permute-start | bytes 786440 | tf_op jit(solution)/shard_map/ppermute | solution.py:497
  92.0 12.0 %collective-permute-start.18 = (bf16[4,2,5,16,128]{4,3,2,1,0:T(8,128)(2,1)}, bf16[4,2,5,16,128]{4,3,2,1,0:T(8,128)(2,1)}, u32[]{:S(2)}, u32[]{:S(2)}) collective-permute-start(bf16[4,2,5,16,128]{4,3,2,1,0:T(8,128)(2,1)} %get-tuple-element.147), channel_id=1, source_target_pairs={{0,4},{4,8},{8,12},{12,0},{1,5},{5,9},{9,13},{13,1},{2,6},{6,10},{... | collective-permute-start | bytes 491528 | tf_op jit(solution)/shard_map/ppermute | solution.py:497
  92.0 24.8 %collective-permute-start.20 = (bf16[4,2,2,16,16,128]{5,4,3,2,1,0:T(8,128)(2,1)}, bf16[4,2,2,16,16,128]{5,4,3,2,1,0:T(8,128)(2,1)}, u32[]{:S(2)}, u32[]{:S(2)}) collective-permute-start(bf16[4,2,2,16,16,128]{5,4,3,2,1,0:T(8,128)(2,1)} %get-tuple-element.156.refs_7_), channel_id=1, source_target_pairs={{0,2},{1,3},{2,0},{3,1},{4,6},{5,7},{6,4},{7,5},{8,10},{9,11},{10,... | collective-permute-start | bytes 3145736 | tf_op jit(solution)/shard_map/ppermute | solution.py:492
  93.5 10.5 %collective-permute-start.19 = (bf16[4,2,3,16,128]{4,3,2,1,0:T(8,128)(2,1)}, bf16[4,2,3,16,128]{4,3,2,1,0:T(8,128)(2,1)}, u32[]{:S(2)}, u32[]{:S(2)}) collective-permute-start(bf16[4,2,3,16,128]{4,3,2,1,0:T(8,128)(2,1)} %get-tuple-element.149), channel_id=1, source_target_pairs={{0,8},{4,12},{8,0},{12,4},{1,9},{5,13},{9,1},{13,5},{2,10},{6,14},... | collective-permute-start | bytes 294920 | tf_op jit(solution)/shard_map/ppermute | solution.py:497
  100.2 8.5 %collective-permute-start.17 = (bf16[4,2,8,16,128]{4,3,2,1,0:T(8,128)(2,1)}, bf16[4,2,8,16,128]{4,3,2,1,0:T(8,128)(2,1)}, u32[]{:S(2)}, u32[]{:S(2)}) collective-permute-start(bf16[4,2,8,16,128]{4,3,2,1,0:T(8,128)(2,1)} %get-tuple-element.144), channel_id=1, source_target_pairs={{0,12},{4,0},{8,4},{12,8},{1,13},{5,1},{9,5},{13,9},{2,14},{6,2},{... | collective-permute-start | bytes 786440 | tf_op jit(solution)/shard_map/ppermute | solution.py:497
  110.8 15.6 %collective-permute-start.25 = (bf16[4,2,8,16,128]{4,3,2,1,0:T(8,128)(2,1)}, bf16[4,2,8,16,128]{4,3,2,1,0:T(8,128)(2,1)}, u32[]{:S(2)}, u32[]{:S(2)}) collective-permute-start(bf16[4,2,8,16,128]{4,3,2,1,0:T(8,128)(2,1)} %get-tuple-element.171), channel_id=1, source_target_pairs={{0,12},{4,0},{8,4},{12,8},{1,13},{5,1},{9,5},{13,9},{2,14},{6,2},{... | collective-permute-start | bytes 786440 | tf_op jit(solution)/shard_map/ppermute | solution.py:497
  114.6 14.2 %collective-permute-start.21 = (bf16[4,2,5,16,128]{4,3,2,1,0:T(8,128)(2,1)}, bf16[4,2,5,16,128]{4,3,2,1,0:T(8,128)(2,1)}, u32[]{:S(2)}, u32[]{:S(2)}) collective-permute-start(bf16[4,2,5,16,128]{4,3,2,1,0:T(8,128)(2,1)} %get-tuple-element.160), channel_id=1, source_target_pairs={{0,4},{4,8},{8,12},{12,0},{1,5},{5,9},{9,13},{13,1},{2,6},{6,10},{... | collective-permute-start | bytes 491528 | tf_op jit(solution)/shard_map/ppermute | solution.py:497
  114.6 14.0 %collective-permute-start.22 = (bf16[4,2,3,16,128]{4,3,2,1,0:T(8,128)(2,1)}, bf16[4,2,3,16,128]{4,3,2,1,0:T(8,128)(2,1)}, u32[]{:S(2)}, u32[]{:S(2)}) collective-permute-start(bf16[4,2,3,16,128]{4,3,2,1,0:T(8,128)(2,1)} %get-tuple-element.162), channel_id=1, source_target_pairs={{0,8},{4,12},{8,0},{12,4},{1,9},{5,13},{9,1},{13,5},{2,10},{6,14},... | collective-permute-start | bytes 294920 | tf_op jit(solution)/shard_map/ppermute | solution.py:497
  115.2 16.0 %collective-permute-start.23 = (bf16[2,2,2,16,16,128]{5,4,3,2,1,0:T(8,128)(2,1)}, bf16[2,2,2,16,16,128]{5,4,3,2,1,0:T(8,128)(2,1)}, u32[]{:S(2)}, u32[]{:S(2)}) collective-permute-start(bf16[2,2,2,16,16,128]{5,4,3,2,1,0:T(8,128)(2,1)} %get-tuple-element.167.refs_7_), channel_id=1, source_target_pairs={{0,2},{1,3},{2,0},{3,1},{4,6},{5,7},{6,4},{7,5},{8,10},{9,11},{10,... | collective-permute-start | bytes 1572872 | tf_op jit(solution)/shard_map/ppermute | solution.py:492
  122.6 22.4 %collective-permute-start.33 = (bf16[4,2,5,16,128]{4,3,2,1,0:T(8,128)(2,1)}, bf16[4,2,5,16,128]{4,3,2,1,0:T(8,128)(2,1)}, u32[]{:S(2)}, u32[]{:S(2)}) collective-permute-start(bf16[4,2,5,16,128]{4,3,2,1,0:T(8,128)(2,1)} %get-tuple-element.186), channel_id=1, source_target_pairs={{0,4},{4,8},{8,12},{12,0},{1,5},{5,9},{9,13},{13,1},{2,6},{6,10},{... | collective-permute-start | bytes 491528 | tf_op jit(solution)/shard_map/ppermute | solution.py:497
  126.4 16.2 %collective-permute-start.34 = (bf16[4,2,3,16,128]{4,3,2,1,0:T(8,128)(2,1)}, bf16[4,2,3,16,128]{4,3,2,1,0:T(8,128)(2,1)}, u32[]{:S(2)}, u32[]{:S(2)}) collective-permute-start(bf16[4,2,3,16,128]{4,3,2,1,0:T(8,128)(2,1)} %get-tuple-element.188), channel_id=1, source_target_pairs={{0,8},{4,12},{8,0},{12,4},{1,9},{5,13},{9,1},{13,5},{2,10},{6,14},... | collective-permute-start | bytes 294920 | tf_op jit(solution)/shard_map/ppermute | solution.py:497
  128.7 9.1 %collective-permute-start.26 = (bf16[4,2,8,16,128]{4,3,2,1,0:T(8,128)(2,1)}, bf16[4,2,8,16,128]{4,3,2,1,0:T(8,128)(2,1)}, u32[]{:S(2)}, u32[]{:S(2)}) collective-permute-start(bf16[4,2,8,16,128]{4,3,2,1,0:T(8,128)(2,1)} %get-tuple-element.172), channel_id=1, source_target_pairs={{0,12},{4,0},{8,4},{12,8},{1,13},{5,1},{9,5},{13,9},{2,14},{6,2},{... | collective-permute-start | bytes 786440 | tf_op jit(solution)/shard_map/ppermute | solution.py:497
  135.2 12.3 %collective-permute-start.24 = (bf16[2,2,8,16,128]{4,3,2,1,0:T(8,128)(2,1)}, bf16[2,2,8,16,128]{4,3,2,1,0:T(8,128)(2,1)}, u32[]{:S(2)}, u32[]{:S(2)}) collective-permute-start(bf16[2,2,8,16,128]{4,3,2,1,0:T(8,128)(2,1)} %get-tuple-element.169), channel_id=1, source_target_pairs={{0,12},{4,0},{8,4},{12,8},{1,13},{5,1},{9,5},{13,9},{2,14},{6,2},{... | collective-permute-start | bytes 393224 | tf_op jit(solution)/shard_map/ppermute | solution.py:497
  139.9 11.3 %collective-permute-start.30 = (bf16[4,2,5,16,128]{4,3,2,1,0:T(8,128)(2,1)}, bf16[4,2,5,16,128]{4,3,2,1,0:T(8,128)(2,1)}, u32[]{:S(2)}, u32[]{:S(2)}) collective-permute-start(bf16[4,2,5,16,128]{4,3,2,1,0:T(8,128)(2,1)} %get-tuple-element.181), channel_id=1, source_target_pairs={{0,4},{4,8},{8,12},{12,0},{1,5},{5,9},{9,13},{13,1},{2,6},{6,10},{... | collective-permute-start | bytes 491528 | tf_op jit(solution)/shard_map/ppermute | solution.py:497
  142.6 8.5 %collective-permute-start.31 = (bf16[4,2,3,16,128]{4,3,2,1,0:T(8,128)(2,1)}, bf16[4,2,3,16,128]{4,3,2,1,0:T(8,128)(2,1)}, u32[]{:S(2)}, u32[]{:S(2)}) collective-permute-start(bf16[4,2,3,16,128]{4,3,2,1,0:T(8,128)(2,1)} %get-tuple-element.182), channel_id=1, source_target_pairs={{0,8},{4,12},{8,0},{12,4},{1,9},{5,13},{9,1},{13,5},{2,10},{6,14},... | collective-permute-start | bytes 294920 | tf_op jit(solution)/shard_map/ppermute | solution.py:497
  142.6 9.1 %collective-permute-start.32 = (bf16[4,2,8,16,128]{4,3,2,1,0:T(8,128)(2,1)}, bf16[4,2,8,16,128]{4,3,2,1,0:T(8,128)(2,1)}, u32[]{:S(2)}, u32[]{:S(2)}) collective-permute-start(bf16[4,2,8,16,128]{4,3,2,1,0:T(8,128)(2,1)} %get-tuple-element.183), channel_id=1, source_target_pairs={{0,12},{4,0},{8,4},{12,8},{1,13},{5,1},{9,5},{13,9},{2,14},{6,2},{... | collective-permute-start | bytes 786440 | tf_op jit(solution)/shard_map/ppermute | solution.py:497
  154.1 5.9 %collective-permute-start.35 = (bf16[28,16,2304]{2,1,0:T(8,128)(2,1)}, bf16[28,16,2304]{2,1,0:T(8,128)(2,1)}, u32[]{:S(2)}, u32[]{:S(2)}) collective-permute-start(bf16[28,16,2304]{2,1,0:T(8,128)(2,1)} %get-tuple-element.194), channel_id=1, source_target_pairs={{0,1},{1,0},{2,3},{3,2},{4,5},{5,4},{6,7},{7,6},{8,9},{9,8},{10,11... | collective-permute-start | bytes 6193160 | tf_op jit(solution)/shard_map/ppermute | solution.py:492
  154.2 13.3 %collective-permute-start.29 = (bf16[2,2,8,16,128]{4,3,2,1,0:T(8,128)(2,1)}, bf16[2,2,8,16,128]{4,3,2,1,0:T(8,128)(2,1)}, u32[]{:S(2)}, u32[]{:S(2)}) collective-permute-start(bf16[2,2,8,16,128]{4,3,2,1,0:T(8,128)(2,1)} %get-tuple-element.179), channel_id=1, source_target_pairs={{0,12},{4,0},{8,4},{12,8},{1,13},{5,1},{9,5},{13,9},{2,14},{6,2},{... | collective-permute-start | bytes 393224 | tf_op jit(solution)/shard_map/ppermute | solution.py:497
  159.4 8.1 %collective-permute-start.27 = (bf16[2,2,5,16,128]{4,3,2,1,0:T(8,128)(2,1)}, bf16[2,2,5,16,128]{4,3,2,1,0:T(8,128)(2,1)}, u32[]{:S(2)}, u32[]{:S(2)}) collective-permute-start(bf16[2,2,5,16,128]{4,3,2,1,0:T(8,128)(2,1)} %get-tuple-element.177), channel_id=1, source_target_pairs={{0,4},{4,8},{8,12},{12,0},{1,5},{5,9},{9,13},{13,1},{2,6},{6,10},{... | collective-permute-start | bytes 245768 | tf_op jit(solution)/shard_map/ppermute | solution.py:497
  159.4 8.1 %collective-permute-start.28 = (bf16[2,2,3,16,128]{4,3,2,1,0:T(8,128)(2,1)}, bf16[2,2,3,16,128]{4,3,2,1,0:T(8,128)(2,1)}, u32[]{:S(2)}, u32[]{:S(2)}) collective-permute-start(bf16[2,2,3,16,128]{4,3,2,1,0:T(8,128)(2,1)} %get-tuple-element.178), channel_id=1, source_target_pairs={{0,8},{4,12},{8,0},{12,4},{1,9},{5,13},{9,1},{13,5},{2,10},{6,14},... | collective-permute-start | bytes 147464 | tf_op jit(solution)/shard_map/ppermute | solution.py:497
  169.5 1.9 %collective-permute-start.36 = (bf16[28,16,256]{2,1,0:T(8,128)(2,1)}, bf16[28,16,256]{2,1,0:T(8,128)(2,1)}, u32[]{:S(2)}, u32[]{:S(2)}) collective-permute-start(bf16[28,16,256]{2,1,0:T(8,128)(2,1)} %get-tuple-element.199), channel_id=1, source_target_pairs={{0,1},{1,0},{2,3},{3,2},{4,5},{5,4},{6,7},{7,6},{8,9},{9,8},{10,11... | collective-permute-start | bytes 688136 | tf_op jit(solution)/shard_map/ppermute | solution.py:492

commit v4 on v3

--- a/solution.py
+++ b/solution.py
@@ -42,10 +42,13 @@
 STAGE_COST = 0.0
 BLEND_COST = 0.0
 SWAP = 1
-PLACE_COST = 6.0
+PLACE_COST = 7.5
 TAIL_COST = 0.0
 LATE_CHUNKS = 1
-FREE = 2
+FREE = 1
+P3_TIE = 0
+CHAIN = 1
+OX_TIE = 0
 SMEM = pl.BlockSpec(memory_space=pltpu.SMEM)
 
 
@@ -723,17 +726,17 @@
         )
         return left
 
-    def mix(chunk, *earlier):
+    def mix(chunk, earlier, gate=()):
         ready = after(arrived[chunk], *earlier)
         (((homes[chunk], *waiting[chunk]),), (left,)) = run_stage(
             tables, [blend_task(attended[chunk], ready, 0, windows)], BLEND_COST
         )
-        received[chunk] = [shift(left, -1)]
-
-    def send_around(chunk, *earlier):
+        received[chunk] = [shift(after(left, *gate), -1)]
+
+    def send_around(chunk, gates):
         received[chunk] = [
-            shift(after(array, *earlier), distance)
-            for distance, array in enumerate(waiting[chunk], 1)
+            shift(after(array, *gate), distance)
+            for distance, (array, gate) in enumerate(zip(waiting[chunk], gates), 1)
         ] + received[chunk]
 
     swapped = SWAP if count > 3 else 0
@@ -742,12 +745,12 @@
         gate = received[chunk - 1] if chunk else []
         arrived[chunk] = shift(after(left, *gate), -1)
         if chunk >= 1:
-            send_around(chunk - 1, attended[chunk])
+            send_around(chunk - 1, [[attended[chunk]]] * windows)
         if chunk >= 2:
             targets = place_chunk(chunk - 2, attended[chunk])
         if chunk == count - 1 - swapped and swapped:
             break
-        mix(chunk, *targets[:1])
+        mix(chunk, targets[:1])
         if chunk == 0:
             join_group(2, homes[0])
             for later in range(2, count):
@@ -755,14 +758,20 @@
     if swapped:
         left = attend(count - 1, attended[count - 2], targets[0])
         arrived[count - 1] = shift(left, -1)
-        mix(count - 2, attended[count - 1])
-        send_around(count - 2)
-        targets = place_chunk(count - 3, homes[count - 2])
-        mix(count - 1, homes[count - 2])
-    send_around(count - 1)
+        mix(count - 2, [attended[count - 1]])
+        send_around(count - 2, [[]] * windows)
+        if P3_TIE == 0:
+            targets = place_chunk(count - 3, homes[count - 2])
+        mix(count - 1, [homes[count - 2]], received[count - 2][-1:] if CHAIN else [])
+    chained = CHAIN and swapped
+    gates = [[array] for array in received[count - 2]] if chained else [[]] * windows
+    send_around(count - 1, gates)
+    if swapped and P3_TIE:
+        targets = place_chunk(count - 3, homes[count - 1])
     targets = place_chunk(count - 2, homes[count - 1])
     if LATE_CHUNKS > 1:
-        arrived = exchange(after(others[False], homes[count - 1]), 1)
+        tie = (homes[count - 1], attended[count - 1], homes[count - 2])[OX_TIE]
+        arrived = exchange(after(others[False], tie), 1)
     else:
         arrived = exchange(others[False], 1)
     targets = finish(near, [arrived], [0], head_size, targets)

time: 174 us -> 173 us (level)
  transfers between devices with their start and end apart: 37 -> 37, of which waited for: 14 -> 15; matrix products, arithmetic and copies ran while one was open for 0% -> 0% of each run, Pallas kernels for 39% -> 39%
where the time goes in v4:
time: 173 us; the launch traced here: 172 us
  Pallas kernels  80.9 us (47%)
  starting transfers between devices  59.8 us (35%)
  waiting for transfers between devices  30.5 us (18%)
    ppermute x24, starting transfers between devices, shift(): lax.ppermute(array, 'win', [(i, (i + step) % count) for i in range(count)])  49.4 us
    pallas_call x12, Pallas kernels, run_stage(): pl.pallas_call(kernel, grid=(steps,), in_specs=[SMEM for _ in tables] + [...  43.6 us
    ppermute x24, waiting for transfers between devices, shift(): lax.ppermute(array, 'win', [(i, (i + step) % count) for i in range(count)])  20 us
    pallas_call x6, Pallas kernels, place(): pl.pallas_call(kernel, grid=(1,), in_specs=[SMEM for _ in tables] + [firs...  13.5 us
    ppermute x13, waiting for transfers between devices, exchange(): lax.ppermute(array, 'uly', [(i, i ^ bit) for i in range(lax.axis_size('ul...  10.5 us
    ppermute x13, starting transfers between devices, exchange(): lax.ppermute(array, 'uly', [(i, i ^ bit) for i in range(lax.axis_size('ul...  10.4 us
    pallas_call x3, Pallas kernels, join_halves(): pl.pallas_call(kernel, grid=(sum(counts) // STEP_HEADS,), in_specs=[pl.Bl...  10.4 us
    pallas_call x2, Pallas kernels, split_heads(): pl.pallas_call(kernel, grid=(frames // frames_per_step,), in_specs=[SMEM,...  8.88 us
  transfers between devices with their start and end apart: 37, of which 15 were waited for; matrix products, arithmetic and copies ran while one was open for 0% of the time, Pallas kernels for 39%

profile of v4, /device:TPU:0, one launch (start us, length us, event | category | flops | bytes accessed | tf_op | source)
XLA Modules:
  0.0 172.3 jit_solution(11712547913423549083)
XLA Ops:
  0.6 5.2 %norm_split.2 = (bf16[20,2,16,16,128]{4,3,2,1,0:T(8,128)(2,1)}, bf16[2,2,16,16,128]{4,3,2,1,0:T(8,128)(2,1)}, bf16[4,2,16,16,128]{4,3,2,1,0:T(8,128)(2,1)}, bf16[14,2,16,16,128]{4,3,2,1,0:T(8,128)(2,1)}) custom-call(s32[1]{0:T(128)} %bitcast.near_ref.refs_4_, bf16[16,16,5120]{2,1,0:T(8,128)(2,1)} %bitcast.9, f32[1,1,5120]{2,1,0:T(1,128)} %bitcast.12, ...), custom_call_target="tpu_custom_call" | custom-call | flops 10005000192 | tf_op jit(solution)/shard_map/norm_split/pallas_call | solution.py:98
  6.3 1.5 collective-permute-done.other_ref
  7.8 1.9 %join_halves.3.refs_7_ = bf16[2,2,2,16,16,128]{5,4,3,2,1,0:T(8,128)(2,1)} custom-call(bf16[20,2,16,16,128]{4,3,2,1,0:T(8,128)(2,1)} %get-tuple-element.106.own_ref, bf16[2,2,16,16,128]{4,3,2,1,0:T(8,128)(2,1)} %collective-permute-done.other_ref), custom_call_target="tpu_custom_call" | custom-call | flops 10005000192 | tf_op jit(solution)/shard_map/join_halves/pallas_call | solution.py:133
  9.7 2.9 %collective-permute-start.3 = (bf16[2,2,2,16,16,128]{5,4,3,2,1,0:T(8,128)(2,1)}, bf16[2,2,2,16,16,128]{5,4,3,2,1,0:T(8,128)(2,1)}, u32[]{:S(2)}, u32[]{:S(2)}) collective-permute-start(bf16[2,2,2,16,16,128]{5,4,3,2,1,0:T(8,128)(2,1)} %join_halves.3.refs_7_), channel_id=1, source_target_pairs={{0,2},{1,3},{2,0},{3,1},{4,6},{5,7},{6,4},{7,5},{8,10},{9,11},{10,... | collective-permute-start | bytes 1572872 | tf_op jit(solution)/shard_map/ppermute | solution.py:495
  13.0 3.7 %norm_split.3 = (bf16[20,16,16,128]{3,2,1,0:T(8,128)(2,1)}, bf16[2,16,16,128]{3,2,1,0:T(8,128)(2,1)}, bf16[18,16,16,128]{3,2,1,0:T(8,128)(2,1)}) custom-call(s32[1]{0:T(128)} %bitcast.near_ref.refs_4_, bf16[16,16,5120]{2,1,0:T(8,128)(2,1)} %bitcast.11, f32[1,1,5120]{2,1,0:T(1,128)} %bitcast.13), custom_call_target="tpu_custom_call" | custom-call | flops 10005000192 | tf_op jit(solution)/shard_map/norm_split/pallas_call | solution.py:98
  16.7 2.2 %join_halves.4.refs_7_ = bf16[4,2,2,16,16,128]{5,4,3,2,1,0:T(8,128)(2,1)} custom-call(bf16[20,2,16,16,128]{4,3,2,1,0:T(8,128)(2,1)} %get-tuple-element.106.own_ref, bf16[4,2,16,16,128]{4,3,2,1,0:T(8,128)(2,1)} %collective-permute-done.1.other_ref), custom_call_target="tpu_custom_call" | custom-call | flops 10005000192 | tf_op jit(solution)/shard_map/join_halves/pallas_call | solution.py:133
  20.7 4.8 %collective-permute-done.3.refs_8_ = bf16[2,2,2,16,16,128]{5,4,3,2,1,0:T(8,128)(2,1)} collective-permute-done((bf16[2,2,2,16,16,128]{5,4,3,2,1,0:T(8,128)(2,1)}, bf16[2,2,2,16,16,128]{5,4,3,2,1,0:T(8,128)(2,1)}, u32[]{:S(2)}, u32[]{:S(2)}) %collective-permute-start.3) | collective-permute-done | bytes 524320 | tf_op jit(solution)/shard_map/ppermute | solution.py:495
  25.5 3.9 %stage.12 = (bf16[2,2,16,16,128]{4,3,2,1,0:T(8,128)(2,1)}, bf16[2,2,8,16,128]{4,3,2,1,0:T(8,128)(2,1)}) custom-call(s32[1]{0:T(128)} %bitcast.1.refs_0_, s32[4]{0:T(128)} %refs_1_.35, s32[4]{0:T(128)} %refs_2_.35, s32[4,16]{1,0:T(4,128)} %refs_3_.35, s32[1]{0:T(128)} %bitcast.near_ref.refs_4_, bf16[20,16,16,128]{3,2,1,0:T(8,128)(2,1)} %get-tuple-element.169.refs_5_, ...), custom_call_target="tpu_custom_call" | custom-call | tf_op jit(solution)/shard_map/stage/pallas_call | solution.py:378
  29.4 4.2 %collective-permute-start.4 = (bf16[2,2,8,16,128]{4,3,2,1,0:T(8,128)(2,1)}, bf16[2,2,8,16,128]{4,3,2,1,0:T(8,128)(2,1)}, u32[]{:S(2)}, u32[]{:S(2)}) collective-permute-start(bf16[2,2,8,16,128]{4,3,2,1,0:T(8,128)(2,1)} %get-tuple-element.116), channel_id=1, source_target_pairs={{0,12},{4,0},{8,4},{12,8},{1,13},{5,1},{9,5},{13,9},{2,14},{6,2},{... | collective-permute-start | bytes 393224 | tf_op jit(solution)/shard_map/ppermute | solution.py:500
  33.6 2.8 %collective-permute-done.4.refs_6_ = bf16[2,2,8,16,128]{4,3,2,1,0:T(8,128)(2,1)} collective-permute-done((bf16[2,2,8,16,128]{4,3,2,1,0:T(8,128)(2,1)}, bf16[2,2,8,16,128]{4,3,2,1,0:T(8,128)(2,1)}, u32[]{:S(2)}, u32[]{:S(2)}) %collective-permute-start.4) | collective-permute-done | bytes 131104 | tf_op jit(solution)/shard_map/ppermute | solution.py:500
  36.4 1.9 %stage.13 = (bf16[2,2,12,16,128]{4,3,2,1,0:T(8,128)(2,1)}, bf16[2,2,5,16,128]{4,3,2,1,0:T(8,128)(2,1)}, bf16[2,2,3,16,128]{4,3,2,1,0:T(8,128)(2,1)}, bf16[2,2,8,16,128]{4,3,2,1,0:T(8,128)(2,1)}) custom-call(s32[1]{0:T(128)} %bitcast.1.refs_0_, s32[4]{0:T(128)} %refs_1_.35, s32[4]{0:T(128)} %refs_2_.35, s32[4,16]{1,0:T(4,128)} %refs_3_.35, ...), custom_call_target="tpu_custom_call" | custom-call | tf_op jit(solution)/shard_map/stage/pallas_call | solution.py:378
  38.3 6.4 %join_halves.5 = (bf16[4,2,2,16,16,128]{5,4,3,2,1,0:T(8,128)(2,1)}, bf16[4,2,2,16,16,128]{5,4,3,2,1,0:T(8,128)(2,1)}, bf16[4,2,2,16,16,128]{5,4,3,2,1,0:T(8,128)(2,1)}, bf16[2,2,2,16,16,128]{5,4,3,2,1,0:T(8,128)(2,1)}) custom-call(bf16[20,2,16,16,128]{4,3,2,1,0:T(8,128)(2,1)} %get-tuple-element.106.own_ref, ...), custom_call_target="tpu_custom_call" | custom-call | tf_op jit(solution)/shard_map/join_halves/pallas_call | solution.py:133
  46.2 4.2 %collective-permute-start.7 = (bf16[2,2,8,16,128]{4,3,2,1,0:T(8,128)(2,1)}, bf16[2,2,8,16,128]{4,3,2,1,0:T(8,128)(2,1)}, u32[]{:S(2)}, u32[]{:S(2)}) collective-permute-start(bf16[2,2,8,16,128]{4,3,2,1,0:T(8,128)(2,1)} %get-tuple-element.122), channel_id=1, source_target_pairs={{0,12},{4,0},{8,4},{12,8},{1,13},{5,1},{9,5},{13,9},{2,14},{6,2},{... | collective-permute-start | bytes 393224 | tf_op jit(solution)/shard_map/ppermute | solution.py:500
  50.4 5.9 %stage.14 = (bf16[4,2,16,16,128]{4,3,2,1,0:T(8,128)(2,1)}, bf16[4,2,8,16,128]{4,3,2,1,0:T(8,128)(2,1)}) custom-call(s32[1]{0:T(128)} %bitcast.1.refs_0_, s32[4]{0:T(128)} %refs_1_.35, s32[4]{0:T(128)} %refs_2_.35, s32[4,16]{1,0:T(4,128)} %refs_3_.35, s32[1]{0:T(128)} %bitcast.near_ref.refs_4_, bf16[20,16,16,128]{3,2,1,0:T(8,128)(2,1)} %get-tuple-element.169.refs_5_, ...), custom_call_target="tpu_custom_call" | custom-call | tf_op jit(solution)/shard_map/stage/pallas_call | solution.py:378
  56.3 1.8 %collective-permute-start.8 = (bf16[4,2,8,16,128]{4,3,2,1,0:T(8,128)(2,1)}, bf16[4,2,8,16,128]{4,3,2,1,0:T(8,128)(2,1)}, u32[]{:S(2)}, u32[]{:S(2)}) collective-permute-start(bf16[4,2,8,16,128]{4,3,2,1,0:T(8,128)(2,1)} %get-tuple-element.123), channel_id=1, source_target_pairs={{0,12},{4,0},{8,4},{12,8},{1,13},{5,1},{9,5},{13,9},{2,14},{6,2},{... | collective-permute-start | bytes 786440 | tf_op jit(solution)/shard_map/ppermute | solution.py:500
  58.1 5.0 %collective-permute-done.8.refs_6_ = bf16[4,2,8,16,128]{4,3,2,1,0:T(8,128)(2,1)} collective-permute-done((bf16[4,2,8,16,128]{4,3,2,1,0:T(8,128)(2,1)}, bf16[4,2,8,16,128]{4,3,2,1,0:T(8,128)(2,1)}, u32[]{:S(2)}, u32[]{:S(2)}) %collective-permute-start.8) | collective-permute-done | bytes 262176 | tf_op jit(solution)/shard_map/ppermute | solution.py:500
  63.1 2.1 %stage.15 = (bf16[4,2,12,16,128]{4,3,2,1,0:T(8,128)(2,1)}, bf16[4,2,5,16,128]{4,3,2,1,0:T(8,128)(2,1)}, bf16[4,2,3,16,128]{4,3,2,1,0:T(8,128)(2,1)}, bf16[4,2,8,16,128]{4,3,2,1,0:T(8,128)(2,1)}) custom-call(s32[1]{0:T(128)} %bitcast.1.refs_0_, s32[4]{0:T(128)} %refs_1_.35, s32[4]{0:T(128)} %refs_2_.35, s32[4,16]{1,0:T(4,128)} %refs_3_.35, ...), custom_call_target="tpu_custom_call" | custom-call | tf_op jit(solution)/shard_map/stage/pallas_call | solution.py:378
  65.2 3.9 %collective-permute-start.11 = (bf16[4,2,8,16,128]{4,3,2,1,0:T(8,128)(2,1)}, bf16[4,2,8,16,128]{4,3,2,1,0:T(8,128)(2,1)}, u32[]{:S(2)}, u32[]{:S(2)}) collective-permute-start(bf16[4,2,8,16,128]{4,3,2,1,0:T(8,128)(2,1)} %get-tuple-element.132), channel_id=1, source_target_pairs={{0,12},{4,0},{8,4},{12,8},{1,13},{5,1},{9,5},{13,9},{2,14},{6,2},{... | collective-permute-start | bytes 786440 | tf_op jit(solution)/shard_map/ppermute | solution.py:500
  71.2 5.9 %stage.16 = (bf16[4,2,16,16,128]{4,3,2,1,0:T(8,128)(2,1)}, bf16[4,2,8,16,128]{4,3,2,1,0:T(8,128)(2,1)}) custom-call(s32[1]{0:T(128)} %bitcast.1.refs_0_, s32[4]{0:T(128)} %refs_1_.35, s32[4]{0:T(128)} %refs_2_.35, s32[4,16]{1,0:T(4,128)} %refs_3_.35, s32[1]{0:T(128)} %bitcast.near_ref.refs_4_, bf16[20,16,16,128]{3,2,1,0:T(8,128)(2,1)} %get-tuple-element.169.refs_5_, ...), custom_call_target="tpu_custom_call" | custom-call | tf_op jit(solution)/shard_map/stage/pallas_call | solution.py:378
  77.1 3.6 %collective-permute-start.12 = (bf16[4,2,8,16,128]{4,3,2,1,0:T(8,128)(2,1)}, bf16[4,2,8,16,128]{4,3,2,1,0:T(8,128)(2,1)}, u32[]{:S(2)}, u32[]{:S(2)}) collective-permute-start(bf16[4,2,8,16,128]{4,3,2,1,0:T(8,128)(2,1)} %get-tuple-element.133), channel_id=1, source_target_pairs={{0,12},{4,0},{8,4},{12,8},{1,13},{5,1},{9,5},{13,9},{2,14},{6,2},{... | collective-permute-start | bytes 786440 | tf_op jit(solution)/shard_map/ppermute | solution.py:500
  80.7 2.0 %place.6 = (bf16[12,16,5120]{2,1,0:T(8,128)(2,1)}, bf16[16,16,5120]{2,1,0:T(8,128)(2,1)}, bf16[28,16,2304]{2,1,0:T(8,128)(2,1)}) custom-call(s32[1]{0:T(128)} %bitcast.1.refs_0_, s32[4]{0:T(128)} %refs_1_.35, s32[4]{0:T(128)} %refs_2_.35, s32[4,16]{1,0:T(4,128)} %refs_3_.35, s32[1]{0:T(128)} %bitcast.near_ref.refs_4_, ...), custom_call_target="tpu_custom_call" | custom-call | flops 8625000448 | tf_op jit(solution)/shard_map/place/pallas_call | solution.py:429
  82.8 2.8 %collective-permute-done.12.refs_6_ = bf16[4,2,8,16,128]{4,3,2,1,0:T(8,128)(2,1)} collective-permute-done((bf16[4,2,8,16,128]{4,3,2,1,0:T(8,128)(2,1)}, bf16[4,2,8,16,128]{4,3,2,1,0:T(8,128)(2,1)}, u32[]{:S(2)}, u32[]{:S(2)}) %collective-permute-start.12) | collective-permute-done | bytes 262176 | tf_op jit(solution)/shard_map/ppermute | solution.py:500
  85.6 2.2 %stage.17 = (bf16[4,2,12,16,128]{4,3,2,1,0:T(8,128)(2,1)}, bf16[4,2,5,16,128]{4,3,2,1,0:T(8,128)(2,1)}, bf16[4,2,3,16,128]{4,3,2,1,0:T(8,128)(2,1)}, bf16[4,2,8,16,128]{4,3,2,1,0:T(8,128)(2,1)}) custom-call(s32[1]{0:T(128)} %bitcast.1.refs_0_, s32[4]{0:T(128)} %refs_1_.35, s32[4]{0:T(128)} %refs_2_.35, s32[4,16]{1,0:T(4,128)} %refs_3_.35, ...), custom_call_target="tpu_custom_call" | custom-call | tf_op jit(solution)/shard_map/stage/pallas_call | solution.py:378
  87.7 3.7 %collective-permute-start.16 = (bf16[4,2,8,16,128]{4,3,2,1,0:T(8,128)(2,1)}, bf16[4,2,8,16,128]{4,3,2,1,0:T(8,128)(2,1)}, u32[]{:S(2)}, u32[]{:S(2)}) collective-permute-start(bf16[4,2,8,16,128]{4,3,2,1,0:T(8,128)(2,1)} %get-tuple-element.146), channel_id=1, source_target_pairs={{0,12},{4,0},{8,4},{12,8},{1,13},{5,1},{9,5},{13,9},{2,14},{6,2},{... | collective-permute-start | bytes 786440 | tf_op jit(solution)/shard_map/ppermute | solution.py:500
  93.9 5.9 %stage.18 = (bf16[4,2,16,16,128]{4,3,2,1,0:T(8,128)(2,1)}, bf16[4,2,8,16,128]{4,3,2,1,0:T(8,128)(2,1)}) custom-call(s32[1]{0:T(128)} %bitcast.1.refs_0_, s32[4]{0:T(128)} %refs_1_.35, s32[4]{0:T(128)} %refs_2_.35, s32[4,16]{1,0:T(4,128)} %refs_3_.35, s32[1]{0:T(128)} %bitcast.near_ref.refs_4_, bf16[20,16,16,128]{3,2,1,0:T(8,128)(2,1)} %get-tuple-element.169.refs_5_, ...), custom_call_target="tpu_custom_call" | custom-call | tf_op jit(solution)/shard_map/stage/pallas_call | solution.py:378
  99.8 4.7 %collective-permute-start.17 = (bf16[4,2,8,16,128]{4,3,2,1,0:T(8,128)(2,1)}, bf16[4,2,8,16,128]{4,3,2,1,0:T(8,128)(2,1)}, u32[]{:S(2)}, u32[]{:S(2)}) collective-permute-start(bf16[4,2,8,16,128]{4,3,2,1,0:T(8,128)(2,1)} %get-tuple-element.147), channel_id=1, source_target_pairs={{0,12},{4,0},{8,4},{12,8},{1,13},{5,1},{9,5},{13,9},{2,14},{6,2},{... | collective-permute-start | bytes 786440 | tf_op jit(solution)/shard_map/ppermute | solution.py:500
  104.6 2.4 %place.7 = (bf16[12,16,5120]{2,1,0:T(8,128)(2,1)}, bf16[16,16,5120]{2,1,0:T(8,128)(2,1)}, bf16[28,16,2304]{2,1,0:T(8,128)(2,1)}) custom-call(s32[1]{0:T(128)} %bitcast.1.refs_0_, s32[4]{0:T(128)} %refs_1_.35, s32[4]{0:T(128)} %refs_2_.35, s32[4,16]{1,0:T(4,128)} %refs_3_.35, ...), custom_call_target="tpu_custom_call", output_to_operand_aliasing={{0}: (9, {}), {1}: (10, {}), {2}: (11, {})} | custom-call | flops 8625000448 | tf_op jit(solution)/shard_map/place/pallas_call | solution.py:429
  106.9 1.8 %collective-permute-done.17.refs_6_ = bf16[4,2,8,16,128]{4,3,2,1,0:T(8,128)(2,1)} collective-permute-done((bf16[4,2,8,16,128]{4,3,2,1,0:T(8,128)(2,1)}, bf16[4,2,8,16,128]{4,3,2,1,0:T(8,128)(2,1)}, u32[]{:S(2)}, u32[]{:S(2)}) %collective-permute-start.17) | collective-permute-done | bytes 262176 | tf_op jit(solution)/shard_map/ppermute | solution.py:500
  108.8 2.1 %stage.19 = (bf16[4,2,12,16,128]{4,3,2,1,0:T(8,128)(2,1)}, bf16[4,2,5,16,128]{4,3,2,1,0:T(8,128)(2,1)}, bf16[4,2,3,16,128]{4,3,2,1,0:T(8,128)(2,1)}, bf16[4,2,8,16,128]{4,3,2,1,0:T(8,128)(2,1)}) custom-call(s32[1]{0:T(128)} %bitcast.1.refs_0_, s32[4]{0:T(128)} %refs_1_.35, s32[4]{0:T(128)} %refs_2_.35, s32[4,16]{1,0:T(4,128)} %refs_3_.35, ...), custom_call_target="tpu_custom_call" | custom-call | tf_op jit(solution)/shard_map/stage/pallas_call | solution.py:378
  110.9 4.4 %collective-permute-start.25 = (bf16[4,2,8,16,128]{4,3,2,1,0:T(8,128)(2,1)}, bf16[4,2,8,16,128]{4,3,2,1,0:T(8,128)(2,1)}, u32[]{:S(2)}, u32[]{:S(2)}) collective-permute-start(bf16[4,2,8,16,128]{4,3,2,1,0:T(8,128)(2,1)} %get-tuple-element.174), channel_id=1, source_target_pairs={{0,12},{4,0},{8,4},{12,8},{1,13},{5,1},{9,5},{13,9},{2,14},{6,2},{... | collective-permute-start | bytes 786440 | tf_op jit(solution)/shard_map/ppermute | solution.py:500
  117.8 5.9 %stage.20 = (bf16[4,2,16,16,128]{4,3,2,1,0:T(8,128)(2,1)}, bf16[4,2,8,16,128]{4,3,2,1,0:T(8,128)(2,1)}) custom-call(s32[1]{0:T(128)} %bitcast.1.refs_0_, s32[4]{0:T(128)} %refs_1_.35, s32[4]{0:T(128)} %refs_2_.35, s32[4,16]{1,0:T(4,128)} %refs_3_.35, s32[1]{0:T(128)} %bitcast.near_ref.refs_4_, bf16[20,16,16,128]{3,2,1,0:T(8,128)(2,1)} %get-tuple-element.169.refs_5_, ...), custom_call_target="tpu_custom_call" | custom-call | tf_op jit(solution)/shard_map/stage/pallas_call | solution.py:378
  123.6 3.5 %collective-permute-start.33 = (bf16[4,2,5,16,128]{4,3,2,1,0:T(8,128)(2,1)}, bf16[4,2,5,16,128]{4,3,2,1,0:T(8,128)(2,1)}, u32[]{:S(2)}, u32[]{:S(2)}) collective-permute-start(bf16[4,2,5,16,128]{4,3,2,1,0:T(8,128)(2,1)} %get-tuple-element.192), channel_id=1, source_target_pairs={{0,4},{4,8},{8,12},{12,0},{1,5},{5,9},{9,13},{13,1},{2,6},{6,10},{... | collective-permute-start | bytes 491528 | tf_op jit(solution)/shard_map/ppermute | solution.py:500
  129.6 2.4 %place.8 = (bf16[12,16,5120]{2,1,0:T(8,128)(2,1)}, bf16[16,16,5120]{2,1,0:T(8,128)(2,1)}, bf16[28,16,2304]{2,1,0:T(8,128)(2,1)}) custom-call(s32[1]{0:T(128)} %bitcast.1.refs_0_, s32[4]{0:T(128)} %refs_1_.35, s32[4]{0:T(128)} %refs_2_.35, s32[4,16]{1,0:T(4,128)} %refs_3_.35, ...), custom_call_target="tpu_custom_call", output_to_operand_aliasing={{0}: (9, {}), {1}: (10, {}), {2}: (11, {})} | custom-call | flops 8625000448 | tf_op jit(solution)/shard_map/place/pallas_call | solution.py:429
  132.0 3.9 %stage.21 = (bf16[2,2,16,16,128]{4,3,2,1,0:T(8,128)(2,1)}, bf16[2,2,8,16,128]{4,3,2,1,0:T(8,128)(2,1)}) custom-call(s32[1]{0:T(128)} %bitcast.1.refs_0_, s32[4]{0:T(128)} %refs_1_.35, s32[4]{0:T(128)} %refs_2_.35, s32[4,16]{1,0:T(4,128)} %refs_3_.35, s32[1]{0:T(128)} %bitcast.near_ref.refs_4_, bf16[20,16,16,128]{3,2,1,0:T(8,128)(2,1)} %get-tuple-element.169.refs_5_, ...), custom_call_target="tpu_custom_call" | custom-call | tf_op jit(solution)/shard_map/stage/pallas_call | solution.py:378
  135.9 1.9 %collective-permute-start.24 = (bf16[2,2,8,16,128]{4,3,2,1,0:T(8,128)(2,1)}, bf16[2,2,8,16,128]{4,3,2,1,0:T(8,128)(2,1)}, u32[]{:S(2)}, u32[]{:S(2)}) collective-permute-start(bf16[2,2,8,16,128]{4,3,2,1,0:T(8,128)(2,1)} %get-tuple-element.172), channel_id=1, source_target_pairs={{0,12},{4,0},{8,4},{12,8},{1,13},{5,1},{9,5},{13,9},{2,14},{6,2},{... | collective-permute-start | bytes 393224 | tf_op jit(solution)/shard_map/ppermute | solution.py:500
  139.0 2.1 %stage.22 = (bf16[4,2,12,16,128]{4,3,2,1,0:T(8,128)(2,1)}, bf16[4,2,5,16,128]{4,3,2,1,0:T(8,128)(2,1)}, bf16[4,2,3,16,128]{4,3,2,1,0:T(8,128)(2,1)}, bf16[4,2,8,16,128]{4,3,2,1,0:T(8,128)(2,1)}) custom-call(s32[1]{0:T(128)} %bitcast.1.refs_0_, s32[4]{0:T(128)} %refs_1_.35, s32[4]{0:T(128)} %refs_2_.35, s32[4,16]{1,0:T(4,128)} %refs_3_.35, ...), custom_call_target="tpu_custom_call" | custom-call | tf_op jit(solution)/shard_map/stage/pallas_call | solution.py:378
  141.2 2.5 %collective-permute-start.27 = (bf16[4,2,5,16,128]{4,3,2,1,0:T(8,128)(2,1)}, bf16[4,2,5,16,128]{4,3,2,1,0:T(8,128)(2,1)}, u32[]{:S(2)}, u32[]{:S(2)}) collective-permute-start(bf16[4,2,5,16,128]{4,3,2,1,0:T(8,128)(2,1)} %get-tuple-element.181), channel_id=1, source_target_pairs={{0,4},{4,8},{8,12},{12,0},{1,5},{5,9},{9,13},{13,1},{2,6},{6,10},{... | collective-permute-start | bytes 491528 | tf_op jit(solution)/shard_map/ppermute | solution.py:500
  143.7 2.4 %collective-permute-start.31 = (bf16[4,2,8,16,128]{4,3,2,1,0:T(8,128)(2,1)}, bf16[4,2,8,16,128]{4,3,2,1,0:T(8,128)(2,1)}, u32[]{:S(2)}, u32[]{:S(2)}) collective-permute-start(bf16[4,2,8,16,128]{4,3,2,1,0:T(8,128)(2,1)} %get-tuple-element.187), channel_id=1, source_target_pairs={{0,12},{4,0},{8,4},{12,8},{1,13},{5,1},{9,5},{13,9},{2,14},{6,2},{... | collective-permute-start | bytes 786440 | tf_op jit(solution)/shard_map/ppermute | solution.py:500
  146.1 2.4 %place.9 = (bf16[12,16,5120]{2,1,0:T(8,128)(2,1)}, bf16[16,16,5120]{2,1,0:T(8,128)(2,1)}, bf16[28,16,2304]{2,1,0:T(8,128)(2,1)}) custom-call(s32[1]{0:T(128)} %bitcast.1.refs_0_, s32[4]{0:T(128)} %refs_1_.35, s32[4]{0:T(128)} %refs_2_.35, s32[4,16]{1,0:T(4,128)} %refs_3_.35, ...), custom_call_target="tpu_custom_call", output_to_operand_aliasing={{0}: (9, {}), {1}: (10, {}), {2}: (11, {})} | custom-call | flops 8625000448 | tf_op jit(solution)/shard_map/place/pallas_call | solution.py:429
  148.5 1.9 %stage.23 = (bf16[2,2,12,16,128]{4,3,2,1,0:T(8,128)(2,1)}, bf16[2,2,5,16,128]{4,3,2,1,0:T(8,128)(2,1)}, bf16[2,2,3,16,128]{4,3,2,1,0:T(8,128)(2,1)}, bf16[2,2,8,16,128]{4,3,2,1,0:T(8,128)(2,1)}) custom-call(s32[1]{0:T(128)} %bitcast.1.refs_0_, s32[4]{0:T(128)} %refs_1_.35, s32[4]{0:T(128)} %refs_2_.35, s32[4,16]{1,0:T(4,128)} %refs_3_.35, ...), custom_call_target="tpu_custom_call" | custom-call | tf_op jit(solution)/shard_map/stage/pallas_call | solution.py:378
  150.8 1.7 collective-permute-done.31.refs_8_
  152.5 2.4 %place.10 = (bf16[12,16,5120]{2,1,0:T(8,128)(2,1)}, bf16[16,16,5120]{2,1,0:T(8,128)(2,1)}, bf16[28,16,2304]{2,1,0:T(8,128)(2,1)}) custom-call(s32[1]{0:T(128)} %bitcast.1.refs_0_, s32[4]{0:T(128)} %refs_1_.35, s32[4]{0:T(128)} %refs_2_.35, s32[4,16]{1,0:T(4,128)} %refs_3_.35, ...), custom_call_target="tpu_custom_call", output_to_operand_aliasing={{0}: (9, {}), {1}: (10, {}), {2}: (11, {})} | custom-call | flops 8625000448 | tf_op jit(solution)/shard_map/place/pallas_call | solution.py:429
  155.0 3.5 %collective-permute-start.32 = (bf16[2,2,8,16,128]{4,3,2,1,0:T(8,128)(2,1)}, bf16[2,2,8,16,128]{4,3,2,1,0:T(8,128)(2,1)}, u32[]{:S(2)}, u32[]{:S(2)}) collective-permute-start(bf16[2,2,8,16,128]{4,3,2,1,0:T(8,128)(2,1)} %get-tuple-element.188), channel_id=1, source_target_pairs={{0,12},{4,0},{8,4},{12,8},{1,13},{5,1},{9,5},{13,9},{2,14},{6,2},{... | collective-permute-start | bytes 393224 | tf_op jit(solution)/shard_map/ppermute | solution.py:500
  159.4 2.9 %finish.2 = (bf16[12,16,5120]{2,1,0:T(8,128)(2,1)}, bf16[16,16,5120]{2,1,0:T(8,128)(2,1)}) custom-call(s32[1]{0:T(128)} %bitcast.near_ref.refs_4_, bf16[28,16,2304]{2,1,0:T(8,128)(2,1)} %collective-permute-done.35.refs_0_, bf16[12,16,5120]{2,1,0:T(8,128)(2,1)} %get-tuple-element.201.refs_1_, ...), custom_call_target="tpu_custom_call", output_to_operand_aliasing={{0}: (2, {}), {1}: (3, {})} | custom-call | tf_op jit(solution)/shard_map/finish/pallas_call | solution.py:478
  162.3 4.2 %collective-permute-done.30.refs_7_ = bf16[2,2,3,16,128]{4,3,2,1,0:T(8,128)(2,1)} collective-permute-done((bf16[2,2,3,16,128]{4,3,2,1,0:T(8,128)(2,1)}, bf16[2,2,3,16,128]{4,3,2,1,0:T(8,128)(2,1)}, u32[]{:S(2)}, u32[]{:S(2)}) %collective-permute-start.30) | collective-permute-done | bytes 49184 | tf_op jit(solution)/shard_map/ppermute | solution.py:500
  166.6 2.0 %place.11 = (bf16[12,16,5120]{2,1,0:T(8,128)(2,1)}, bf16[16,16,5120]{2,1,0:T(8,128)(2,1)}, bf16[28,16,256]{2,1,0:T(8,128)(2,1)}) custom-call(s32[1]{0:T(128)} %bitcast.1.refs_0_, s32[4]{0:T(128)} %refs_1_.35, s32[4]{0:T(128)} %refs_2_.35, s32[4,16]{1,0:T(4,128)} %refs_3_.35, s32[1]{0:T(128)} %bitcast.near_ref.refs_4_, ...), custom_call_target="tpu_custom_call", output_to_operand_aliasing={{0}: (9, {}), {1}: (10, {})} | custom-call | tf_op jit(solution)/shard_map/place/pallas_call | solution.py:429
  168.7 1.8 %collective-permute-done.36.refs_0_ = bf16[28,16,256]{2,1,0:T(8,128)(2,1)} collective-permute-done((bf16[28,16,256]{2,1,0:T(8,128)(2,1)}, bf16[28,16,256]{2,1,0:T(8,128)(2,1)}, u32[]{:S(2)}, u32[]{:S(2)}) %collective-permute-start.36) | collective-permute-done | bytes 229408 | tf_op jit(solution)/shard_map/ppermute | solution.py:495
  170.5 1.6 finish.3
  (51 shorter events, 16.5 us)
Async XLA Ops:
  5.8 2.0 %collective-permute-start = (bf16[2,2,16,16,128]{4,3,2,1,0:T(8,128)(2,1)}, bf16[2,2,16,16,128]{4,3,2,1,0:T(8,128)(2,1)}, u32[]{:S(2)}, u32[]{:S(2)}) collective-permute-start(bf16[2,2,16,16,128]{4,3,2,1,0:T(8,128)(2,1)} %get-tuple-element.107), channel_id=1, source_target_pairs={{0,1},{1,0},{2,3},{3,2},{4,5},{5,4},{6,7},{7,6},{8,9},{9,8},{10,11... | collective-permute-start | bytes 786440 | tf_op jit(solution)/shard_map/ppermute | solution.py:495
  9.7 15.9 %collective-permute-start.3 = (bf16[2,2,2,16,16,128]{5,4,3,2,1,0:T(8,128)(2,1)}, bf16[2,2,2,16,16,128]{5,4,3,2,1,0:T(8,128)(2,1)}, u32[]{:S(2)}, u32[]{:S(2)}) collective-permute-start(bf16[2,2,2,16,16,128]{5,4,3,2,1,0:T(8,128)(2,1)} %join_halves.3.refs_7_), channel_id=1, source_target_pairs={{0,2},{1,3},{2,0},{3,1},{4,6},{5,7},{6,4},{7,5},{8,10},{9,11},{10,... | collective-permute-start | bytes 1572872 | tf_op jit(solution)/shard_map/ppermute | solution.py:495
  12.5 4.2 %collective-permute-start.1 = (bf16[4,2,16,16,128]{4,3,2,1,0:T(8,128)(2,1)}, bf16[4,2,16,16,128]{4,3,2,1,0:T(8,128)(2,1)}, u32[]{:S(2)}, u32[]{:S(2)}) collective-permute-start(bf16[4,2,16,16,128]{4,3,2,1,0:T(8,128)(2,1)} %get-tuple-element.111), channel_id=1, source_target_pairs={{0,1},{1,0},{2,3},{3,2},{4,5},{5,4},{6,7},{7,6},{8,9},{9,8},{10,11... | collective-permute-start | bytes 1572872 | tf_op jit(solution)/shard_map/ppermute | solution.py:495
  12.5 25.8 %collective-permute-start.9 = (bf16[14,2,16,16,128]{4,3,2,1,0:T(8,128)(2,1)}, bf16[14,2,16,16,128]{4,3,2,1,0:T(8,128)(2,1)}, u32[]{:S(2)}, u32[]{:S(2)}) collective-permute-start(bf16[14,2,16,16,128]{4,3,2,1,0:T(8,128)(2,1)} %get-tuple-element.127), channel_id=1, source_target_pairs={{0,1},{1,0},{2,3},{3,2},{4,5},{5,4},{6,7},{7,6},{8,9},{9,8},{10,11... | collective-permute-start | bytes 5505032 | tf_op jit(solution)/shard_map/ppermute | solution.py:495
  16.7 33.7 %collective-permute-start.5 = (bf16[18,16,16,128]{3,2,1,0:T(8,128)(2,1)}, bf16[18,16,16,128]{3,2,1,0:T(8,128)(2,1)}, u32[]{:S(2)}, u32[]{:S(2)}) collective-permute-start(bf16[18,16,16,128]{3,2,1,0:T(8,128)(2,1)} %get-tuple-element.119), channel_id=1, source_target_pairs={{0,1},{1,0},{2,3},{3,2},{4,5},{5,4},{6,7},{7,6},{8,9},{9,8},{10,11... | collective-permute-start | bytes 3538952 | tf_op jit(solution)/shard_map/ppermute | solution.py:495
  18.9 31.5 %collective-permute-start.6 = (bf16[4,2,2,16,16,128]{5,4,3,2,1,0:T(8,128)(2,1)}, bf16[4,2,2,16,16,128]{5,4,3,2,1,0:T(8,128)(2,1)}, u32[]{:S(2)}, u32[]{:S(2)}) collective-permute-start(bf16[4,2,2,16,16,128]{5,4,3,2,1,0:T(8,128)(2,1)} %join_halves.4.refs_7_), channel_id=1, source_target_pairs={{0,2},{1,3},{2,0},{3,1},{4,6},{5,7},{6,4},{7,5},{8,10},{9,11},{10,... | collective-permute-start | bytes 3145736 | tf_op jit(solution)/shard_map/ppermute | solution.py:495
  19.0 1.7 collective-permute-start.2
  29.4 7.0 %collective-permute-start.4 = (bf16[2,2,8,16,128]{4,3,2,1,0:T(8,128)(2,1)}, bf16[2,2,8,16,128]{4,3,2,1,0:T(8,128)(2,1)}, u32[]{:S(2)}, u32[]{:S(2)}) collective-permute-start(bf16[2,2,8,16,128]{4,3,2,1,0:T(8,128)(2,1)} %get-tuple-element.116), channel_id=1, source_target_pairs={{0,12},{4,0},{8,4},{12,8},{1,13},{5,1},{9,5},{13,9},{2,14},{6,2},{... | collective-permute-start | bytes 393224 | tf_op jit(solution)/shard_map/ppermute | solution.py:500
  44.7 26.5 %collective-permute-start.10 = (bf16[4,2,2,16,16,128]{5,4,3,2,1,0:T(8,128)(2,1)}, bf16[4,2,2,16,16,128]{5,4,3,2,1,0:T(8,128)(2,1)}, u32[]{:S(2)}, u32[]{:S(2)}) collective-permute-start(bf16[4,2,2,16,16,128]{5,4,3,2,1,0:T(8,128)(2,1)} %get-tuple-element.129.refs_7_), channel_id=1, source_target_pairs={{0,2},{1,3},{2,0},{3,1},{4,6},{5,7},{6,4},{7,5},{8,10},{9,11},{10,... | collective-permute-start | bytes 3145736 | tf_op jit(solution)/shard_map/ppermute | solution.py:495
  46.2 10.1 %collective-permute-start.7 = (bf16[2,2,8,16,128]{4,3,2,1,0:T(8,128)(2,1)}, bf16[2,2,8,16,128]{4,3,2,1,0:T(8,128)(2,1)}, u32[]{:S(2)}, u32[]{:S(2)}) collective-permute-start(bf16[2,2,8,16,128]{4,3,2,1,0:T(8,128)(2,1)} %get-tuple-element.122), channel_id=1, source_target_pairs={{0,12},{4,0},{8,4},{12,8},{1,13},{5,1},{9,5},{13,9},{2,14},{6,2},{... | collective-permute-start | bytes 393224 | tf_op jit(solution)/shard_map/ppermute | solution.py:500
  56.3 6.7 %collective-permute-start.8 = (bf16[4,2,8,16,128]{4,3,2,1,0:T(8,128)(2,1)}, bf16[4,2,8,16,128]{4,3,2,1,0:T(8,128)(2,1)}, u32[]{:S(2)}, u32[]{:S(2)}) collective-permute-start(bf16[4,2,8,16,128]{4,3,2,1,0:T(8,128)(2,1)} %get-tuple-element.123), channel_id=1, source_target_pairs={{0,12},{4,0},{8,4},{12,8},{1,13},{5,1},{9,5},{13,9},{2,14},{6,2},{... | collective-permute-start | bytes 786440 | tf_op jit(solution)/shard_map/ppermute | solution.py:500
  65.2 12.0 %collective-permute-start.11 = (bf16[4,2,8,16,128]{4,3,2,1,0:T(8,128)(2,1)}, bf16[4,2,8,16,128]{4,3,2,1,0:T(8,128)(2,1)}, u32[]{:S(2)}, u32[]{:S(2)}) collective-permute-start(bf16[4,2,8,16,128]{4,3,2,1,0:T(8,128)(2,1)} %get-tuple-element.132), channel_id=1, source_target_pairs={{0,12},{4,0},{8,4},{12,8},{1,13},{5,1},{9,5},{13,9},{2,14},{6,2},{... | collective-permute-start | bytes 786440 | tf_op jit(solution)/shard_map/ppermute | solution.py:500
  69.1 11.7 %collective-permute-start.13 = (bf16[2,2,5,16,128]{4,3,2,1,0:T(8,128)(2,1)}, bf16[2,2,5,16,128]{4,3,2,1,0:T(8,128)(2,1)}, u32[]{:S(2)}, u32[]{:S(2)}) collective-permute-start(bf16[2,2,5,16,128]{4,3,2,1,0:T(8,128)(2,1)} %get-tuple-element.136), channel_id=1, source_target_pairs={{0,4},{4,8},{8,12},{12,0},{1,5},{5,9},{9,13},{13,1},{2,6},{6,10},{... | collective-permute-start | bytes 245768 | tf_op jit(solution)/shard_map/ppermute | solution.py:500
  69.1 11.6 %collective-permute-start.14 = (bf16[2,2,3,16,128]{4,3,2,1,0:T(8,128)(2,1)}, bf16[2,2,3,16,128]{4,3,2,1,0:T(8,128)(2,1)}, u32[]{:S(2)}, u32[]{:S(2)}) collective-permute-start(bf16[2,2,3,16,128]{4,3,2,1,0:T(8,128)(2,1)} %get-tuple-element.138), channel_id=1, source_target_pairs={{0,8},{4,12},{8,0},{12,4},{1,9},{5,13},{9,1},{13,5},{2,10},{6,14},... | collective-permute-start | bytes 147464 | tf_op jit(solution)/shard_map/ppermute | solution.py:500
  69.7 24.2 %collective-permute-start.15 = (bf16[4,2,2,16,16,128]{5,4,3,2,1,0:T(8,128)(2,1)}, bf16[4,2,2,16,16,128]{5,4,3,2,1,0:T(8,128)(2,1)}, u32[]{:S(2)}, u32[]{:S(2)}) collective-permute-start(bf16[4,2,2,16,16,128]{5,4,3,2,1,0:T(8,128)(2,1)} %get-tuple-element.143.refs_7_), channel_id=1, source_target_pairs={{0,2},{1,3},{2,0},{3,1},{4,6},{5,7},{6,4},{7,5},{8,10},{9,11},{10,... | collective-permute-start | bytes 3145736 | tf_op jit(solution)/shard_map/ppermute | solution.py:495
  77.1 8.5 %collective-permute-start.12 = (bf16[4,2,8,16,128]{4,3,2,1,0:T(8,128)(2,1)}, bf16[4,2,8,16,128]{4,3,2,1,0:T(8,128)(2,1)}, u32[]{:S(2)}, u32[]{:S(2)}) collective-permute-start(bf16[4,2,8,16,128]{4,3,2,1,0:T(8,128)(2,1)} %get-tuple-element.133), channel_id=1, source_target_pairs={{0,12},{4,0},{8,4},{12,8},{1,13},{5,1},{9,5},{13,9},{2,14},{6,2},{... | collective-permute-start | bytes 786440 | tf_op jit(solution)/shard_map/ppermute | solution.py:500
  87.7 12.1 %collective-permute-start.16 = (bf16[4,2,8,16,128]{4,3,2,1,0:T(8,128)(2,1)}, bf16[4,2,8,16,128]{4,3,2,1,0:T(8,128)(2,1)}, u32[]{:S(2)}, u32[]{:S(2)}) collective-permute-start(bf16[4,2,8,16,128]{4,3,2,1,0:T(8,128)(2,1)} %get-tuple-element.146), channel_id=1, source_target_pairs={{0,12},{4,0},{8,4},{12,8},{1,13},{5,1},{9,5},{13,9},{2,14},{6,2},{... | collective-permute-start | bytes 786440 | tf_op jit(solution)/shard_map/ppermute | solution.py:500
  91.4 13.1 %collective-permute-start.18 = (bf16[4,2,5,16,128]{4,3,2,1,0:T(8,128)(2,1)}, bf16[4,2,5,16,128]{4,3,2,1,0:T(8,128)(2,1)}, u32[]{:S(2)}, u32[]{:S(2)}) collective-permute-start(bf16[4,2,5,16,128]{4,3,2,1,0:T(8,128)(2,1)} %get-tuple-element.150), channel_id=1, source_target_pairs={{0,4},{4,8},{8,12},{12,0},{1,5},{5,9},{9,13},{13,1},{2,6},{6,10},{... | collective-permute-start | bytes 491528 | tf_op jit(solution)/shard_map/ppermute | solution.py:500
  91.4 13.1 %collective-permute-start.19 = (bf16[4,2,3,16,128]{4,3,2,1,0:T(8,128)(2,1)}, bf16[4,2,3,16,128]{4,3,2,1,0:T(8,128)(2,1)}, u32[]{:S(2)}, u32[]{:S(2)}) collective-permute-start(bf16[4,2,3,16,128]{4,3,2,1,0:T(8,128)(2,1)} %get-tuple-element.152), channel_id=1, source_target_pairs={{0,8},{4,12},{8,0},{12,4},{1,9},{5,13},{9,1},{13,5},{2,10},{6,14},... | collective-permute-start | bytes 294920 | tf_op jit(solution)/shard_map/ppermute | solution.py:500
  92.1 25.7 %collective-permute-start.20 = (bf16[4,2,2,16,16,128]{5,4,3,2,1,0:T(8,128)(2,1)}, bf16[4,2,2,16,16,128]{5,4,3,2,1,0:T(8,128)(2,1)}, u32[]{:S(2)}, u32[]{:S(2)}) collective-permute-start(bf16[4,2,2,16,16,128]{5,4,3,2,1,0:T(8,128)(2,1)} %get-tuple-element.159.refs_7_), channel_id=1, source_target_pairs={{0,2},{1,3},{2,0},{3,1},{4,6},{5,7},{6,4},{7,5},{8,10},{9,11},{10,... | collective-permute-start | bytes 3145736 | tf_op jit(solution)/shard_map/ppermute | solution.py:495
  99.8 9.0 %collective-permute-start.17 = (bf16[4,2,8,16,128]{4,3,2,1,0:T(8,128)(2,1)}, bf16[4,2,8,16,128]{4,3,2,1,0:T(8,128)(2,1)}, u32[]{:S(2)}, u32[]{:S(2)}) collective-permute-start(bf16[4,2,8,16,128]{4,3,2,1,0:T(8,128)(2,1)} %get-tuple-element.147), channel_id=1, source_target_pairs={{0,12},{4,0},{8,4},{12,8},{1,13},{5,1},{9,5},{13,9},{2,14},{6,2},{... | collective-permute-start | bytes 786440 | tf_op jit(solution)/shard_map/ppermute | solution.py:500
  110.9 16.2 %collective-permute-start.25 = (bf16[4,2,8,16,128]{4,3,2,1,0:T(8,128)(2,1)}, bf16[4,2,8,16,128]{4,3,2,1,0:T(8,128)(2,1)}, u32[]{:S(2)}, u32[]{:S(2)}) collective-permute-start(bf16[4,2,8,16,128]{4,3,2,1,0:T(8,128)(2,1)} %get-tuple-element.174), channel_id=1, source_target_pairs={{0,12},{4,0},{8,4},{12,8},{1,13},{5,1},{9,5},{13,9},{2,14},{6,2},{... | collective-permute-start | bytes 786440 | tf_op jit(solution)/shard_map/ppermute | solution.py:500
  115.4 14.2 %collective-permute-start.21 = (bf16[4,2,5,16,128]{4,3,2,1,0:T(8,128)(2,1)}, bf16[4,2,5,16,128]{4,3,2,1,0:T(8,128)(2,1)}, u32[]{:S(2)}, u32[]{:S(2)}) collective-permute-start(bf16[4,2,5,16,128]{4,3,2,1,0:T(8,128)(2,1)} %get-tuple-element.163), channel_id=1, source_target_pairs={{0,4},{4,8},{8,12},{12,0},{1,5},{5,9},{9,13},{13,1},{2,6},{6,10},{... | collective-permute-start | bytes 491528 | tf_op jit(solution)/shard_map/ppermute | solution.py:500
  115.4 12.8 %collective-permute-start.22 = (bf16[4,2,3,16,128]{4,3,2,1,0:T(8,128)(2,1)}, bf16[4,2,3,16,128]{4,3,2,1,0:T(8,128)(2,1)}, u32[]{:S(2)}, u32[]{:S(2)}) collective-permute-start(bf16[4,2,3,16,128]{4,3,2,1,0:T(8,128)(2,1)} %get-tuple-element.165), channel_id=1, source_target_pairs={{0,8},{4,12},{8,0},{12,4},{1,9},{5,13},{9,1},{13,5},{2,10},{6,14},... | collective-permute-start | bytes 294920 | tf_op jit(solution)/shard_map/ppermute | solution.py:500
  116.0 16.0 %collective-permute-start.23 = (bf16[2,2,2,16,16,128]{5,4,3,2,1,0:T(8,128)(2,1)}, bf16[2,2,2,16,16,128]{5,4,3,2,1,0:T(8,128)(2,1)}, u32[]{:S(2)}, u32[]{:S(2)}) collective-permute-start(bf16[2,2,2,16,16,128]{5,4,3,2,1,0:T(8,128)(2,1)} %get-tuple-element.170.refs_7_), channel_id=1, source_target_pairs={{0,2},{1,3},{2,0},{3,1},{4,6},{5,7},{6,4},{7,5},{8,10},{9,11},{10,... | collective-permute-start | bytes 1572872 | tf_op jit(solution)/shard_map/ppermute | solution.py:495
  123.6 22.5 %collective-permute-start.33 = (bf16[4,2,5,16,128]{4,3,2,1,0:T(8,128)(2,1)}, bf16[4,2,5,16,128]{4,3,2,1,0:T(8,128)(2,1)}, u32[]{:S(2)}, u32[]{:S(2)}) collective-permute-start(bf16[4,2,5,16,128]{4,3,2,1,0:T(8,128)(2,1)} %get-tuple-element.192), channel_id=1, source_target_pairs={{0,4},{4,8},{8,12},{12,0},{1,5},{5,9},{9,13},{13,1},{2,6},{6,10},{... | collective-permute-start | bytes 491528 | tf_op jit(solution)/shard_map/ppermute | solution.py:500
  127.1 16.5 %collective-permute-start.34 = (bf16[4,2,3,16,128]{4,3,2,1,0:T(8,128)(2,1)}, bf16[4,2,3,16,128]{4,3,2,1,0:T(8,128)(2,1)}, u32[]{:S(2)}, u32[]{:S(2)}) collective-permute-start(bf16[4,2,3,16,128]{4,3,2,1,0:T(8,128)(2,1)} %get-tuple-element.194), channel_id=1, source_target_pairs={{0,8},{4,12},{8,0},{12,4},{1,9},{5,13},{9,1},{13,5},{2,10},{6,14},... | collective-permute-start | bytes 294920 | tf_op jit(solution)/shard_map/ppermute | solution.py:500
  128.1 10.9 %collective-permute-start.26 = (bf16[4,2,8,16,128]{4,3,2,1,0:T(8,128)(2,1)}, bf16[4,2,8,16,128]{4,3,2,1,0:T(8,128)(2,1)}, u32[]{:S(2)}, u32[]{:S(2)}) collective-permute-start(bf16[4,2,8,16,128]{4,3,2,1,0:T(8,128)(2,1)} %get-tuple-element.175), channel_id=1, source_target_pairs={{0,12},{4,0},{8,4},{12,8},{1,13},{5,1},{9,5},{13,9},{2,14},{6,2},{... | collective-permute-start | bytes 786440 | tf_op jit(solution)/shard_map/ppermute | solution.py:500
  135.9 12.6 %collective-permute-start.24 = (bf16[2,2,8,16,128]{4,3,2,1,0:T(8,128)(2,1)}, bf16[2,2,8,16,128]{4,3,2,1,0:T(8,128)(2,1)}, u32[]{:S(2)}, u32[]{:S(2)}) collective-permute-start(bf16[2,2,8,16,128]{4,3,2,1,0:T(8,128)(2,1)} %get-tuple-element.172), channel_id=1, source_target_pairs={{0,12},{4,0},{8,4},{12,8},{1,13},{5,1},{9,5},{13,9},{2,14},{6,2},{... | collective-permute-start | bytes 393224 | tf_op jit(solution)/shard_map/ppermute | solution.py:500
  141.2 9.7 %collective-permute-start.27 = (bf16[4,2,5,16,128]{4,3,2,1,0:T(8,128)(2,1)}, bf16[4,2,5,16,128]{4,3,2,1,0:T(8,128)(2,1)}, u32[]{:S(2)}, u32[]{:S(2)}) collective-permute-start(bf16[4,2,5,16,128]{4,3,2,1,0:T(8,128)(2,1)} %get-tuple-element.181), channel_id=1, source_target_pairs={{0,4},{4,8},{8,12},{12,0},{1,5},{5,9},{9,13},{13,1},{2,6},{6,10},{... | collective-permute-start | bytes 491528 | tf_op jit(solution)/shard_map/ppermute | solution.py:500
  143.7 7.2 %collective-permute-start.29 = (bf16[4,2,3,16,128]{4,3,2,1,0:T(8,128)(2,1)}, bf16[4,2,3,16,128]{4,3,2,1,0:T(8,128)(2,1)}, u32[]{:S(2)}, u32[]{:S(2)}) collective-permute-start(bf16[4,2,3,16,128]{4,3,2,1,0:T(8,128)(2,1)} %get-tuple-element.184), channel_id=1, source_target_pairs={{0,8},{4,12},{8,0},{12,4},{1,9},{5,13},{9,1},{13,5},{2,10},{6,14},... | collective-permute-start | bytes 294920 | tf_op jit(solution)/shard_map/ppermute | solution.py:500
  143.7 8.8 %collective-permute-start.31 = (bf16[4,2,8,16,128]{4,3,2,1,0:T(8,128)(2,1)}, bf16[4,2,8,16,128]{4,3,2,1,0:T(8,128)(2,1)}, u32[]{:S(2)}, u32[]{:S(2)}) collective-permute-start(bf16[4,2,8,16,128]{4,3,2,1,0:T(8,128)(2,1)} %get-tuple-element.187), channel_id=1, source_target_pairs={{0,12},{4,0},{8,4},{12,8},{1,13},{5,1},{9,5},{13,9},{2,14},{6,2},{... | collective-permute-start | bytes 786440 | tf_op jit(solution)/shard_map/ppermute | solution.py:500
  154.9 4.5 %collective-permute-start.35 = (bf16[28,16,2304]{2,1,0:T(8,128)(2,1)}, bf16[28,16,2304]{2,1,0:T(8,128)(2,1)}, u32[]{:S(2)}, u32[]{:S(2)}) collective-permute-start(bf16[28,16,2304]{2,1,0:T(8,128)(2,1)} %get-tuple-element.200), channel_id=1, source_target_pairs={{0,1},{1,0},{2,3},{3,2},{4,5},{5,4},{6,7},{7,6},{8,9},{9,8},{10,11... | collective-permute-start | bytes 6193160 | tf_op jit(solution)/shard_map/ppermute | solution.py:495
  155.0 11.6 %collective-permute-start.32 = (bf16[2,2,8,16,128]{4,3,2,1,0:T(8,128)(2,1)}, bf16[2,2,8,16,128]{4,3,2,1,0:T(8,128)(2,1)}, u32[]{:S(2)}, u32[]{:S(2)}) collective-permute-start(bf16[2,2,8,16,128]{4,3,2,1,0:T(8,128)(2,1)} %get-tuple-element.188), channel_id=1, source_target_pairs={{0,12},{4,0},{8,4},{12,8},{1,13},{5,1},{9,5},{13,9},{2,14},{6,2},{... | collective-permute-start | bytes 393224 | tf_op jit(solution)/shard_map/ppermute | solution.py:500
  158.4 8.1 %collective-permute-start.28 = (bf16[2,2,5,16,128]{4,3,2,1,0:T(8,128)(2,1)}, bf16[2,2,5,16,128]{4,3,2,1,0:T(8,128)(2,1)}, u32[]{:S(2)}, u32[]{:S(2)}) collective-permute-start(bf16[2,2,5,16,128]{4,3,2,1,0:T(8,128)(2,1)} %get-tuple-element.182), channel_id=1, source_target_pairs={{0,4},{4,8},{8,12},{12,0},{1,5},{5,9},{9,13},{13,1},{2,6},{6,10},{... | collective-permute-start | bytes 245768 | tf_op jit(solution)/shard_map/ppermute | solution.py:500
  158.4 8.1 %collective-permute-start.30 = (bf16[2,2,3,16,128]{4,3,2,1,0:T(8,128)(2,1)}, bf16[2,2,3,16,128]{4,3,2,1,0:T(8,128)(2,1)}, u32[]{:S(2)}, u32[]{:S(2)}) collective-permute-start(bf16[2,2,3,16,128]{4,3,2,1,0:T(8,128)(2,1)} %get-tuple-element.185), channel_id=1, source_target_pairs={{0,8},{4,12},{8,0},{12,4},{1,9},{5,13},{9,1},{13,5},{2,10},{6,14},... | collective-permute-start | bytes 147464 | tf_op jit(solution)/shard_map/ppermute | solution.py:500
  168.6 1.9 %collective-permute-start.36 = (bf16[28,16,256]{2,1,0:T(8,128)(2,1)}, bf16[28,16,256]{2,1,0:T(8,128)(2,1)}, u32[]{:S(2)}, u32[]{:S(2)}) collective-permute-start(bf16[28,16,256]{2,1,0:T(8,128)(2,1)} %get-tuple-element.205), channel_id=1, source_target_pairs={{0,1},{1,0},{2,3},{3,2},{4,5},{5,4},{6,7},{7,6},{8,9},{9,8},{10,11... | collective-permute-start | bytes 688136 | tf_op jit(solution)/shard_map/ppermute | solution.py:495

commit v5 on v4

--- a/solution.py
+++ b/solution.py
@@ -43,7 +43,7 @@
 BLEND_COST = 0.0
 SWAP = 1
 PLACE_COST = 7.5
-TAIL_COST = 0.0
+TAIL_COST = 1.5
 LATE_CHUNKS = 1
 FREE = 1
 P3_TIE = 0

time: 173 us -> 172 us (level)
  transfers between devices with their start and end apart: 37 -> 37, of which waited for: 15 -> 15; matrix products, arithmetic and copies ran while one was open for 0% -> 0% of each run, Pallas kernels for 39% -> 40%
where the time goes in v5:
time: 172 us
  Pallas kernels  80.9 us (47%)
  starting transfers between devices  60.4 us (35%)
  waiting for transfers between devices  29.4 us (17%)
    ppermute x24, starting transfers between devices, shift(): lax.ppermute(array, 'win', [(i, (i + step) % count) for i in range(count)])  49.9 us
    pallas_call x12, Pallas kernels, run_stage(): pl.pallas_call(kernel, grid=(steps,), in_specs=[SMEM for _ in tables] + [...  43.6 us
    ppermute x24, waiting for transfers between devices, shift(): lax.ppermute(array, 'win', [(i, (i + step) % count) for i in range(count)])  19.2 us
    pallas_call x6, Pallas kernels, place(): pl.pallas_call(kernel, grid=(1,), in_specs=[SMEM for _ in tables] + [firs...  13.5 us
    ppermute x13, starting transfers between devices, exchange(): lax.ppermute(array, 'uly', [(i, i ^ bit) for i in range(lax.axis_size('ul...  10.4 us
    pallas_call x3, Pallas kernels, join_halves(): pl.pallas_call(kernel, grid=(sum(counts) // STEP_HEADS,), in_specs=[pl.Bl...  10.4 us
    ppermute x13, waiting for transfers between devices, exchange(): lax.ppermute(array, 'uly', [(i, i ^ bit) for i in range(lax.axis_size('ul...  10.2 us
    pallas_call x2, Pallas kernels, split_heads(): pl.pallas_call(kernel, grid=(frames // frames_per_step,), in_specs=[SMEM,...  8.88 us
  transfers between devices with their start and end apart: 37, of which 15 were waited for; matrix products, arithmetic and copies ran while one was open for 0% of the time, Pallas kernels for 40%

profile of v5, /device:TPU:0, one launch (start us, length us, event | category | flops | bytes accessed | tf_op | source)
XLA Modules:
  0.0 171.7 jit_solution(5382700088696049644)
XLA Ops:
  0.6 5.2 %norm_split.2 = (bf16[20,2,16,16,128]{4,3,2,1,0:T(8,128)(2,1)}, bf16[2,2,16,16,128]{4,3,2,1,0:T(8,128)(2,1)}, bf16[4,2,16,16,128]{4,3,2,1,0:T(8,128)(2,1)}, bf16[14,2,16,16,128]{4,3,2,1,0:T(8,128)(2,1)}) custom-call(s32[1]{0:T(128)} %bitcast.near_ref.refs_4_, bf16[16,16,5120]{2,1,0:T(8,128)(2,1)} %bitcast.9, f32[1,1,5120]{2,1,0:T(1,128)} %bitcast.12, ...), custom_call_target="tpu_custom_call" | custom-call | flops 10005000192 | tf_op jit(solution)/shard_map/norm_split/pallas_call | solution.py:98
  6.3 1.5 collective-permute-done.other_ref
  7.8 1.9 %join_halves.3.refs_7_ = bf16[2,2,2,16,16,128]{5,4,3,2,1,0:T(8,128)(2,1)} custom-call(bf16[20,2,16,16,128]{4,3,2,1,0:T(8,128)(2,1)} %get-tuple-element.106.own_ref, bf16[2,2,16,16,128]{4,3,2,1,0:T(8,128)(2,1)} %collective-permute-done.other_ref), custom_call_target="tpu_custom_call" | custom-call | flops 10005000192 | tf_op jit(solution)/shard_map/join_halves/pallas_call | solution.py:133
  9.7 2.9 %collective-permute-start.3 = (bf16[2,2,2,16,16,128]{5,4,3,2,1,0:T(8,128)(2,1)}, bf16[2,2,2,16,16,128]{5,4,3,2,1,0:T(8,128)(2,1)}, u32[]{:S(2)}, u32[]{:S(2)}) collective-permute-start(bf16[2,2,2,16,16,128]{5,4,3,2,1,0:T(8,128)(2,1)} %join_halves.3.refs_7_), channel_id=1, source_target_pairs={{0,2},{1,3},{2,0},{3,1},{4,6},{5,7},{6,4},{7,5},{8,10},{9,11},{10,... | collective-permute-start | bytes 1572872 | tf_op jit(solution)/shard_map/ppermute | solution.py:495
  13.0 3.7 %norm_split.3 = (bf16[20,16,16,128]{3,2,1,0:T(8,128)(2,1)}, bf16[2,16,16,128]{3,2,1,0:T(8,128)(2,1)}, bf16[18,16,16,128]{3,2,1,0:T(8,128)(2,1)}) custom-call(s32[1]{0:T(128)} %bitcast.near_ref.refs_4_, bf16[16,16,5120]{2,1,0:T(8,128)(2,1)} %bitcast.11, f32[1,1,5120]{2,1,0:T(1,128)} %bitcast.13), custom_call_target="tpu_custom_call" | custom-call | flops 10005000192 | tf_op jit(solution)/shard_map/norm_split/pallas_call | solution.py:98
  16.7 2.2 %join_halves.4.refs_7_ = bf16[4,2,2,16,16,128]{5,4,3,2,1,0:T(8,128)(2,1)} custom-call(bf16[20,2,16,16,128]{4,3,2,1,0:T(8,128)(2,1)} %get-tuple-element.106.own_ref, bf16[4,2,16,16,128]{4,3,2,1,0:T(8,128)(2,1)} %collective-permute-done.1.other_ref), custom_call_target="tpu_custom_call" | custom-call | flops 10005000192 | tf_op jit(solution)/shard_map/join_halves/pallas_call | solution.py:133
  20.7 4.8 %collective-permute-done.3.refs_8_ = bf16[2,2,2,16,16,128]{5,4,3,2,1,0:T(8,128)(2,1)} collective-permute-done((bf16[2,2,2,16,16,128]{5,4,3,2,1,0:T(8,128)(2,1)}, bf16[2,2,2,16,16,128]{5,4,3,2,1,0:T(8,128)(2,1)}, u32[]{:S(2)}, u32[]{:S(2)}) %collective-permute-start.3) | collective-permute-done | bytes 524320 | tf_op jit(solution)/shard_map/ppermute | solution.py:495
  25.5 3.9 %stage.12 = (bf16[2,2,16,16,128]{4,3,2,1,0:T(8,128)(2,1)}, bf16[2,2,8,16,128]{4,3,2,1,0:T(8,128)(2,1)}) custom-call(s32[1]{0:T(128)} %bitcast.1.refs_0_, s32[4]{0:T(128)} %refs_1_.35, s32[4]{0:T(128)} %refs_2_.35, s32[4,16]{1,0:T(4,128)} %refs_3_.35, s32[1]{0:T(128)} %bitcast.near_ref.refs_4_, bf16[20,16,16,128]{3,2,1,0:T(8,128)(2,1)} %get-tuple-element.169.refs_5_, ...), custom_call_target="tpu_custom_call" | custom-call | tf_op jit(solution)/shard_map/stage/pallas_call | solution.py:378
  29.4 4.2 %collective-permute-start.4 = (bf16[2,2,8,16,128]{4,3,2,1,0:T(8,128)(2,1)}, bf16[2,2,8,16,128]{4,3,2,1,0:T(8,128)(2,1)}, u32[]{:S(2)}, u32[]{:S(2)}) collective-permute-start(bf16[2,2,8,16,128]{4,3,2,1,0:T(8,128)(2,1)} %get-tuple-element.116), channel_id=1, source_target_pairs={{0,12},{4,0},{8,4},{12,8},{1,13},{5,1},{9,5},{13,9},{2,14},{6,2},{... | collective-permute-start | bytes 393224 | tf_op jit(solution)/shard_map/ppermute | solution.py:500
  33.6 2.8 %collective-permute-done.4.refs_6_ = bf16[2,2,8,16,128]{4,3,2,1,0:T(8,128)(2,1)} collective-permute-done((bf16[2,2,8,16,128]{4,3,2,1,0:T(8,128)(2,1)}, bf16[2,2,8,16,128]{4,3,2,1,0:T(8,128)(2,1)}, u32[]{:S(2)}, u32[]{:S(2)}) %collective-permute-start.4) | collective-permute-done | bytes 131104 | tf_op jit(solution)/shard_map/ppermute | solution.py:500
  36.4 1.9 %stage.13 = (bf16[2,2,12,16,128]{4,3,2,1,0:T(8,128)(2,1)}, bf16[2,2,5,16,128]{4,3,2,1,0:T(8,128)(2,1)}, bf16[2,2,3,16,128]{4,3,2,1,0:T(8,128)(2,1)}, bf16[2,2,8,16,128]{4,3,2,1,0:T(8,128)(2,1)}) custom-call(s32[1]{0:T(128)} %bitcast.1.refs_0_, s32[4]{0:T(128)} %refs_1_.35, s32[4]{0:T(128)} %refs_2_.35, s32[4,16]{1,0:T(4,128)} %refs_3_.35, ...), custom_call_target="tpu_custom_call" | custom-call | tf_op jit(solution)/shard_map/stage/pallas_call | solution.py:378
  38.3 6.4 %join_halves.5 = (bf16[4,2,2,16,16,128]{5,4,3,2,1,0:T(8,128)(2,1)}, bf16[4,2,2,16,16,128]{5,4,3,2,1,0:T(8,128)(2,1)}, bf16[4,2,2,16,16,128]{5,4,3,2,1,0:T(8,128)(2,1)}, bf16[2,2,2,16,16,128]{5,4,3,2,1,0:T(8,128)(2,1)}) custom-call(bf16[20,2,16,16,128]{4,3,2,1,0:T(8,128)(2,1)} %get-tuple-element.106.own_ref, ...), custom_call_target="tpu_custom_call" | custom-call | tf_op jit(solution)/shard_map/join_halves/pallas_call | solution.py:133
  46.2 4.2 %collective-permute-start.7 = (bf16[2,2,8,16,128]{4,3,2,1,0:T(8,128)(2,1)}, bf16[2,2,8,16,128]{4,3,2,1,0:T(8,128)(2,1)}, u32[]{:S(2)}, u32[]{:S(2)}) collective-permute-start(bf16[2,2,8,16,128]{4,3,2,1,0:T(8,128)(2,1)} %get-tuple-element.122), channel_id=1, source_target_pairs={{0,12},{4,0},{8,4},{12,8},{1,13},{5,1},{9,5},{13,9},{2,14},{6,2},{... | collective-permute-start | bytes 393224 | tf_op jit(solution)/shard_map/ppermute | solution.py:500
  50.4 5.9 %stage.14 = (bf16[4,2,16,16,128]{4,3,2,1,0:T(8,128)(2,1)}, bf16[4,2,8,16,128]{4,3,2,1,0:T(8,128)(2,1)}) custom-call(s32[1]{0:T(128)} %bitcast.1.refs_0_, s32[4]{0:T(128)} %refs_1_.35, s32[4]{0:T(128)} %refs_2_.35, s32[4,16]{1,0:T(4,128)} %refs_3_.35, s32[1]{0:T(128)} %bitcast.near_ref.refs_4_, bf16[20,16,16,128]{3,2,1,0:T(8,128)(2,1)} %get-tuple-element.169.refs_5_, ...), custom_call_target="tpu_custom_call" | custom-call | tf_op jit(solution)/shard_map/stage/pallas_call | solution.py:378
  56.3 1.8 %collective-permute-start.8 = (bf16[4,2,8,16,128]{4,3,2,1,0:T(8,128)(2,1)}, bf16[4,2,8,16,128]{4,3,2,1,0:T(8,128)(2,1)}, u32[]{:S(2)}, u32[]{:S(2)}) collective-permute-start(bf16[4,2,8,16,128]{4,3,2,1,0:T(8,128)(2,1)} %get-tuple-element.123), channel_id=1, source_target_pairs={{0,12},{4,0},{8,4},{12,8},{1,13},{5,1},{9,5},{13,9},{2,14},{6,2},{... | collective-permute-start | bytes 786440 | tf_op jit(solution)/shard_map/ppermute | solution.py:500
  58.1 5.0 %collective-permute-done.8.refs_6_ = bf16[4,2,8,16,128]{4,3,2,1,0:T(8,128)(2,1)} collective-permute-done((bf16[4,2,8,16,128]{4,3,2,1,0:T(8,128)(2,1)}, bf16[4,2,8,16,128]{4,3,2,1,0:T(8,128)(2,1)}, u32[]{:S(2)}, u32[]{:S(2)}) %collective-permute-start.8) | collective-permute-done | bytes 262176 | tf_op jit(solution)/shard_map/ppermute | solution.py:500
  63.0 2.1 %stage.15 = (bf16[4,2,12,16,128]{4,3,2,1,0:T(8,128)(2,1)}, bf16[4,2,5,16,128]{4,3,2,1,0:T(8,128)(2,1)}, bf16[4,2,3,16,128]{4,3,2,1,0:T(8,128)(2,1)}, bf16[4,2,8,16,128]{4,3,2,1,0:T(8,128)(2,1)}) custom-call(s32[1]{0:T(128)} %bitcast.1.refs_0_, s32[4]{0:T(128)} %refs_1_.35, s32[4]{0:T(128)} %refs_2_.35, s32[4,16]{1,0:T(4,128)} %refs_3_.35, ...), custom_call_target="tpu_custom_call" | custom-call | tf_op jit(solution)/shard_map/stage/pallas_call | solution.py:378
  65.2 3.9 %collective-permute-start.11 = (bf16[4,2,8,16,128]{4,3,2,1,0:T(8,128)(2,1)}, bf16[4,2,8,16,128]{4,3,2,1,0:T(8,128)(2,1)}, u32[]{:S(2)}, u32[]{:S(2)}) collective-permute-start(bf16[4,2,8,16,128]{4,3,2,1,0:T(8,128)(2,1)} %get-tuple-element.132), channel_id=1, source_target_pairs={{0,12},{4,0},{8,4},{12,8},{1,13},{5,1},{9,5},{13,9},{2,14},{6,2},{... | collective-permute-start | bytes 786440 | tf_op jit(solution)/shard_map/ppermute | solution.py:500
  71.2 5.9 %stage.16 = (bf16[4,2,16,16,128]{4,3,2,1,0:T(8,128)(2,1)}, bf16[4,2,8,16,128]{4,3,2,1,0:T(8,128)(2,1)}) custom-call(s32[1]{0:T(128)} %bitcast.1.refs_0_, s32[4]{0:T(128)} %refs_1_.35, s32[4]{0:T(128)} %refs_2_.35, s32[4,16]{1,0:T(4,128)} %refs_3_.35, s32[1]{0:T(128)} %bitcast.near_ref.refs_4_, bf16[20,16,16,128]{3,2,1,0:T(8,128)(2,1)} %get-tuple-element.169.refs_5_, ...), custom_call_target="tpu_custom_call" | custom-call | tf_op jit(solution)/shard_map/stage/pallas_call | solution.py:378
  77.1 3.6 %collective-permute-start.12 = (bf16[4,2,8,16,128]{4,3,2,1,0:T(8,128)(2,1)}, bf16[4,2,8,16,128]{4,3,2,1,0:T(8,128)(2,1)}, u32[]{:S(2)}, u32[]{:S(2)}) collective-permute-start(bf16[4,2,8,16,128]{4,3,2,1,0:T(8,128)(2,1)} %get-tuple-element.133), channel_id=1, source_target_pairs={{0,12},{4,0},{8,4},{12,8},{1,13},{5,1},{9,5},{13,9},{2,14},{6,2},{... | collective-permute-start | bytes 786440 | tf_op jit(solution)/shard_map/ppermute | solution.py:500
  80.7 2.0 %place.6 = (bf16[12,16,5120]{2,1,0:T(8,128)(2,1)}, bf16[16,16,5120]{2,1,0:T(8,128)(2,1)}, bf16[28,16,2304]{2,1,0:T(8,128)(2,1)}) custom-call(s32[1]{0:T(128)} %bitcast.1.refs_0_, s32[4]{0:T(128)} %refs_1_.35, s32[4]{0:T(128)} %refs_2_.35, s32[4,16]{1,0:T(4,128)} %refs_3_.35, s32[1]{0:T(128)} %bitcast.near_ref.refs_4_, ...), custom_call_target="tpu_custom_call" | custom-call | flops 8625000448 | tf_op jit(solution)/shard_map/place/pallas_call | solution.py:429
  82.7 2.8 %collective-permute-done.12.refs_6_ = bf16[4,2,8,16,128]{4,3,2,1,0:T(8,128)(2,1)} collective-permute-done((bf16[4,2,8,16,128]{4,3,2,1,0:T(8,128)(2,1)}, bf16[4,2,8,16,128]{4,3,2,1,0:T(8,128)(2,1)}, u32[]{:S(2)}, u32[]{:S(2)}) %collective-permute-start.12) | collective-permute-done | bytes 262176 | tf_op jit(solution)/shard_map/ppermute | solution.py:500
  85.6 2.1 %stage.17 = (bf16[4,2,12,16,128]{4,3,2,1,0:T(8,128)(2,1)}, bf16[4,2,5,16,128]{4,3,2,1,0:T(8,128)(2,1)}, bf16[4,2,3,16,128]{4,3,2,1,0:T(8,128)(2,1)}, bf16[4,2,8,16,128]{4,3,2,1,0:T(8,128)(2,1)}) custom-call(s32[1]{0:T(128)} %bitcast.1.refs_0_, s32[4]{0:T(128)} %refs_1_.35, s32[4]{0:T(128)} %refs_2_.35, s32[4,16]{1,0:T(4,128)} %refs_3_.35, ...), custom_call_target="tpu_custom_call" | custom-call | tf_op jit(solution)/shard_map/stage/pallas_call | solution.py:378
  87.7 3.7 %collective-permute-start.16 = (bf16[4,2,8,16,128]{4,3,2,1,0:T(8,128)(2,1)}, bf16[4,2,8,16,128]{4,3,2,1,0:T(8,128)(2,1)}, u32[]{:S(2)}, u32[]{:S(2)}) collective-permute-start(bf16[4,2,8,16,128]{4,3,2,1,0:T(8,128)(2,1)} %get-tuple-element.146), channel_id=1, source_target_pairs={{0,12},{4,0},{8,4},{12,8},{1,13},{5,1},{9,5},{13,9},{2,14},{6,2},{... | collective-permute-start | bytes 786440 | tf_op jit(solution)/shard_map/ppermute | solution.py:500
  93.9 5.9 %stage.18 = (bf16[4,2,16,16,128]{4,3,2,1,0:T(8,128)(2,1)}, bf16[4,2,8,16,128]{4,3,2,1,0:T(8,128)(2,1)}) custom-call(s32[1]{0:T(128)} %bitcast.1.refs_0_, s32[4]{0:T(128)} %refs_1_.35, s32[4]{0:T(128)} %refs_2_.35, s32[4,16]{1,0:T(4,128)} %refs_3_.35, s32[1]{0:T(128)} %bitcast.near_ref.refs_4_, bf16[20,16,16,128]{3,2,1,0:T(8,128)(2,1)} %get-tuple-element.169.refs_5_, ...), custom_call_target="tpu_custom_call" | custom-call | tf_op jit(solution)/shard_map/stage/pallas_call | solution.py:378
  99.8 4.7 %collective-permute-start.17 = (bf16[4,2,8,16,128]{4,3,2,1,0:T(8,128)(2,1)}, bf16[4,2,8,16,128]{4,3,2,1,0:T(8,128)(2,1)}, u32[]{:S(2)}, u32[]{:S(2)}) collective-permute-start(bf16[4,2,8,16,128]{4,3,2,1,0:T(8,128)(2,1)} %get-tuple-element.147), channel_id=1, source_target_pairs={{0,12},{4,0},{8,4},{12,8},{1,13},{5,1},{9,5},{13,9},{2,14},{6,2},{... | collective-permute-start | bytes 786440 | tf_op jit(solution)/shard_map/ppermute | solution.py:500
  104.6 2.4 %place.7 = (bf16[12,16,5120]{2,1,0:T(8,128)(2,1)}, bf16[16,16,5120]{2,1,0:T(8,128)(2,1)}, bf16[28,16,2304]{2,1,0:T(8,128)(2,1)}) custom-call(s32[1]{0:T(128)} %bitcast.1.refs_0_, s32[4]{0:T(128)} %refs_1_.35, s32[4]{0:T(128)} %refs_2_.35, s32[4,16]{1,0:T(4,128)} %refs_3_.35, ...), custom_call_target="tpu_custom_call", output_to_operand_aliasing={{0}: (9, {}), {1}: (10, {}), {2}: (11, {})} | custom-call | flops 8625000448 | tf_op jit(solution)/shard_map/place/pallas_call | solution.py:429
  106.9 1.8 %collective-permute-done.17.refs_6_ = bf16[4,2,8,16,128]{4,3,2,1,0:T(8,128)(2,1)} collective-permute-done((bf16[4,2,8,16,128]{4,3,2,1,0:T(8,128)(2,1)}, bf16[4,2,8,16,128]{4,3,2,1,0:T(8,128)(2,1)}, u32[]{:S(2)}, u32[]{:S(2)}) %collective-permute-start.17) | collective-permute-done | bytes 262176 | tf_op jit(solution)/shard_map/ppermute | solution.py:500
  108.8 2.1 %stage.19 = (bf16[4,2,12,16,128]{4,3,2,1,0:T(8,128)(2,1)}, bf16[4,2,5,16,128]{4,3,2,1,0:T(8,128)(2,1)}, bf16[4,2,3,16,128]{4,3,2,1,0:T(8,128)(2,1)}, bf16[4,2,8,16,128]{4,3,2,1,0:T(8,128)(2,1)}) custom-call(s32[1]{0:T(128)} %bitcast.1.refs_0_, s32[4]{0:T(128)} %refs_1_.35, s32[4]{0:T(128)} %refs_2_.35, s32[4,16]{1,0:T(4,128)} %refs_3_.35, ...), custom_call_target="tpu_custom_call" | custom-call | tf_op jit(solution)/shard_map/stage/pallas_call | solution.py:378
  110.9 4.4 %collective-permute-start.25 = (bf16[4,2,8,16,128]{4,3,2,1,0:T(8,128)(2,1)}, bf16[4,2,8,16,128]{4,3,2,1,0:T(8,128)(2,1)}, u32[]{:S(2)}, u32[]{:S(2)}) collective-permute-start(bf16[4,2,8,16,128]{4,3,2,1,0:T(8,128)(2,1)} %get-tuple-element.174), channel_id=1, source_target_pairs={{0,12},{4,0},{8,4},{12,8},{1,13},{5,1},{9,5},{13,9},{2,14},{6,2},{... | collective-permute-start | bytes 786440 | tf_op jit(solution)/shard_map/ppermute | solution.py:500
  117.7 5.9 %stage.20 = (bf16[4,2,16,16,128]{4,3,2,1,0:T(8,128)(2,1)}, bf16[4,2,8,16,128]{4,3,2,1,0:T(8,128)(2,1)}) custom-call(s32[1]{0:T(128)} %bitcast.1.refs_0_, s32[4]{0:T(128)} %refs_1_.35, s32[4]{0:T(128)} %refs_2_.35, s32[4,16]{1,0:T(4,128)} %refs_3_.35, s32[1]{0:T(128)} %bitcast.near_ref.refs_4_, bf16[20,16,16,128]{3,2,1,0:T(8,128)(2,1)} %get-tuple-element.169.refs_5_, ...), custom_call_target="tpu_custom_call" | custom-call | tf_op jit(solution)/shard_map/stage/pallas_call | solution.py:378
  123.6 3.5 %collective-permute-start.33 = (bf16[4,2,5,16,128]{4,3,2,1,0:T(8,128)(2,1)}, bf16[4,2,5,16,128]{4,3,2,1,0:T(8,128)(2,1)}, u32[]{:S(2)}, u32[]{:S(2)}) collective-permute-start(bf16[4,2,5,16,128]{4,3,2,1,0:T(8,128)(2,1)} %get-tuple-element.192), channel_id=1, source_target_pairs={{0,4},{4,8},{8,12},{12,0},{1,5},{5,9},{9,13},{13,1},{2,6},{6,10},{... | collective-permute-start | bytes 491528 | tf_op jit(solution)/shard_map/ppermute | solution.py:500
  129.6 2.4 %place.8 = (bf16[12,16,5120]{2,1,0:T(8,128)(2,1)}, bf16[16,16,5120]{2,1,0:T(8,128)(2,1)}, bf16[28,16,2304]{2,1,0:T(8,128)(2,1)}) custom-call(s32[1]{0:T(128)} %bitcast.1.refs_0_, s32[4]{0:T(128)} %refs_1_.35, s32[4]{0:T(128)} %refs_2_.35, s32[4,16]{1,0:T(4,128)} %refs_3_.35, ...), custom_call_target="tpu_custom_call", output_to_operand_aliasing={{0}: (9, {}), {1}: (10, {}), {2}: (11, {})} | custom-call | flops 8625000448 | tf_op jit(solution)/shard_map/place/pallas_call | solution.py:429
  132.0 3.9 %stage.21 = (bf16[2,2,16,16,128]{4,3,2,1,0:T(8,128)(2,1)}, bf16[2,2,8,16,128]{4,3,2,1,0:T(8,128)(2,1)}) custom-call(s32[1]{0:T(128)} %bitcast.1.refs_0_, s32[4]{0:T(128)} %refs_1_.35, s32[4]{0:T(128)} %refs_2_.35, s32[4,16]{1,0:T(4,128)} %refs_3_.35, s32[1]{0:T(128)} %bitcast.near_ref.refs_4_, bf16[20,16,16,128]{3,2,1,0:T(8,128)(2,1)} %get-tuple-element.169.refs_5_, ...), custom_call_target="tpu_custom_call" | custom-call | tf_op jit(solution)/shard_map/stage/pallas_call | solution.py:378
  135.9 2.0 %collective-permute-start.24 = (bf16[2,2,8,16,128]{4,3,2,1,0:T(8,128)(2,1)}, bf16[2,2,8,16,128]{4,3,2,1,0:T(8,128)(2,1)}, u32[]{:S(2)}, u32[]{:S(2)}) collective-permute-start(bf16[2,2,8,16,128]{4,3,2,1,0:T(8,128)(2,1)} %get-tuple-element.172), channel_id=1, source_target_pairs={{0,12},{4,0},{8,4},{12,8},{1,13},{5,1},{9,5},{13,9},{2,14},{6,2},{... | collective-permute-start | bytes 393224 | tf_op jit(solution)/shard_map/ppermute | solution.py:500
  139.0 2.1 %stage.22 = (bf16[4,2,12,16,128]{4,3,2,1,0:T(8,128)(2,1)}, bf16[4,2,5,16,128]{4,3,2,1,0:T(8,128)(2,1)}, bf16[4,2,3,16,128]{4,3,2,1,0:T(8,128)(2,1)}, bf16[4,2,8,16,128]{4,3,2,1,0:T(8,128)(2,1)}) custom-call(s32[1]{0:T(128)} %bitcast.1.refs_0_, s32[4]{0:T(128)} %refs_1_.35, s32[4]{0:T(128)} %refs_2_.35, s32[4,16]{1,0:T(4,128)} %refs_3_.35, ...), custom_call_target="tpu_custom_call" | custom-call | tf_op jit(solution)/shard_map/stage/pallas_call | solution.py:378
  141.2 2.5 %collective-permute-start.27 = (bf16[4,2,5,16,128]{4,3,2,1,0:T(8,128)(2,1)}, bf16[4,2,5,16,128]{4,3,2,1,0:T(8,128)(2,1)}, u32[]{:S(2)}, u32[]{:S(2)}) collective-permute-start(bf16[4,2,5,16,128]{4,3,2,1,0:T(8,128)(2,1)} %get-tuple-element.181), channel_id=1, source_target_pairs={{0,4},{4,8},{8,12},{12,0},{1,5},{5,9},{9,13},{13,1},{2,6},{6,10},{... | collective-permute-start | bytes 491528 | tf_op jit(solution)/shard_map/ppermute | solution.py:500
  143.6 2.4 %collective-permute-start.31 = (bf16[4,2,8,16,128]{4,3,2,1,0:T(8,128)(2,1)}, bf16[4,2,8,16,128]{4,3,2,1,0:T(8,128)(2,1)}, u32[]{:S(2)}, u32[]{:S(2)}) collective-permute-start(bf16[4,2,8,16,128]{4,3,2,1,0:T(8,128)(2,1)} %get-tuple-element.187), channel_id=1, source_target_pairs={{0,12},{4,0},{8,4},{12,8},{1,13},{5,1},{9,5},{13,9},{2,14},{6,2},{... | collective-permute-start | bytes 786440 | tf_op jit(solution)/shard_map/ppermute | solution.py:500
  146.1 2.4 %place.9 = (bf16[12,16,5120]{2,1,0:T(8,128)(2,1)}, bf16[16,16,5120]{2,1,0:T(8,128)(2,1)}, bf16[28,16,2304]{2,1,0:T(8,128)(2,1)}) custom-call(s32[1]{0:T(128)} %bitcast.1.refs_0_, s32[4]{0:T(128)} %refs_1_.35, s32[4]{0:T(128)} %refs_2_.35, s32[4,16]{1,0:T(4,128)} %refs_3_.35, ...), custom_call_target="tpu_custom_call", output_to_operand_aliasing={{0}: (9, {}), {1}: (10, {}), {2}: (11, {})} | custom-call | flops 8625000448 | tf_op jit(solution)/shard_map/place/pallas_call | solution.py:429
  148.5 1.9 %stage.23 = (bf16[2,2,12,16,128]{4,3,2,1,0:T(8,128)(2,1)}, bf16[2,2,5,16,128]{4,3,2,1,0:T(8,128)(2,1)}, bf16[2,2,3,16,128]{4,3,2,1,0:T(8,128)(2,1)}, bf16[2,2,8,16,128]{4,3,2,1,0:T(8,128)(2,1)}) custom-call(s32[1]{0:T(128)} %bitcast.1.refs_0_, s32[4]{0:T(128)} %refs_1_.35, s32[4]{0:T(128)} %refs_2_.35, s32[4,16]{1,0:T(4,128)} %refs_3_.35, ...), custom_call_target="tpu_custom_call" | custom-call | tf_op jit(solution)/shard_map/stage/pallas_call | solution.py:378
  150.8 1.7 collective-permute-done.31.refs_8_
  152.5 2.4 %place.10 = (bf16[12,16,5120]{2,1,0:T(8,128)(2,1)}, bf16[16,16,5120]{2,1,0:T(8,128)(2,1)}, bf16[28,16,2304]{2,1,0:T(8,128)(2,1)}) custom-call(s32[1]{0:T(128)} %bitcast.1.refs_0_, s32[4]{0:T(128)} %refs_1_.35, s32[4]{0:T(128)} %refs_2_.35, s32[4,16]{1,0:T(4,128)} %refs_3_.35, ...), custom_call_target="tpu_custom_call", output_to_operand_aliasing={{0}: (9, {}), {1}: (10, {}), {2}: (11, {})} | custom-call | flops 8625000448 | tf_op jit(solution)/shard_map/place/pallas_call | solution.py:429
  155.8 3.3 %collective-permute-start.28 = (bf16[2,2,5,16,128]{4,3,2,1,0:T(8,128)(2,1)}, bf16[2,2,5,16,128]{4,3,2,1,0:T(8,128)(2,1)}, u32[]{:S(2)}, u32[]{:S(2)}) collective-permute-start(bf16[2,2,5,16,128]{4,3,2,1,0:T(8,128)(2,1)} %get-tuple-element.182), channel_id=1, source_target_pairs={{0,4},{4,8},{8,12},{12,0},{1,5},{5,9},{9,13},{13,1},{2,6},{6,10},{... | collective-permute-start | bytes 245768 | tf_op jit(solution)/shard_map/ppermute | solution.py:500
  159.6 2.9 %finish.2 = (bf16[12,16,5120]{2,1,0:T(8,128)(2,1)}, bf16[16,16,5120]{2,1,0:T(8,128)(2,1)}) custom-call(s32[1]{0:T(128)} %bitcast.near_ref.refs_4_, bf16[28,16,2304]{2,1,0:T(8,128)(2,1)} %collective-permute-done.35.refs_0_, bf16[12,16,5120]{2,1,0:T(8,128)(2,1)} %get-tuple-element.201.refs_1_, ...), custom_call_target="tpu_custom_call", output_to_operand_aliasing={{0}: (2, {}), {1}: (3, {})} | custom-call | flops 1724999936 | tf_op jit(solution)/shard_map/finish/pallas_call | solution.py:478
  163.6 2.4 %collective-permute-done.32.refs_8_ = bf16[2,2,8,16,128]{4,3,2,1,0:T(8,128)(2,1)} collective-permute-done((bf16[2,2,8,16,128]{4,3,2,1,0:T(8,128)(2,1)}, bf16[2,2,8,16,128]{4,3,2,1,0:T(8,128)(2,1)}, u32[]{:S(2)}, u32[]{:S(2)}) %collective-permute-start.32) | collective-permute-done | bytes 131104 | tf_op jit(solution)/shard_map/ppermute | solution.py:500
  165.9 2.0 %place.11 = (bf16[12,16,5120]{2,1,0:T(8,128)(2,1)}, bf16[16,16,5120]{2,1,0:T(8,128)(2,1)}, bf16[28,16,256]{2,1,0:T(8,128)(2,1)}) custom-call(s32[1]{0:T(128)} %bitcast.1.refs_0_, s32[4]{0:T(128)} %refs_1_.35, s32[4]{0:T(128)} %refs_2_.35, s32[4,16]{1,0:T(4,128)} %refs_3_.35, s32[1]{0:T(128)} %bitcast.near_ref.refs_4_, ...), custom_call_target="tpu_custom_call", output_to_operand_aliasing={{0}: (9, {}), {1}: (10, {})} | custom-call | flops 1724999936 | tf_op jit(solution)/shard_map/place/pallas_call | solution.py:429
  168.0 1.8 %collective-permute-done.36.refs_0_ = bf16[28,16,256]{2,1,0:T(8,128)(2,1)} collective-permute-done((bf16[28,16,256]{2,1,0:T(8,128)(2,1)}, bf16[28,16,256]{2,1,0:T(8,128)(2,1)}, u32[]{:S(2)}, u32[]{:S(2)}) %collective-permute-start.36) | collective-permute-done | bytes 229408 | tf_op jit(solution)/shard_map/ppermute | solution.py:495
  169.9 1.6 finish.3
  (51 shorter events, 18.0 us)
Async XLA Ops:
  5.8 2.0 %collective-permute-start = (bf16[2,2,16,16,128]{4,3,2,1,0:T(8,128)(2,1)}, bf16[2,2,16,16,128]{4,3,2,1,0:T(8,128)(2,1)}, u32[]{:S(2)}, u32[]{:S(2)}) collective-permute-start(bf16[2,2,16,16,128]{4,3,2,1,0:T(8,128)(2,1)} %get-tuple-element.107), channel_id=1, source_target_pairs={{0,1},{1,0},{2,3},{3,2},{4,5},{5,4},{6,7},{7,6},{8,9},{9,8},{10,11... | collective-permute-start | bytes 786440 | tf_op jit(solution)/shard_map/ppermute | solution.py:495
  9.7 15.9 %collective-permute-start.3 = (bf16[2,2,2,16,16,128]{5,4,3,2,1,0:T(8,128)(2,1)}, bf16[2,2,2,16,16,128]{5,4,3,2,1,0:T(8,128)(2,1)}, u32[]{:S(2)}, u32[]{:S(2)}) collective-permute-start(bf16[2,2,2,16,16,128]{5,4,3,2,1,0:T(8,128)(2,1)} %join_halves.3.refs_7_), channel_id=1, source_target_pairs={{0,2},{1,3},{2,0},{3,1},{4,6},{5,7},{6,4},{7,5},{8,10},{9,11},{10,... | collective-permute-start | bytes 1572872 | tf_op jit(solution)/shard_map/ppermute | solution.py:495
  12.5 4.2 %collective-permute-start.1 = (bf16[4,2,16,16,128]{4,3,2,1,0:T(8,128)(2,1)}, bf16[4,2,16,16,128]{4,3,2,1,0:T(8,128)(2,1)}, u32[]{:S(2)}, u32[]{:S(2)}) collective-permute-start(bf16[4,2,16,16,128]{4,3,2,1,0:T(8,128)(2,1)} %get-tuple-element.111), channel_id=1, source_target_pairs={{0,1},{1,0},{2,3},{3,2},{4,5},{5,4},{6,7},{7,6},{8,9},{9,8},{10,11... | collective-permute-start | bytes 1572872 | tf_op jit(solution)/shard_map/ppermute | solution.py:495
  12.5 25.8 %collective-permute-start.9 = (bf16[14,2,16,16,128]{4,3,2,1,0:T(8,128)(2,1)}, bf16[14,2,16,16,128]{4,3,2,1,0:T(8,128)(2,1)}, u32[]{:S(2)}, u32[]{:S(2)}) collective-permute-start(bf16[14,2,16,16,128]{4,3,2,1,0:T(8,128)(2,1)} %get-tuple-element.127), channel_id=1, source_target_pairs={{0,1},{1,0},{2,3},{3,2},{4,5},{5,4},{6,7},{7,6},{8,9},{9,8},{10,11... | collective-permute-start | bytes 5505032 | tf_op jit(solution)/shard_map/ppermute | solution.py:495
  16.7 33.7 %collective-permute-start.5 = (bf16[18,16,16,128]{3,2,1,0:T(8,128)(2,1)}, bf16[18,16,16,128]{3,2,1,0:T(8,128)(2,1)}, u32[]{:S(2)}, u32[]{:S(2)}) collective-permute-start(bf16[18,16,16,128]{3,2,1,0:T(8,128)(2,1)} %get-tuple-element.119), channel_id=1, source_target_pairs={{0,1},{1,0},{2,3},{3,2},{4,5},{5,4},{6,7},{7,6},{8,9},{9,8},{10,11... | collective-permute-start | bytes 3538952 | tf_op jit(solution)/shard_map/ppermute | solution.py:495
  18.9 31.5 %collective-permute-start.6 = (bf16[4,2,2,16,16,128]{5,4,3,2,1,0:T(8,128)(2,1)}, bf16[4,2,2,16,16,128]{5,4,3,2,1,0:T(8,128)(2,1)}, u32[]{:S(2)}, u32[]{:S(2)}) collective-permute-start(bf16[4,2,2,16,16,128]{5,4,3,2,1,0:T(8,128)(2,1)} %join_halves.4.refs_7_), channel_id=1, source_target_pairs={{0,2},{1,3},{2,0},{3,1},{4,6},{5,7},{6,4},{7,5},{8,10},{9,11},{10,... | collective-permute-start | bytes 3145736 | tf_op jit(solution)/shard_map/ppermute | solution.py:495
  19.0 1.7 collective-permute-start.2
  29.4 7.0 %collective-permute-start.4 = (bf16[2,2,8,16,128]{4,3,2,1,0:T(8,128)(2,1)}, bf16[2,2,8,16,128]{4,3,2,1,0:T(8,128)(2,1)}, u32[]{:S(2)}, u32[]{:S(2)}) collective-permute-start(bf16[2,2,8,16,128]{4,3,2,1,0:T(8,128)(2,1)} %get-tuple-element.116), channel_id=1, source_target_pairs={{0,12},{4,0},{8,4},{12,8},{1,13},{5,1},{9,5},{13,9},{2,14},{6,2},{... | collective-permute-start | bytes 393224 | tf_op jit(solution)/shard_map/ppermute | solution.py:500
  44.7 26.5 %collective-permute-start.10 = (bf16[4,2,2,16,16,128]{5,4,3,2,1,0:T(8,128)(2,1)}, bf16[4,2,2,16,16,128]{5,4,3,2,1,0:T(8,128)(2,1)}, u32[]{:S(2)}, u32[]{:S(2)}) collective-permute-start(bf16[4,2,2,16,16,128]{5,4,3,2,1,0:T(8,128)(2,1)} %get-tuple-element.129.refs_7_), channel_id=1, source_target_pairs={{0,2},{1,3},{2,0},{3,1},{4,6},{5,7},{6,4},{7,5},{8,10},{9,11},{10,... | collective-permute-start | bytes 3145736 | tf_op jit(solution)/shard_map/ppermute | solution.py:495
  46.2 10.1 %collective-permute-start.7 = (bf16[2,2,8,16,128]{4,3,2,1,0:T(8,128)(2,1)}, bf16[2,2,8,16,128]{4,3,2,1,0:T(8,128)(2,1)}, u32[]{:S(2)}, u32[]{:S(2)}) collective-permute-start(bf16[2,2,8,16,128]{4,3,2,1,0:T(8,128)(2,1)} %get-tuple-element.122), channel_id=1, source_target_pairs={{0,12},{4,0},{8,4},{12,8},{1,13},{5,1},{9,5},{13,9},{2,14},{6,2},{... | collective-permute-start | bytes 393224 | tf_op jit(solution)/shard_map/ppermute | solution.py:500
  56.3 6.7 %collective-permute-start.8 = (bf16[4,2,8,16,128]{4,3,2,1,0:T(8,128)(2,1)}, bf16[4,2,8,16,128]{4,3,2,1,0:T(8,128)(2,1)}, u32[]{:S(2)}, u32[]{:S(2)}) collective-permute-start(bf16[4,2,8,16,128]{4,3,2,1,0:T(8,128)(2,1)} %get-tuple-element.123), channel_id=1, source_target_pairs={{0,12},{4,0},{8,4},{12,8},{1,13},{5,1},{9,5},{13,9},{2,14},{6,2},{... | collective-permute-start | bytes 786440 | tf_op jit(solution)/shard_map/ppermute | solution.py:500
  65.2 12.0 %collective-permute-start.11 = (bf16[4,2,8,16,128]{4,3,2,1,0:T(8,128)(2,1)}, bf16[4,2,8,16,128]{4,3,2,1,0:T(8,128)(2,1)}, u32[]{:S(2)}, u32[]{:S(2)}) collective-permute-start(bf16[4,2,8,16,128]{4,3,2,1,0:T(8,128)(2,1)} %get-tuple-element.132), channel_id=1, source_target_pairs={{0,12},{4,0},{8,4},{12,8},{1,13},{5,1},{9,5},{13,9},{2,14},{6,2},{... | collective-permute-start | bytes 786440 | tf_op jit(solution)/shard_map/ppermute | solution.py:500
  69.1 11.6 %collective-permute-start.13 = (bf16[2,2,5,16,128]{4,3,2,1,0:T(8,128)(2,1)}, bf16[2,2,5,16,128]{4,3,2,1,0:T(8,128)(2,1)}, u32[]{:S(2)}, u32[]{:S(2)}) collective-permute-start(bf16[2,2,5,16,128]{4,3,2,1,0:T(8,128)(2,1)} %get-tuple-element.136), channel_id=1, source_target_pairs={{0,4},{4,8},{8,12},{12,0},{1,5},{5,9},{9,13},{13,1},{2,6},{6,10},{... | collective-permute-start | bytes 245768 | tf_op jit(solution)/shard_map/ppermute | solution.py:500
  69.1 11.6 %collective-permute-start.14 = (bf16[2,2,3,16,128]{4,3,2,1,0:T(8,128)(2,1)}, bf16[2,2,3,16,128]{4,3,2,1,0:T(8,128)(2,1)}, u32[]{:S(2)}, u32[]{:S(2)}) collective-permute-start(bf16[2,2,3,16,128]{4,3,2,1,0:T(8,128)(2,1)} %get-tuple-element.138), channel_id=1, source_target_pairs={{0,8},{4,12},{8,0},{12,4},{1,9},{5,13},{9,1},{13,5},{2,10},{6,14},... | collective-permute-start | bytes 147464 | tf_op jit(solution)/shard_map/ppermute | solution.py:500
  69.7 24.2 %collective-permute-start.15 = (bf16[4,2,2,16,16,128]{5,4,3,2,1,0:T(8,128)(2,1)}, bf16[4,2,2,16,16,128]{5,4,3,2,1,0:T(8,128)(2,1)}, u32[]{:S(2)}, u32[]{:S(2)}) collective-permute-start(bf16[4,2,2,16,16,128]{5,4,3,2,1,0:T(8,128)(2,1)} %get-tuple-element.143.refs_7_), channel_id=1, source_target_pairs={{0,2},{1,3},{2,0},{3,1},{4,6},{5,7},{6,4},{7,5},{8,10},{9,11},{10,... | collective-permute-start | bytes 3145736 | tf_op jit(solution)/shard_map/ppermute | solution.py:495
  77.1 8.5 %collective-permute-start.12 = (bf16[4,2,8,16,128]{4,3,2,1,0:T(8,128)(2,1)}, bf16[4,2,8,16,128]{4,3,2,1,0:T(8,128)(2,1)}, u32[]{:S(2)}, u32[]{:S(2)}) collective-permute-start(bf16[4,2,8,16,128]{4,3,2,1,0:T(8,128)(2,1)} %get-tuple-element.133), channel_id=1, source_target_pairs={{0,12},{4,0},{8,4},{12,8},{1,13},{5,1},{9,5},{13,9},{2,14},{6,2},{... | collective-permute-start | bytes 786440 | tf_op jit(solution)/shard_map/ppermute | solution.py:500
  87.7 12.1 %collective-permute-start.16 = (bf16[4,2,8,16,128]{4,3,2,1,0:T(8,128)(2,1)}, bf16[4,2,8,16,128]{4,3,2,1,0:T(8,128)(2,1)}, u32[]{:S(2)}, u32[]{:S(2)}) collective-permute-start(bf16[4,2,8,16,128]{4,3,2,1,0:T(8,128)(2,1)} %get-tuple-element.146), channel_id=1, source_target_pairs={{0,12},{4,0},{8,4},{12,8},{1,13},{5,1},{9,5},{13,9},{2,14},{6,2},{... | collective-permute-start | bytes 786440 | tf_op jit(solution)/shard_map/ppermute | solution.py:500
  91.4 13.2 %collective-permute-start.18 = (bf16[4,2,5,16,128]{4,3,2,1,0:T(8,128)(2,1)}, bf16[4,2,5,16,128]{4,3,2,1,0:T(8,128)(2,1)}, u32[]{:S(2)}, u32[]{:S(2)}) collective-permute-start(bf16[4,2,5,16,128]{4,3,2,1,0:T(8,128)(2,1)} %get-tuple-element.150), channel_id=1, source_target_pairs={{0,4},{4,8},{8,12},{12,0},{1,5},{5,9},{9,13},{13,1},{2,6},{6,10},{... | collective-permute-start | bytes 491528 | tf_op jit(solution)/shard_map/ppermute | solution.py:500
  91.4 13.1 %collective-permute-start.19 = (bf16[4,2,3,16,128]{4,3,2,1,0:T(8,128)(2,1)}, bf16[4,2,3,16,128]{4,3,2,1,0:T(8,128)(2,1)}, u32[]{:S(2)}, u32[]{:S(2)}) collective-permute-start(bf16[4,2,3,16,128]{4,3,2,1,0:T(8,128)(2,1)} %get-tuple-element.152), channel_id=1, source_target_pairs={{0,8},{4,12},{8,0},{12,4},{1,9},{5,13},{9,1},{13,5},{2,10},{6,14},... | collective-permute-start | bytes 294920 | tf_op jit(solution)/shard_map/ppermute | solution.py:500
  92.0 25.7 %collective-permute-start.20 = (bf16[4,2,2,16,16,128]{5,4,3,2,1,0:T(8,128)(2,1)}, bf16[4,2,2,16,16,128]{5,4,3,2,1,0:T(8,128)(2,1)}, u32[]{:S(2)}, u32[]{:S(2)}) collective-permute-start(bf16[4,2,2,16,16,128]{5,4,3,2,1,0:T(8,128)(2,1)} %get-tuple-element.159.refs_7_), channel_id=1, source_target_pairs={{0,2},{1,3},{2,0},{3,1},{4,6},{5,7},{6,4},{7,5},{8,10},{9,11},{10,... | collective-permute-start | bytes 3145736 | tf_op jit(solution)/shard_map/ppermute | solution.py:495
  99.8 9.0 %collective-permute-start.17 = (bf16[4,2,8,16,128]{4,3,2,1,0:T(8,128)(2,1)}, bf16[4,2,8,16,128]{4,3,2,1,0:T(8,128)(2,1)}, u32[]{:S(2)}, u32[]{:S(2)}) collective-permute-start(bf16[4,2,8,16,128]{4,3,2,1,0:T(8,128)(2,1)} %get-tuple-element.147), channel_id=1, source_target_pairs={{0,12},{4,0},{8,4},{12,8},{1,13},{5,1},{9,5},{13,9},{2,14},{6,2},{... | collective-permute-start | bytes 786440 | tf_op jit(solution)/shard_map/ppermute | solution.py:500
  110.9 16.2 %collective-permute-start.25 = (bf16[4,2,8,16,128]{4,3,2,1,0:T(8,128)(2,1)}, bf16[4,2,8,16,128]{4,3,2,1,0:T(8,128)(2,1)}, u32[]{:S(2)}, u32[]{:S(2)}) collective-permute-start(bf16[4,2,8,16,128]{4,3,2,1,0:T(8,128)(2,1)} %get-tuple-element.174), channel_id=1, source_target_pairs={{0,12},{4,0},{8,4},{12,8},{1,13},{5,1},{9,5},{13,9},{2,14},{6,2},{... | collective-permute-start | bytes 786440 | tf_op jit(solution)/shard_map/ppermute | solution.py:500
  115.4 14.2 %collective-permute-start.21 = (bf16[4,2,5,16,128]{4,3,2,1,0:T(8,128)(2,1)}, bf16[4,2,5,16,128]{4,3,2,1,0:T(8,128)(2,1)}, u32[]{:S(2)}, u32[]{:S(2)}) collective-permute-start(bf16[4,2,5,16,128]{4,3,2,1,0:T(8,128)(2,1)} %get-tuple-element.163), channel_id=1, source_target_pairs={{0,4},{4,8},{8,12},{12,0},{1,5},{5,9},{9,13},{13,1},{2,6},{6,10},{... | collective-permute-start | bytes 491528 | tf_op jit(solution)/shard_map/ppermute | solution.py:500
  115.4 12.8 %collective-permute-start.22 = (bf16[4,2,3,16,128]{4,3,2,1,0:T(8,128)(2,1)}, bf16[4,2,3,16,128]{4,3,2,1,0:T(8,128)(2,1)}, u32[]{:S(2)}, u32[]{:S(2)}) collective-permute-start(bf16[4,2,3,16,128]{4,3,2,1,0:T(8,128)(2,1)} %get-tuple-element.165), channel_id=1, source_target_pairs={{0,8},{4,12},{8,0},{12,4},{1,9},{5,13},{9,1},{13,5},{2,10},{6,14},... | collective-permute-start | bytes 294920 | tf_op jit(solution)/shard_map/ppermute | solution.py:500
  116.0 16.0 %collective-permute-start.23 = (bf16[2,2,2,16,16,128]{5,4,3,2,1,0:T(8,128)(2,1)}, bf16[2,2,2,16,16,128]{5,4,3,2,1,0:T(8,128)(2,1)}, u32[]{:S(2)}, u32[]{:S(2)}) collective-permute-start(bf16[2,2,2,16,16,128]{5,4,3,2,1,0:T(8,128)(2,1)} %get-tuple-element.170.refs_7_), channel_id=1, source_target_pairs={{0,2},{1,3},{2,0},{3,1},{4,6},{5,7},{6,4},{7,5},{8,10},{9,11},{10,... | collective-permute-start | bytes 1572872 | tf_op jit(solution)/shard_map/ppermute | solution.py:495
  123.6 22.4 %collective-permute-start.33 = (bf16[4,2,5,16,128]{4,3,2,1,0:T(8,128)(2,1)}, bf16[4,2,5,16,128]{4,3,2,1,0:T(8,128)(2,1)}, u32[]{:S(2)}, u32[]{:S(2)}) collective-permute-start(bf16[4,2,5,16,128]{4,3,2,1,0:T(8,128)(2,1)} %get-tuple-element.192), channel_id=1, source_target_pairs={{0,4},{4,8},{8,12},{12,0},{1,5},{5,9},{9,13},{13,1},{2,6},{6,10},{... | collective-permute-start | bytes 491528 | tf_op jit(solution)/shard_map/ppermute | solution.py:500
  127.1 16.5 %collective-permute-start.34 = (bf16[4,2,3,16,128]{4,3,2,1,0:T(8,128)(2,1)}, bf16[4,2,3,16,128]{4,3,2,1,0:T(8,128)(2,1)}, u32[]{:S(2)}, u32[]{:S(2)}) collective-permute-start(bf16[4,2,3,16,128]{4,3,2,1,0:T(8,128)(2,1)} %get-tuple-element.194), channel_id=1, source_target_pairs={{0,8},{4,12},{8,0},{12,4},{1,9},{5,13},{9,1},{13,5},{2,10},{6,14},... | collective-permute-start | bytes 294920 | tf_op jit(solution)/shard_map/ppermute | solution.py:500
  128.1 10.9 %collective-permute-start.26 = (bf16[4,2,8,16,128]{4,3,2,1,0:T(8,128)(2,1)}, bf16[4,2,8,16,128]{4,3,2,1,0:T(8,128)(2,1)}, u32[]{:S(2)}, u32[]{:S(2)}) collective-permute-start(bf16[4,2,8,16,128]{4,3,2,1,0:T(8,128)(2,1)} %get-tuple-element.175), channel_id=1, source_target_pairs={{0,12},{4,0},{8,4},{12,8},{1,13},{5,1},{9,5},{13,9},{2,14},{6,2},{... | collective-permute-start | bytes 786440 | tf_op jit(solution)/shard_map/ppermute | solution.py:500
  135.9 12.5 %collective-permute-start.24 = (bf16[2,2,8,16,128]{4,3,2,1,0:T(8,128)(2,1)}, bf16[2,2,8,16,128]{4,3,2,1,0:T(8,128)(2,1)}, u32[]{:S(2)}, u32[]{:S(2)}) collective-permute-start(bf16[2,2,8,16,128]{4,3,2,1,0:T(8,128)(2,1)} %get-tuple-element.172), channel_id=1, source_target_pairs={{0,12},{4,0},{8,4},{12,8},{1,13},{5,1},{9,5},{13,9},{2,14},{6,2},{... | collective-permute-start | bytes 393224 | tf_op jit(solution)/shard_map/ppermute | solution.py:500
  141.2 9.7 %collective-permute-start.27 = (bf16[4,2,5,16,128]{4,3,2,1,0:T(8,128)(2,1)}, bf16[4,2,5,16,128]{4,3,2,1,0:T(8,128)(2,1)}, u32[]{:S(2)}, u32[]{:S(2)}) collective-permute-start(bf16[4,2,5,16,128]{4,3,2,1,0:T(8,128)(2,1)} %get-tuple-element.181), channel_id=1, source_target_pairs={{0,4},{4,8},{8,12},{12,0},{1,5},{5,9},{9,13},{13,1},{2,6},{6,10},{... | collective-permute-start | bytes 491528 | tf_op jit(solution)/shard_map/ppermute | solution.py:500
  143.6 7.2 %collective-permute-start.29 = (bf16[4,2,3,16,128]{4,3,2,1,0:T(8,128)(2,1)}, bf16[4,2,3,16,128]{4,3,2,1,0:T(8,128)(2,1)}, u32[]{:S(2)}, u32[]{:S(2)}) collective-permute-start(bf16[4,2,3,16,128]{4,3,2,1,0:T(8,128)(2,1)} %get-tuple-element.184), channel_id=1, source_target_pairs={{0,8},{4,12},{8,0},{12,4},{1,9},{5,13},{9,1},{13,5},{2,10},{6,14},... | collective-permute-start | bytes 294920 | tf_op jit(solution)/shard_map/ppermute | solution.py:500
  143.6 8.9 %collective-permute-start.31 = (bf16[4,2,8,16,128]{4,3,2,1,0:T(8,128)(2,1)}, bf16[4,2,8,16,128]{4,3,2,1,0:T(8,128)(2,1)}, u32[]{:S(2)}, u32[]{:S(2)}) collective-permute-start(bf16[4,2,8,16,128]{4,3,2,1,0:T(8,128)(2,1)} %get-tuple-element.187), channel_id=1, source_target_pairs={{0,12},{4,0},{8,4},{12,8},{1,13},{5,1},{9,5},{13,9},{2,14},{6,2},{... | collective-permute-start | bytes 786440 | tf_op jit(solution)/shard_map/ppermute | solution.py:500
  154.9 4.7 %collective-permute-start.35 = (bf16[28,16,2304]{2,1,0:T(8,128)(2,1)}, bf16[28,16,2304]{2,1,0:T(8,128)(2,1)}, u32[]{:S(2)}, u32[]{:S(2)}) collective-permute-start(bf16[28,16,2304]{2,1,0:T(8,128)(2,1)} %get-tuple-element.200), channel_id=1, source_target_pairs={{0,1},{1,0},{2,3},{3,2},{4,5},{5,4},{6,7},{7,6},{8,9},{9,8},{10,11... | collective-permute-start | bytes 6193160 | tf_op jit(solution)/shard_map/ppermute | solution.py:495
  155.0 7.5 %collective-permute-start.30 = (bf16[2,2,3,16,128]{4,3,2,1,0:T(8,128)(2,1)}, bf16[2,2,3,16,128]{4,3,2,1,0:T(8,128)(2,1)}, u32[]{:S(2)}, u32[]{:S(2)}) collective-permute-start(bf16[2,2,3,16,128]{4,3,2,1,0:T(8,128)(2,1)} %get-tuple-element.185), channel_id=1, source_target_pairs={{0,8},{4,12},{8,0},{12,4},{1,9},{5,13},{9,1},{13,5},{2,10},{6,14},... | collective-permute-start | bytes 147464 | tf_op jit(solution)/shard_map/ppermute | solution.py:500
  155.8 7.8 %collective-permute-start.28 = (bf16[2,2,5,16,128]{4,3,2,1,0:T(8,128)(2,1)}, bf16[2,2,5,16,128]{4,3,2,1,0:T(8,128)(2,1)}, u32[]{:S(2)}, u32[]{:S(2)}) collective-permute-start(bf16[2,2,5,16,128]{4,3,2,1,0:T(8,128)(2,1)} %get-tuple-element.182), channel_id=1, source_target_pairs={{0,4},{4,8},{8,12},{12,0},{1,5},{5,9},{9,13},{13,1},{2,6},{6,10},{... | collective-permute-start | bytes 245768 | tf_op jit(solution)/shard_map/ppermute | solution.py:500
  159.0 6.9 %collective-permute-start.32 = (bf16[2,2,8,16,128]{4,3,2,1,0:T(8,128)(2,1)}, bf16[2,2,8,16,128]{4,3,2,1,0:T(8,128)(2,1)}, u32[]{:S(2)}, u32[]{:S(2)}) collective-permute-start(bf16[2,2,8,16,128]{4,3,2,1,0:T(8,128)(2,1)} %get-tuple-element.188), channel_id=1, source_target_pairs={{0,12},{4,0},{8,4},{12,8},{1,13},{5,1},{9,5},{13,9},{2,14},{6,2},{... | collective-permute-start | bytes 393224 | tf_op jit(solution)/shard_map/ppermute | solution.py:500
  168.0 1.9 %collective-permute-start.36 = (bf16[28,16,256]{2,1,0:T(8,128)(2,1)}, bf16[28,16,256]{2,1,0:T(8,128)(2,1)}, u32[]{:S(2)}, u32[]{:S(2)}) collective-permute-start(bf16[28,16,256]{2,1,0:T(8,128)(2,1)} %get-tuple-element.205), channel_id=1, source_target_pairs={{0,1},{1,0},{2,3},{3,2},{4,5},{5,4},{6,7},{7,6},{8,9},{9,8},{10,11... | collective-permute-start | bytes 688136 | tf_op jit(solution)/shard_map/ppermute | solution.py:495
